TPU v7x, 512 devices: a whole 4x8x8 slice. The times are simulated.
512 devices in a mesh: own: 64 (over y, z), rep: 8 (over x, core).
Axes of the slice: x: 4, y: 8, z: 8, core: 2. Of those that a mesh axis runs over, the one named last changes fastest.
Arguments:
- sample_rows: bfloat16 [524288, 768], P(('own', 'rep'))
- destination: int32 [524288], P(('own', 'rep')), may hold values from 0 to 524287, as said below
- neighbours: int32 [524288, 4], P(('own', 'rep')), may hold values from 0 to 2047, as said below
- centroids: bfloat16 [256, 8, 128, 768], P('own', 'rep'), may hold values from -6 to 6
Outputs:
- new_centroids: bfloat16 [256, 8, 128, 768], P('own', 'rep')
- row_cost: float32 [524288], P(('own', 'rep'))
Inputs may be any that keep to these rules, and one draw needn't show every extreme that they name: destination is a permutation. Numbering devices own-major (device t = own index * 8 + rep index), ingested row i of device s goes to device t = destination[i] // 1024, and the rows that device t receives from device s fill its positions s * 2 up to (s + 1) * 2 - 1; every device sends exactly 2 rows to every device. `neighbours`: each regrouped row on the device with own index o and rep index r lists 4 different blocks a * 8 + r with a inside the grid and o * 4 - 1 <= a <= o * 4 + 4.
All inputs are finite; a program needn't handle non-finite values.
Results may differ from a plain program's by a relative error of at most 0.0075.
Values may be sent and summed in bfloat16 or wider, within the bound.
No kernel may reach another device: no remote copies, remote signals or barrier semaphores. Data moves between devices by JAX's collectives and lax.ppermute only.
A program may use at most 64 MiB of HBM per device.

v0:
```python
import math

import jax
import jax.numpy as jnp
from jax import lax
from jax.sharding import PartitionSpec as P

ITERS = 2


PRIOR = 1.0


def passed_along(array, axis, by):
    devices = lax.axis_size(axis)
    pairs = [(i, i + by) for i in range(devices) if 0 <= i + by < devices]
    return lax.ppermute(array, axis, pairs)


def padded_2(array, sides, width):
    for axis, dim in sides:
        devices, length = (lax.axis_size(axis), array.shape[dim])
        up = [(i, (i + 1) % devices) for i in range(devices - 1)]
        down = [(j, i) for i, j in up]
        last = lax.slice_in_dim(array, length - width, length, axis=dim)
        initial = lax.slice_in_dim(array, 0, width, axis=dim)
        before = lax.ppermute(last, axis, up)
        after = lax.ppermute(initial, axis, down)
        array = jnp.concatenate([before, array, after], axis=dim)
    return array


def soft_assign(local_rows, local_ids, candidates):
    window, per_block, features = candidates.shape
    flat_blocks = candidates.reshape(window * per_block, features)
    inv_scale = 0.5 / math.sqrt(features)
    cross = lax.dot_general(
        local_rows, flat_blocks, (((1,), (1,)), ((), ())), preferred_element_type=jnp.float32
    )
    cand_wide = flat_blocks.astype(jnp.float32)
    cand_norm = jnp.sum(cand_wide * cand_wide, axis=1)
    rows_wide = local_rows.astype(jnp.float32)
    rows_norm = jnp.sum(rows_wide * rows_wide, axis=1)
    logits = (2.0 * cross - rows_norm[:, None] - cand_norm[None, :]) * inv_scale
    logits = logits.reshape(local_rows.shape[0], window, per_block)
    slots = jnp.arange(window, dtype=jnp.int32)
    chosen = jnp.any(local_ids[:, :, None] == slots[None, None, :], axis=1)[:, :, None]
    masked = jnp.where(chosen, logits, -jnp.inf)
    row_top = jnp.max(masked, axis=(1, 2), keepdims=True)
    weights = jnp.where(chosen, jnp.exp(masked - row_top), 0.0)
    row_total = jnp.sum(weights, axis=(1, 2), keepdims=True)
    responses = weights / row_total
    row_cost = -(row_top[:, 0, 0] + jnp.log(row_total[:, 0, 0]))
    resp_half = responses.reshape(local_rows.shape[0], window * per_block).astype(jnp.bfloat16)
    part_sums = lax.dot_general(
        resp_half, local_rows, (((0,), (0,)), ((), ())), preferred_element_type=jnp.float32
    )
    part_counts = jnp.sum(responses, axis=0)
    return (part_sums.reshape(window, per_block, features), part_counts, row_cost)


def refresh(total, tally, previous):
    return ((total + PRIOR * previous.astype(jnp.float32)) / (tally[..., None] + PRIOR)).astype(
        jnp.bfloat16
    )


def settle_edges(part_sums, part_counts, current):
    blocks = part_sums.shape[0] - 2
    arrivals = []
    for shift_by, edge_index in ((1, blocks + 1), (-1, 0)):
        arrivals.append(
            (
                passed_along(part_sums[edge_index].astype(jnp.bfloat16), "own", shift_by).astype(
                    jnp.float32
                ),
                passed_along(part_counts[edge_index].astype(jnp.bfloat16), "own", shift_by).astype(
                    jnp.float32
                ),
            )
        )
    from_left, from_right = arrivals
    total = part_sums[1 : blocks + 1].at[0].add(from_left[0]).at[blocks - 1].add(from_right[0])
    tally = part_counts[1 : blocks + 1].at[0].add(from_left[1]).at[blocks - 1].add(from_right[1])
    return refresh(total, tally, current)


def per_device(sample_rows, destination, neighbours, centroids):
    own_count = lax.axis_size("own")
    rep_count = lax.axis_size("rep")
    count_rows, features = sample_rows.shape
    per_pair = count_rows // (own_count * rep_count)
    target = destination // count_rows
    slot_index = destination % per_pair
    outgoing = jnp.zeros((own_count, rep_count, per_pair, features), sample_rows.dtype)
    outgoing = outgoing.at[target // rep_count, target % rep_count, slot_index].set(sample_rows)
    arrived = lax.all_to_all(
        lax.all_to_all(outgoing, "own", split_axis=0, concat_axis=0, tiled=True),
        "rep",
        split_axis=1,
        concat_axis=1,
        tiled=True,
    )
    local_rows = arrived.reshape(count_rows, features)
    blocks = centroids.shape[0]
    per_block = centroids.shape[2]
    first_block = lax.axis_index("own") * blocks - 1
    local_ids = neighbours // rep_count - first_block
    current = centroids.reshape(blocks, per_block, features)
    padded = padded_2(centroids, (("own", 0),), 1)
    candidates = padded.reshape(blocks + 2, per_block, features)
    row_cost = jnp.zeros((count_rows,), jnp.float32)
    for iteration in range(ITERS):
        part_sums, part_counts, row_cost = soft_assign(local_rows, local_ids, candidates)
        if iteration + 1 == ITERS:
            current = settle_edges(part_sums, part_counts, current)
        else:
            current = settle_edges(part_sums, part_counts, current)
            padded = padded_2(current.reshape(blocks, 1, per_block, features), (("own", 0),), 1)
            candidates = padded.reshape(blocks + 2, per_block, features)
    return (current.reshape(centroids.shape), row_cost)


def solution(mesh):
    return jax.shard_map(
        per_device,
        mesh=mesh,
        in_specs=(
            P(("own", "rep"), None),
            P(("own", "rep")),
            P(("own", "rep"), None),
            P("own", "rep", None, None),
        ),
        out_specs=(P("own", "rep", None, None), P(("own", "rep"))),
        check_vma=False,
    )
```

profile of v0, /device:TPU:32, one launch (start us, length us, event | category | flops | bytes accessed | tf_op | source)
XLA Modules:
  0.0 187.8 jit_solution(11261145202051379233)
XLA Ops:
  0.6 0.7 compare_select_fusion.2
  1.3 0.7 and_reduce_fusion
  2.1 0.7 multiply_reduce_fusion.3
  2.8 6.2 %scatter_custom_fusion = bf16[1024,768]{1,0:T(8,128)(2,1)S(1)} fusion(s32[1024]{0:T(1024)S(1)} %broadcast_select_fusion, bf16[1024,768]{1,0:T(8,128)(2,1)} %param.20, bf16[]{:T(256)} %constant.263.clone.1), kind=kCustom, calls=%fused_computation.21 | custom fusion | bytes 1573376
  9.1 0.6 reshape.395
  9.7 54.8 %all_to_all.10 = bf16[64,8,2,768]{3,2,1,0:T(2,128)(2,1)S(1)} all-to-all(bf16[64,8,2,768]{3,2,1,0:T(2,128)(2,1)S(1)} %reshape.395), channel_id=1, replica_groups=mesh['own'=64,'rep'=8] {'own'}, dimensions={0} | all-to-all | bytes 3145728 | tf_op jit(solution)/shard_map/all_to_all | solution.py:98
  64.5 2.4 %copy.42 = bf16[64,8,2,768]{3,2,0,1:T(2,128)(2,1)} copy(bf16[64,8,2,768]{3,2,1,0:T(2,128)(2,1)S(1)} %all_to_all.10) | data formatting | bytes 3145728 | tf_op jit(solution)/shard_map/all_to_all | solution.py:98
  66.9 4.4 %all-to-all-start.1 = ((bf16[64,8,2,768]{3,2,0,1:T(2,128)(2,1)}), bf16[64,8,2,768]{3,2,0,1:T(2,128)(2,1)S(1)}, u32[]{:S(2)}, u32[]{:S(2)}) async-start(bf16[64,8,2,768]{3,2,0,1:T(2,128)(2,1)} %copy.42), calls=%async_computation.1 | async-start | bytes 3145728 | tf_op jit(solution)/shard_map/all_to_all | solution.py:97
  71.3 0.0 copy-done.1
  71.4 7.2 %collective-permute-start.1 = (bf16[1,1,128,768]{3,2,1,0:T(8,128)(2,1)S(1)}, bf16[1,1,128,768]{3,2,1,0:T(8,128)(2,1)S(1)}, u32[]{:S(2)}, u32[]{:S(2)}) collective-permute-start(bf16[1,1,128,768]{3,2,1,0:T(8,128)(2,1)S(1)} %get-tuple-element.122), channel_id=1, source_target_pairs={{8,0},{16,8},{24,16},{32,24},{40,32},{48,40},{56,48},{64,56},{72,6... | collective-permute-start | bytes 589832 | tf_op jit(solution)/shard_map/ppermute | solution.py:28
  78.6 2.1 %collective-permute-start = (bf16[1,1,128,768]{3,2,1,0:T(8,128)(2,1)S(1)}, bf16[1,1,128,768]{3,2,1,0:T(8,128)(2,1)S(1)}, u32[]{:S(2)}, u32[]{:S(2)}) collective-permute-start(bf16[1,1,128,768]{3,2,1,0:T(8,128)(2,1)S(1)} %get-tuple-element.123), channel_id=1, source_target_pairs={{0,8},{8,16},{16,24},{24,32},{32,40},{40,48},{48,56},{56,64},{64,7... | collective-permute-start | bytes 589832 | tf_op jit(solution)/shard_map/ppermute | solution.py:27
  80.7 0.0 copy-done.5
  80.8 0.1 fusion.19
  80.8 10.0 %collective-permute-done = bf16[1,1,128,768]{3,2,1,0:T(8,128)(2,1)S(1)} collective-permute-done((bf16[1,1,128,768]{3,2,1,0:T(8,128)(2,1)S(1)}, bf16[1,1,128,768]{3,2,1,0:T(8,128)(2,1)S(1)}, u32[]{:S(2)}, u32[]{:S(2)}) %collective-permute-start) | collective-permute-done | bytes 196640 | tf_op jit(solution)/shard_map/ppermute | solution.py:27
  90.9 0.1 constant_dynamic-update-slice_fusion.1
  90.9 0.0 collective-permute-done.1
  91.0 0.0 copy-start
  91.0 1.0 copy-done
  92.0 0.3 multiply_reduce_fusion.2
  92.3 0.7 all-to-all-done.1
  92.9 2.2 %copy.43 = bf16[64,8,2,768]{3,2,1,0:T(2,128)(2,1)} copy(bf16[64,8,2,768]{3,2,0,1:T(2,128)(2,1)S(1)} %all-to-all-done.1) | data formatting | bytes 3145728 | tf_op jit(solution)/shard_map/all_to_all | solution.py:97
  95.2 3.7 %reshape.385 = bf16[1024,768]{1,0:T(8,128)(2,1)S(1)} reshape(bf16[64,8,2,768]{3,2,1,0:T(2,128)(2,1)} %copy.43) | data formatting | bytes 3145728 | tf_op jit(solution)/shard_map/reshape | solution.py:104
  98.8 1.7 multiply_reduce_fusion
  100.5 0.2 copy.44
  100.7 0.2 sub.89
  100.9 2.8 %fusion.29 = (f32[1024]{0:T(1024)S(1)}, f32[1024,768]{0,1:T(8,128)S(1)}) fusion(f32[768]{0:T(1024)S(1)} %bitcast.101, f32[1024]{0:T(1024)S(1)} %sub.89, pred[1024,6]{0,1:T(8,128)(4,1)S(1)} %fusion.19, bf16[1024,768]{1,0:T(8,128)(2,1)S(1)} %reshape.385, bf16[768,768]{1,0:T(8,128)(2,1)} %bitcast.98), kind=kOutput, calls=%fused_computation.84 | convolution fusion | flops 1212677120 | bytes 5915648 | tf_op jit(solution)/shard_map/dot_general | solution.py:37
  103.7 1.1 fusion.1
  104.8 1.4 fusion.32
  106.3 7.2 %collective-permute-start.5 = (bf16[128]{0:T(256)(128)(2,1)S(1)}, bf16[128]{0:T(256)(128)(2,1)S(1)}, u32[]{:S(2)}, u32[]{:S(2)}) collective-permute-start(bf16[128]{0:T(256)(128)(2,1)S(1)} %get-tuple-element.129), channel_id=1, source_target_pairs={{8,0},{16,8},{24,16},{32,24},{40,32},{48,40},{56,48},{64,56},{72,6... | collective-permute-start | bytes 776 | tf_op jit(solution)/shard_map/ppermute | solution.py:17
  113.5 1.9 %collective-permute-start.4 = (bf16[128]{0:T(256)(128)(2,1)S(1)}, bf16[128]{0:T(256)(128)(2,1)S(1)}, u32[]{:S(2)}, u32[]{:S(2)}) collective-permute-start(bf16[128]{0:T(256)(128)(2,1)S(1)} %get-tuple-element.130), channel_id=1, source_target_pairs={{0,8},{8,16},{16,24},{24,32},{32,40},{40,48},{48,56},{56,64},{64,7... | collective-permute-start | bytes 776 | tf_op jit(solution)/shard_map/ppermute | solution.py:17
  115.4 1.4 fusion.39
  116.8 0.0 copy-start.4
  116.9 7.2 %collective-permute-start.3 = (bf16[128,768]{1,0:T(8,128)(2,1)S(1)}, bf16[128,768]{1,0:T(8,128)(2,1)S(1)}, u32[]{:S(2)}, u32[]{:S(2)}) collective-permute-start(bf16[128,768]{1,0:T(8,128)(2,1)S(1)} %get-tuple-element.118), channel_id=1, source_target_pairs={{8,0},{16,8},{24,16},{32,24},{40,32},{48,40},{56,48},{64,56},{72,6... | collective-permute-start | bytes 589832 | tf_op jit(solution)/shard_map/ppermute | solution.py:17
  124.1 1.9 %collective-permute-start.2 = (bf16[128,768]{1,0:T(8,128)(2,1)S(1)}, bf16[128,768]{1,0:T(8,128)(2,1)S(1)}, u32[]{:S(2)}, u32[]{:S(2)}) collective-permute-start(bf16[128,768]{1,0:T(8,128)(2,1)S(1)} %get-tuple-element.119), channel_id=1, source_target_pairs={{0,8},{8,16},{16,24},{24,32},{32,40},{40,48},{48,56},{56,64},{64,7... | collective-permute-start | bytes 589832 | tf_op jit(solution)/shard_map/ppermute | solution.py:17
  126.0 1.3 slice.288
  127.3 0.0 collective-permute-done.4
  127.4 0.0 collective-permute-done.5
  127.4 7.6 %collective-permute-done.2 = bf16[128,768]{1,0:T(8,128)(2,1)S(1)} collective-permute-done((bf16[128,768]{1,0:T(8,128)(2,1)S(1)}, bf16[128,768]{1,0:T(8,128)(2,1)S(1)}, u32[]{:S(2)}, u32[]{:S(2)}) %collective-permute-start.2) | collective-permute-done | bytes 196640 | tf_op jit(solution)/shard_map/ppermute | solution.py:17
  135.0 1.8 fusion.18
  136.8 0.0 collective-permute-done.3
  136.8 1.8 fusion.16
  138.5 1.6 fusion.5
  140.2 1.9 %collective-permute-start.6 = (bf16[1,1,128,768]{3,2,0,1:T(8,128)(2,1)S(1)}, bf16[1,1,128,768]{3,2,0,1:T(8,128)(2,1)S(1)}, u32[]{:S(2)}, u32[]{:S(2)}) collective-permute-start(bf16[1,1,128,768]{3,2,0,1:T(8,128)(2,1)S(1)} %get-tuple-element.120), channel_id=1, source_target_pairs={{0,8},{8,16},{16,24},{24,32},{32,40},{40,48},{48,56},{56,64},{64,7... | collective-permute-start | bytes 589832 | tf_op jit(solution)/shard_map/ppermute | solution.py:27
  142.1 7.5 %collective-permute-start.7 = (bf16[1,1,128,768]{3,2,1,0:T(8,128)(2,1)S(1)}, bf16[1,1,128,768]{3,2,1,0:T(8,128)(2,1)S(1)}, u32[]{:S(2)}, u32[]{:S(2)}) collective-permute-start(bf16[1,1,128,768]{3,2,1,0:T(8,128)(2,1)S(1)} %get-tuple-element.121), channel_id=1, source_target_pairs={{8,0},{16,8},{24,16},{32,24},{40,32},{48,40},{56,48},{64,56},{72,6... | collective-permute-start | bytes 589832 | tf_op jit(solution)/shard_map/ppermute | solution.py:28
  149.6 1.5 collective-permute-done.6
  151.1 1.5 collective-permute-done.7
  152.5 0.3 multiply_reduce_fusion.1
  152.8 1.6 fusion.40
  154.4 0.6 fusion.3
  155.0 0.8 fusion.30
  155.8 0.6 add_negate_fusion
  156.4 7.7 %collective-permute-start.11 = (bf16[128]{0:T(256)(128)(2,1)S(1)}, bf16[128]{0:T(256)(128)(2,1)S(1)}, u32[]{:S(2)}, u32[]{:S(2)}) collective-permute-start(bf16[128]{0:T(256)(128)(2,1)S(1)} %get-tuple-element.127), channel_id=1, source_target_pairs={{8,0},{16,8},{24,16},{32,24},{40,32},{48,40},{56,48},{64,56},{72,6... | collective-permute-start | bytes 776 | tf_op jit(solution)/shard_map/ppermute | solution.py:17
  164.1 1.9 %collective-permute-start.10 = (bf16[128]{0:T(256)(128)(2,1)S(1)}, bf16[128]{0:T(256)(128)(2,1)S(1)}, u32[]{:S(2)}, u32[]{:S(2)}) collective-permute-start(bf16[128]{0:T(256)(128)(2,1)S(1)} %get-tuple-element.128), channel_id=1, source_target_pairs={{0,8},{8,16},{16,24},{24,32},{32,40},{40,48},{48,56},{56,64},{64,7... | collective-permute-start | bytes 776 | tf_op jit(solution)/shard_map/ppermute | solution.py:17
  166.0 1.4 fusion.41
  167.5 7.2 %collective-permute-start.9 = (bf16[128,768]{1,0:T(8,128)(2,1)S(1)}, bf16[128,768]{1,0:T(8,128)(2,1)S(1)}, u32[]{:S(2)}, u32[]{:S(2)}) collective-permute-start(bf16[128,768]{1,0:T(8,128)(2,1)S(1)} %get-tuple-element.116), channel_id=1, source_target_pairs={{8,0},{16,8},{24,16},{32,24},{40,32},{48,40},{56,48},{64,56},{72,6... | collective-permute-start | bytes 589832 | tf_op jit(solution)/shard_map/ppermute | solution.py:17
  174.7 1.9 %collective-permute-start.8 = (bf16[128,768]{1,0:T(8,128)(2,1)S(1)}, bf16[128,768]{1,0:T(8,128)(2,1)S(1)}, u32[]{:S(2)}, u32[]{:S(2)}) collective-permute-start(bf16[128,768]{1,0:T(8,128)(2,1)S(1)} %get-tuple-element.117), channel_id=1, source_target_pairs={{0,8},{8,16},{16,24},{24,32},{32,40},{40,48},{48,56},{56,64},{64,7... | collective-permute-start | bytes 589832 | tf_op jit(solution)/shard_map/ppermute | solution.py:17
  176.6 0.1 slice.295
  176.8 0.0 collective-permute-done.10
  176.8 0.0 collective-permute-done.11
  176.9 8.7 %collective-permute-done.8 = bf16[128,768]{1,0:T(8,128)(2,1)S(1)} collective-permute-done((bf16[128,768]{1,0:T(8,128)(2,1)S(1)}, bf16[128,768]{1,0:T(8,128)(2,1)S(1)}, u32[]{:S(2)}, u32[]{:S(2)}) %collective-permute-start.8) | collective-permute-done | bytes 196640 | tf_op jit(solution)/shard_map/ppermute | solution.py:17
  185.6 1.0 fusion.15
  186.6 0.0 collective-permute-done.9
  186.6 0.1 fusion.13
  186.7 1.1 fusion.12
  (31 shorter events, 0.4 us)
Async XLA Ops:
  66.9 4.4 %copy-start.1 = (bf16[4,1,128,768]{3,2,1,0:T(8,128)(2,1)S(1)}, bf16[4,1,128,768]{3,2,1,0:T(8,128)(2,1)}, u32[]{:S(2)}) copy-start(bf16[4,1,128,768]{3,2,1,0:T(8,128)(2,1)} %param.23) | copy-start | bytes 2359300
  66.9 13.8 %copy-start.5 = (s32[1024,4]{0,1:T(4,128)S(1)}, s32[1024,4]{0,1:T(4,128)}, u32[]{:S(2)}) copy-start(s32[1024,4]{0,1:T(4,128)} %param.22) | copy-start | bytes 49156
  66.9 26.0 %all-to-all-start.1 = ((bf16[64,8,2,768]{3,2,0,1:T(2,128)(2,1)}), bf16[64,8,2,768]{3,2,0,1:T(2,128)(2,1)S(1)}, u32[]{:S(2)}, u32[]{:S(2)}) async-start(bf16[64,8,2,768]{3,2,0,1:T(2,128)(2,1)} %copy.42), calls=%async_computation.1 | async-start | bytes 3145728 | tf_op jit(solution)/shard_map/all_to_all | solution.py:97
  71.4 19.5 %collective-permute-start.1 = (bf16[1,1,128,768]{3,2,1,0:T(8,128)(2,1)S(1)}, bf16[1,1,128,768]{3,2,1,0:T(8,128)(2,1)S(1)}, u32[]{:S(2)}, u32[]{:S(2)}) collective-permute-start(bf16[1,1,128,768]{3,2,1,0:T(8,128)(2,1)S(1)} %get-tuple-element.122), channel_id=1, source_target_pairs={{8,0},{16,8},{24,16},{32,24},{40,32},{48,40},{56,48},{64,56},{72,6... | collective-permute-start | bytes 589832 | tf_op jit(solution)/shard_map/ppermute | solution.py:28
  78.6 12.2 %collective-permute-start = (bf16[1,1,128,768]{3,2,1,0:T(8,128)(2,1)S(1)}, bf16[1,1,128,768]{3,2,1,0:T(8,128)(2,1)S(1)}, u32[]{:S(2)}, u32[]{:S(2)}) collective-permute-start(bf16[1,1,128,768]{3,2,1,0:T(8,128)(2,1)S(1)} %get-tuple-element.123), channel_id=1, source_target_pairs={{0,8},{8,16},{16,24},{24,32},{32,40},{40,48},{48,56},{56,64},{64,7... | collective-permute-start | bytes 589832 | tf_op jit(solution)/shard_map/ppermute | solution.py:27
  91.0 1.0 copy-start
  106.3 21.1 %collective-permute-start.5 = (bf16[128]{0:T(256)(128)(2,1)S(1)}, bf16[128]{0:T(256)(128)(2,1)S(1)}, u32[]{:S(2)}, u32[]{:S(2)}) collective-permute-start(bf16[128]{0:T(256)(128)(2,1)S(1)} %get-tuple-element.129), channel_id=1, source_target_pairs={{8,0},{16,8},{24,16},{32,24},{40,32},{48,40},{56,48},{64,56},{72,6... | collective-permute-start | bytes 776 | tf_op jit(solution)/shard_map/ppermute | solution.py:17
  113.5 13.8 %collective-permute-start.4 = (bf16[128]{0:T(256)(128)(2,1)S(1)}, bf16[128]{0:T(256)(128)(2,1)S(1)}, u32[]{:S(2)}, u32[]{:S(2)}) collective-permute-start(bf16[128]{0:T(256)(128)(2,1)S(1)} %get-tuple-element.130), channel_id=1, source_target_pairs={{0,8},{8,16},{16,24},{24,32},{32,40},{40,48},{48,56},{56,64},{64,7... | collective-permute-start | bytes 776 | tf_op jit(solution)/shard_map/ppermute | solution.py:17
  116.8 10.5 %copy-start.4 = (f32[768,768]{1,0:T(8,128)}, f32[768,768]{1,0:T(8,128)S(1)}, u32[]{:S(2)}) copy-start(f32[768,768]{1,0:T(8,128)S(1)} %get-tuple-element.134) | copy-start | bytes 7077892
  116.9 19.9 %collective-permute-start.3 = (bf16[128,768]{1,0:T(8,128)(2,1)S(1)}, bf16[128,768]{1,0:T(8,128)(2,1)S(1)}, u32[]{:S(2)}, u32[]{:S(2)}) collective-permute-start(bf16[128,768]{1,0:T(8,128)(2,1)S(1)} %get-tuple-element.118), channel_id=1, source_target_pairs={{8,0},{16,8},{24,16},{32,24},{40,32},{48,40},{56,48},{64,56},{72,6... | collective-permute-start | bytes 589832 | tf_op jit(solution)/shard_map/ppermute | solution.py:17
  124.1 10.9 %collective-permute-start.2 = (bf16[128,768]{1,0:T(8,128)(2,1)S(1)}, bf16[128,768]{1,0:T(8,128)(2,1)S(1)}, u32[]{:S(2)}, u32[]{:S(2)}) collective-permute-start(bf16[128,768]{1,0:T(8,128)(2,1)S(1)} %get-tuple-element.119), channel_id=1, source_target_pairs={{0,8},{8,16},{16,24},{24,32},{32,40},{40,48},{48,56},{56,64},{64,7... | collective-permute-start | bytes 589832 | tf_op jit(solution)/shard_map/ppermute | solution.py:17
  127.3 11.2 %copy-start.2 = (bf16[4,1,128,768]{3,2,1,0:T(8,128)(2,1)S(1)}, bf16[4,1,128,768]{3,2,1,0:T(8,128)(2,1)}, u32[]{:S(2)}) copy-start(bf16[4,1,128,768]{3,2,1,0:T(8,128)(2,1)} %param.23) | copy-start | bytes 2359300
  140.2 10.9 %collective-permute-start.6 = (bf16[1,1,128,768]{3,2,0,1:T(8,128)(2,1)S(1)}, bf16[1,1,128,768]{3,2,0,1:T(8,128)(2,1)S(1)}, u32[]{:S(2)}, u32[]{:S(2)}) collective-permute-start(bf16[1,1,128,768]{3,2,0,1:T(8,128)(2,1)S(1)} %get-tuple-element.120), channel_id=1, source_target_pairs={{0,8},{8,16},{16,24},{24,32},{32,40},{40,48},{48,56},{56,64},{64,7... | collective-permute-start | bytes 589832 | tf_op jit(solution)/shard_map/ppermute | solution.py:27
  142.1 10.4 %collective-permute-start.7 = (bf16[1,1,128,768]{3,2,1,0:T(8,128)(2,1)S(1)}, bf16[1,1,128,768]{3,2,1,0:T(8,128)(2,1)S(1)}, u32[]{:S(2)}, u32[]{:S(2)}) collective-permute-start(bf16[1,1,128,768]{3,2,1,0:T(8,128)(2,1)S(1)} %get-tuple-element.121), channel_id=1, source_target_pairs={{8,0},{16,8},{24,16},{32,24},{40,32},{48,40},{56,48},{64,56},{72,6... | collective-permute-start | bytes 589832 | tf_op jit(solution)/shard_map/ppermute | solution.py:28
  156.4 20.5 %collective-permute-start.11 = (bf16[128]{0:T(256)(128)(2,1)S(1)}, bf16[128]{0:T(256)(128)(2,1)S(1)}, u32[]{:S(2)}, u32[]{:S(2)}) collective-permute-start(bf16[128]{0:T(256)(128)(2,1)S(1)} %get-tuple-element.127), channel_id=1, source_target_pairs={{8,0},{16,8},{24,16},{32,24},{40,32},{48,40},{56,48},{64,56},{72,6... | collective-permute-start | bytes 776 | tf_op jit(solution)/shard_map/ppermute | solution.py:17
  164.1 12.7 %collective-permute-start.10 = (bf16[128]{0:T(256)(128)(2,1)S(1)}, bf16[128]{0:T(256)(128)(2,1)S(1)}, u32[]{:S(2)}, u32[]{:S(2)}) collective-permute-start(bf16[128]{0:T(256)(128)(2,1)S(1)} %get-tuple-element.128), channel_id=1, source_target_pairs={{0,8},{8,16},{16,24},{24,32},{32,40},{40,48},{48,56},{56,64},{64,7... | collective-permute-start | bytes 776 | tf_op jit(solution)/shard_map/ppermute | solution.py:17
  167.4 9.3 %copy-start.3 = (f32[768,768]{1,0:T(8,128)}, f32[768,768]{1,0:T(8,128)S(1)}, u32[]{:S(2)}) copy-start(f32[768,768]{1,0:T(8,128)S(1)} %get-tuple-element.138) | copy-start | bytes 7077892
  167.5 19.2 %collective-permute-start.9 = (bf16[128,768]{1,0:T(8,128)(2,1)S(1)}, bf16[128,768]{1,0:T(8,128)(2,1)S(1)}, u32[]{:S(2)}, u32[]{:S(2)}) collective-permute-start(bf16[128,768]{1,0:T(8,128)(2,1)S(1)} %get-tuple-element.116), channel_id=1, source_target_pairs={{8,0},{16,8},{24,16},{32,24},{40,32},{48,40},{56,48},{64,56},{72,6... | collective-permute-start | bytes 589832 | tf_op jit(solution)/shard_map/ppermute | solution.py:17
  174.7 10.9 %collective-permute-start.8 = (bf16[128,768]{1,0:T(8,128)(2,1)S(1)}, bf16[128,768]{1,0:T(8,128)(2,1)S(1)}, u32[]{:S(2)}, u32[]{:S(2)}) collective-permute-start(bf16[128,768]{1,0:T(8,128)(2,1)S(1)} %get-tuple-element.117), channel_id=1, source_target_pairs={{0,8},{8,16},{16,24},{24,32},{32,40},{40,48},{48,56},{56,64},{64,7... | collective-permute-start | bytes 589832 | tf_op jit(solution)/shard_map/ppermute | solution.py:17
where the time goes:
time: 189 us; the launch traced here: 188 us
  starting transfers between devices  60.2 us (32%)
  blocking collectives  54.8 us (29%)
  waiting for transfers between devices  29.9 us (16%)
  local copies, waits for them, and re-layouts  18.2 us (10%)
  other arithmetic  16.4 us (9%)
  matrix products  7.2 us (4%)
    all_to_all x1, blocking collectives, per_device(): lax.all_to_all(outgoing, 'own', split_axis=0, concat_axis=0, tiled=True)  54.8 us
    ppermute x8, starting transfers between devices, passed_along(): return lax.ppermute(array, axis, pairs)  37.1 us
    ppermute x8, waiting for transfers between devices, passed_along(): return lax.ppermute(array, axis, pairs)  16.3 us
    ppermute x2, starting transfers between devices, padded_2(): after = lax.ppermute(initial, axis, down)  14.7 us
    ppermute x2, waiting for transfers between devices, padded_2(): before = lax.ppermute(last, axis, up)  11.5 us
    unnamed x15, local copies, waits for them, and re-layouts  7.31 us
    scatter-add x4, other arithmetic, settle_edges(): part_sums[1:blocks + 1].at[0].add(from_left[0]).at[blocks - 1]  4.64 us
    all_to_all x1, starting transfers between devices, per_device(): lax.all_to_all(lax.all_to_all(outgoing, 'own', split_axis=0, concat_axis=...  4.43 us
  transfers between devices with their start and end apart: 13, of which 6 were waited for; matrix products, arithmetic and copies ran while one was open for 4% of the time, Pallas kernels for 0%

commit v1 on v0

v1 whole, which is shorter than its diff:
```python
import functools
import math

import jax
import jax.numpy as jnp
from jax import lax
from jax.experimental import pallas as pl
from jax.experimental.pallas import tpu as pltpu
from jax.sharding import PartitionSpec as P

PRIOR = 1.0
LOG2E = 1.4426950408889634
LANES = 128
MASS_ROWS = 16
VMEM = pl.BlockSpec(memory_space=pltpu.VMEM)
F32 = jnp.float32
BF16 = jnp.bfloat16


def call(kernel, outs, scratch=(), flops=0, limit=24):
    return pl.pallas_call(
        kernel,
        out_shape=outs,
        out_specs=jax.tree.map(lambda _: VMEM, outs),
        scratch_shapes=list(scratch),
        compiler_params=pltpu.CompilerParams(vmem_limit_bytes=limit << 20),
        cost_estimate=pl.CostEstimate(flops=flops, bytes_accessed=1 << 20, transcendentals=0),
    )


def sds(shape, dtype):
    return jax.ShapeDtypeStruct(shape, dtype)


def matmul(a, b, contract):
    return lax.dot_general(a, b, (contract, ((), ())), preferred_element_type=F32)


def regroup_kernel(pairs, dest_ref, rows_ref, out_ref, wide):
    count, features = rows_ref.shape
    per_pair = count // pairs
    chunks = features // LANES
    dest = dest_ref[...]
    place = lax.rem(dest, per_pair) * pairs + lax.div(dest, count)
    rows = rows_ref[...]
    step = 256
    for start in range(0, count, step):
        ids = lax.broadcasted_iota(jnp.int32, (step, count), 0) + start
        pick = jnp.where(ids == place, 1.0, 0.0).astype(BF16)
        moved = matmul(pick, rows, ((1,), (0,)))
        slot, first = divmod(start, pairs)
        for f in range(chunks):
            line = (first * chunks + f) * per_pair + slot
            wide[pl.ds(line, step, stride=chunks * per_pair), :] = moved[:, f * LANES : (f + 1) * LANES]
    lines = count * chunks
    for start in range(0, lines, 512):
        out_ref[pl.ds(start, 512), :] = wide[pl.ds(start, 512), :].astype(BF16)


def unpack_rows(lines_ref, rows_ref, wide, pairs):
    count, features = rows_ref.shape
    per_pair = count // pairs
    chunks = features // LANES
    for start in range(0, count * chunks, 512):
        wide[pl.ds(start, 512), :] = lines_ref[pl.ds(start, 512), :].astype(F32)
    for slot in range(per_pair):
        for f in range(chunks):
            part = wide[pl.ds(f * per_pair + slot, pairs, stride=chunks * per_pair), :]
            rows_ref[pl.ds(slot * pairs, pairs), f * LANES : (f + 1) * LANES] = part.astype(BF16)


def assign(rows_ref, ids_ref, blocks, resp_ref, tops_ref=None):
    count, features = rows_ref.shape
    window = len(blocks)
    half = 0.5 * LOG2E / math.sqrt(features)
    bias = []
    for block in blocks:
        wide = block.astype(F32)
        bias.append(jnp.sum(wide * wide, axis=1, keepdims=True) * half)
    flat = jnp.concatenate(blocks, axis=0)
    per_block = blocks[0].shape[0]
    mass = [0.0] * window
    step = 256
    for start in range(0, count, step):
        rows = rows_ref[pl.ds(start, step), :]
        ids = ids_ref[:, start : start + step]
        cross = matmul(flat, rows, ((1,), (1,)))
        scores = []
        top = None
        for w in range(window):
            hit = jnp.max(jnp.where(ids == w, 0.0, -jnp.inf), axis=0, keepdims=True)
            score = cross[w * per_block : (w + 1) * per_block] * (2.0 * half) - bias[w] + hit
            scores.append(score)
            here = jnp.max(score, axis=0, keepdims=True)
            top = here if top is None else jnp.maximum(top, here)
        total = None
        for w in range(window):
            scores[w] = jnp.exp2(scores[w] - top)
            here = jnp.sum(scores[w], axis=0, keepdims=True)
            total = here if total is None else total + here
        scale = 1.0 / total
        for w in range(window):
            resp = scores[w] * scale
            resp_ref[w * per_block : (w + 1) * per_block, start : start + step] = resp.astype(BF16)
            mass[w] = mass[w] + resp
        if tops_ref is not None:
            tops_ref[:, start : start + step] = top * (1.0 / LOG2E) + jnp.log(total)
    return [jnp.sum(m, axis=1, keepdims=True) for m in mass]


def diagonal(size):
    across = lax.broadcasted_iota(jnp.int32, (size, size), 0)
    return across == lax.broadcasted_iota(jnp.int32, (size, size), 1)


def pack_mass(masses):
    size = masses[0].shape[0]
    eye = diagonal(size)
    lines = [jnp.sum(jnp.where(eye, m, 0.0), axis=0, keepdims=True) for m in masses]
    line = jnp.concatenate(lines, axis=1)
    high = line.astype(BF16).astype(F32)
    row = lax.broadcasted_iota(jnp.int32, (MASS_ROWS, line.shape[1]), 0)
    return jnp.where(row == 0, high, jnp.where(row == 1, line - high, 0.0)).astype(BF16)


def unpack_mass(packed, which, size):
    line = packed[:, which * size : (which + 1) * size].astype(F32)
    line = jnp.sum(line, axis=0, keepdims=True)
    return jnp.sum(jnp.where(diagonal(size), line, 0.0), axis=1, keepdims=True)


def package(pkg_ref, sums, masses):
    size = masses[0].shape[0]
    blocks = len(sums)
    for k in range(blocks):
        pkg_ref[k * size : (k + 1) * size, :] = sums[k].astype(BF16)
    packed = pack_mass(masses)
    pkg_ref[blocks * size :, : blocks * size] = packed
    rest = pkg_ref.shape[1] - blocks * size
    pkg_ref[blocks * size :, blocks * size :] = jnp.zeros((MASS_ROWS, rest), BF16)


def refresh(total, tally, previous):
    return ((total + PRIOR * previous.astype(F32)) / (tally + PRIOR)).astype(BF16)


def window_blocks(left_ref, own_ref, right_ref):
    return [left_ref[...]] + [own_ref[k] for k in range(own_ref.shape[0])] + [right_ref[...]]


def first_kernel(
    pairs, lines_ref, ids_ref, left_ref, own_ref, right_ref,
    rows_ref, resp_ref, sums_ref, mass_ref, up_ref, down_ref, wide,
):
    unpack_rows(lines_ref, rows_ref, wide, pairs)
    blocks = window_blocks(left_ref, own_ref, right_ref)
    mass = assign(rows_ref, ids_ref, blocks, resp_ref)
    size = own_ref.shape[1]
    last = len(blocks) - 1
    rows = rows_ref[...]
    sums = {}
    for w in (0, 1, last - 1, last):
        sums[w] = matmul(resp_ref[w * size : (w + 1) * size, :], rows, ((1,), (0,)))
        sums_ref[w] = sums[w]
    for w in range(last + 1):
        mass_ref[w * size : (w + 1) * size, :] = mass[w]
    package(up_ref, [sums[last - 1], sums[last]], [mass[last - 1], mass[last]])
    package(down_ref, [sums[0], sums[1]], [mass[0], mass[1]])


def inner_kernel(rows_ref, resp_ref, mass_ref, own_ref, fresh_ref, norm_ref):
    blocks, size, _ = own_ref.shape
    rows = rows_ref[...]
    for k in range(1, blocks - 1):
        w = k + 1
        total = matmul(resp_ref[w * size : (w + 1) * size, :], rows, ((1,), (0,)))
        fresh_ref[k - 1] = refresh(total, mass_ref[w * size : (w + 1) * size, :], own_ref[k])
    eye = diagonal(LANES)
    for start in range(0, rows_ref.shape[0], LANES):
        wide = rows_ref[pl.ds(start, LANES), :].astype(F32)
        norm = jnp.sum(wide * wide, axis=1, keepdims=True)
        norm_ref[:, start : start + LANES] = jnp.sum(jnp.where(eye, norm, 0.0), axis=0, keepdims=True)


def second_kernel(
    rows_ref, ids_ref, left_ref, own_ref, right_ref, sums_ref, mass_ref, fresh_ref, norm_ref, below_ref, above_ref,
    edge_ref, resp_ref, mass_out, cost_ref, up_ref, down_ref,
):
    count, size, _ = own_ref.shape
    last = count + 1
    old = {0: left_ref[...], 1: own_ref[0], last - 1: own_ref[count - 1], last: right_ref[...]}
    new = {}
    for pkg, ws in ((below_ref, (0, 1)), (above_ref, (last - 1, last))):
        packed = pkg[2 * size :, : 2 * size]
        for k, w in enumerate(ws):
            total = sums_ref[w] + pkg[k * size : (k + 1) * size, :].astype(F32)
            tally = mass_ref[w * size : (w + 1) * size, :] + unpack_mass(packed, k, size)
            new[w] = refresh(total, tally, old[w])
    edge_ref[0] = new[1]
    edge_ref[1] = new[last - 1]
    blocks = [new[0], new[1]] + [fresh_ref[k] for k in range(count - 2)] + [new[last - 1], new[last]]
    mass = assign(rows_ref, ids_ref, blocks, resp_ref, cost_ref)
    half = 0.5 / math.sqrt(rows_ref.shape[1])
    cost_ref[...] = norm_ref[...] * half - cost_ref[...]
    for w in range(last + 1):
        mass_out[w * size : (w + 1) * size, :] = mass[w]
    rows = rows_ref[...]
    for pkg, w in ((up_ref, last), (down_ref, 0)):
        total = matmul(resp_ref[w * size : (w + 1) * size, :], rows, ((1,), (0,)))
        package(pkg, [total], [mass[w]])


def own_kernel(rows_ref, resp_ref, mass_ref, edge_ref, fresh_ref, done_ref, part_ref):
    blocks, size, _ = part_ref.shape[0] + fresh_ref.shape[0], part_ref.shape[1], None
    rows = rows_ref[...]
    for k in range(blocks):
        w = k + 1
        total = matmul(resp_ref[w * size : (w + 1) * size, :], rows, ((1,), (0,)))
        if 0 < k < blocks - 1:
            done_ref[k - 1] = refresh(total, mass_ref[w * size : (w + 1) * size, :], fresh_ref[k - 1])
        else:
            part_ref[0 if k == 0 else 1] = total


def last_kernel(done_ref, part_ref, mass_ref, edge_ref, below_ref, above_ref, out_ref):
    blocks, size, _ = out_ref.shape
    for k in range(1, blocks - 1):
        out_ref[k] = done_ref[k - 1]
    for e, (k, pkg) in enumerate(((0, below_ref), (blocks - 1, above_ref))):
        w = k + 1
        total = part_ref[e] + pkg[:size, :].astype(F32)
        tally = mass_ref[w * size : (w + 1) * size, :] + unpack_mass(pkg[size:, :size], 0, size)
        out_ref[k] = refresh(total, tally, edge_ref[e])


def swap(up, down, axis):
    devices = lax.axis_size(axis)
    pairs = [(i, i + 1) for i in range(devices - 1)]
    below = lax.ppermute(up, axis, pairs)
    above = lax.ppermute(down, axis, [(j, i) for i, j in pairs])
    return below, above


def per_device(sample_rows, destination, neighbours, centroids):
    own_count, rep_count = lax.axis_size("own"), lax.axis_size("rep")
    pairs = own_count * rep_count
    count, features = sample_rows.shape
    per_pair = count // pairs
    chunks = features // LANES
    lines = count * chunks
    blocks, _, size, _ = centroids.shape
    window = blocks + 2
    own = centroids.reshape(blocks, size, features)
    wide = pltpu.VMEM((lines + chunks * per_pair + 4, LANES), F32)
    dot = 2 * count * features

    outgoing = call(
        functools.partial(regroup_kernel, pairs), sds((lines, LANES), BF16), [wide], dot * count
    )(destination.reshape(1, count), sample_rows)
    left, right = swap(own[blocks - 1], own[0], "own")
    first_block = lax.axis_index("own") * blocks - 1
    ids = (neighbours // rep_count - first_block).T
    ids = ids.reshape(-1, pairs, per_pair).swapaxes(1, 2).reshape(-1, count)
    arrived = lax.all_to_all(
        outgoing.reshape(pairs, lines // pairs // 4, 4, LANES), ("own", "rep"), split_axis=0, concat_axis=0, tiled=True
    ).reshape(lines, LANES)

    resp = sds((window * size, count), BF16)
    mass = sds((window * size, 1), F32)
    two = sds((2 * size + MASS_ROWS, features), BF16)
    one = sds((size + MASS_ROWS, features), BF16)
    inner = sds((blocks - 2, size, features), BF16)
    rows, resp1, sums1, mass1, up1, down1 = call(
        functools.partial(first_kernel, pairs),
        (sds((count, features), BF16), resp, sds((window, size, features), F32), mass, two, two),
        [wide],
        dot * (window + 4) * size,
    )(arrived, ids, left, own, right)
    below1, above1 = swap(up1, down1, "own")
    fresh, norm = call(inner_kernel, (inner, sds((1, count), F32)), (), dot * 2 * size)(rows, resp1, mass1, own)
    edge, resp2, mass2, cost, up2, down2 = call(
        second_kernel,
        (sds((2, size, features), BF16), resp, mass, sds((1, count), F32), one, one),
        (),
        dot * (window + 2) * size,
    )(rows, ids, left, own, right, sums1, mass1, fresh, norm, below1, above1)
    below2, above2 = swap(up2, down2, "own")
    done, part = call(own_kernel, (inner, sds((2, size, features), F32)), (), dot * blocks * size)(
        rows, resp2, mass2, edge, fresh
    )
    out = call(last_kernel, sds((blocks, size, features), BF16))(done, part, mass2, edge, below2, above2)
    cost = cost.reshape(per_pair, pairs).T.reshape(count)
    return out.reshape(centroids.shape), cost


def solution(mesh):
    return jax.shard_map(
        per_device,
        mesh=mesh,
        in_specs=(
            P(("own", "rep"), None),
            P(("own", "rep")),
            P(("own", "rep"), None),
            P("own", "rep", None, None),
        ),
        out_specs=(P("own", "rep", None, None), P(("own", "rep"))),
        check_vma=False,
    )
```

time: 189 us -> 117 us (0.62)
  the two profiles are of different devices: /device:TPU:32 before, /device:TPU:8 now
where the time goes in v1:
time: 117 us
  starting transfers between devices  47.6 us (41%)
  waiting for transfers between devices  41.2 us (35%)
  Pallas kernels  13 us (11%)
  local copies, waits for them, and re-layouts  12.9 us (11%)
  other arithmetic  1.39 us (1%)
    ppermute x3, waiting for transfers between devices, swap(): below = lax.ppermute(up, axis, pairs)  38.6 us
    all_to_all x1, starting transfers between devices, per_device(): lax.all_to_all(outgoing.reshape(pairs, lines // pairs // 4, 4, LANES), ('...  21.1 us
    ppermute x3, starting transfers between devices, swap(): above = lax.ppermute(down, axis, [(j, i) for i, j in pairs])  17 us
    unnamed x29, local copies, waits for them, and re-layouts  10.5 us
    ppermute x3, starting transfers between devices, swap(): below = lax.ppermute(up, axis, pairs)  9.44 us
    pallas_call x1, Pallas kernels, per_device(): call(second_kernel, (sds((2, size, features), BF16), resp, mass, sds((1,...  3.65 us
    pallas_call x1, Pallas kernels, per_device(): call(functools.partial(first_kernel, pairs), (sds((count, features), BF16...  3.55 us
  transfers between devices with their start and end apart: 7, of which 4 were waited for; matrix products, arithmetic and copies ran while one was open for 3% of the time, Pallas kernels for 1%

profile of v1, /device:TPU:8, one launch (start us, length us, event | category | flops | bytes accessed | tf_op | source)
XLA Modules:
  0.0 117.0 jit_solution(6581960561066432478)
XLA Ops:
  0.6 0.0 copy-start.11
  0.6 1.4 %copy-done.11 = bf16[1024,768]{1,0:T(8,128)(2,1)S(1)} copy-done((bf16[1024,768]{1,0:T(8,128)(2,1)S(1)}, bf16[1024,768]{1,0:T(8,128)(2,1)}, u32[]{:S(2)}) %copy-start.11) | copy-done | bytes 1572888
  2.0 0.0 copy-start.12
  2.0 0.7 copy-done.12
  2.7 1.9 %shard_map.59 = bf16[6144,128]{1,0:T(8,128)(2,1)S(1)} custom-call(s32[1,1024]{1,0:T(1,128)S(1)} %bitcast.28, bf16[1024,768]{1,0:T(8,128)(2,1)S(1)} %copy-done.11), custom_call_target="tpu_custom_call" | custom-call | flops 1610612736 | bytes 1048576 | tf_op jit(solution)/shard_map/pallas_call | solution.py:257
  4.6 0.0 copy-start.3
  4.6 1.1 copy-done.3
  5.8 0.0 copy-start
  5.8 0.0 copy-start.13
  5.8 21.1 %all-to-all-start = ((bf16[512,3,4,128]{3,2,1,0:T(4,128)(2,1)}), bf16[512,3,4,128]{3,2,1,0:T(4,128)(2,1)S(1)}, u32[]{:S(2)}, u32[]{:S(2)}) async-start(bf16[512,3,4,128]{3,2,1,0:T(4,128)(2,1)} %bitcast.25), calls=%async_computation | async-start | bytes 3145728 | tf_op jit(solution)/shard_map/all_to_all | solution.py:264
  26.9 0.0 copy-done
  26.9 0.7 slice_bitcast_fusion
  27.6 3.8 %collective-permute-start = (bf16[128,768]{1,0:T(8,128)(2,1)}, bf16[128,768]{1,0:T(8,128)(2,1)S(1)}, u32[]{:S(2)}, u32[]{:S(2)}) collective-permute-start(bf16[128,768]{1,0:T(8,128)(2,1)} %get-tuple-element.39), channel_id=1, source_target_pairs={{0,8},{8,16},{16,24},{24,32},{32,40},{40,48},{48,56},{56,64},{64,7... | collective-permute-start | bytes 589832 | tf_op jit(solution)/shard_map/ppermute | solution.py:239
  31.4 6.3 %collective-permute-start.1 = (bf16[128,768]{1,0:T(8,128)(2,1)S(1)}, bf16[128,768]{1,0:T(8,128)(2,1)S(1)}, u32[]{:S(2)}, u32[]{:S(2)}) collective-permute-start(bf16[128,768]{1,0:T(8,128)(2,1)S(1)} %get-tuple-element.38), channel_id=1, source_target_pairs={{8,0},{16,8},{24,16},{32,24},{40,32},{48,40},{56,48},{64,56},{72,6... | collective-permute-start | bytes 589832 | tf_op jit(solution)/shard_map/ppermute | solution.py:240
  37.8 0.0 copy-done.13
  37.8 0.2 copy.8
  38.0 0.2 copy.12
  38.2 31.5 %collective-permute-done.left_ref = bf16[128,768]{1,0:T(8,128)(2,1)S(1)} collective-permute-done((bf16[128,768]{1,0:T(8,128)(2,1)}, bf16[128,768]{1,0:T(8,128)(2,1)S(1)}, u32[]{:S(2)}, u32[]{:S(2)}) %collective-permute-start) | collective-permute-done | bytes 196640 | tf_op jit(solution)/shard_map/ppermute | solution.py:239
  69.7 0.0 collective-permute-done.1.right_ref
  69.7 1.5 %all-to-all-done = bf16[512,3,4,128]{3,2,1,0:T(4,128)(2,1)S(1)} async-done(((bf16[512,3,4,128]{3,2,1,0:T(4,128)(2,1)}), bf16[512,3,4,128]{3,2,1,0:T(4,128)(2,1)S(1)}, u32[]{:S(2)}, u32[]{:S(2)}) %all-to-all-start) | async-done | bytes 1572896 | tf_op jit(solution)/shard_map/all_to_all | solution.py:264
  71.2 0.0 copy-start.1
  71.2 1.2 copy-done.1
  72.3 0.0 copy-start.2
  72.3 1.4 %copy-done.2 = bf16[512,3,4,128]{3,2,1,0:T(4,128)(2,1)S(1)} copy-done((bf16[512,3,4,128]{3,2,1,0:T(4,128)(2,1)S(1)}, bf16[512,3,4,128]{3,2,1,0:T(4,128)(2,1)}, u32[]{:S(2)}) %copy-start.2) | copy-done | bytes 1572888
  73.8 3.6 %shard_map.60 = (bf16[1024,768]{1,0:T(8,128)(2,1)S(1)}, bf16[768,1024]{1,0:T(8,128)(2,1)S(1)}, f32[6,128,768]{2,1,0:T(8,128)S(1)}, f32[768,1]{1,0:T(8,128)S(1)},...) custom-call(bf16[6144,128]{1,0:T(8,128)(2,1)S(1)} %bitcast.24, s32[4,1024]{1,0:T(4,128)S(1)} %bitcast.26, ...), custom_call_target="tpu_custom_call" | custom-call | flops 2013265920 | bytes 1048576 | tf_op jit(solution)/shard_map/pallas_call | solution.py:273
  77.3 0.0 copy-start.6
  77.3 0.7 copy-done.6
  78.0 0.0 copy-start.8
  78.0 0.7 copy-done.8
  78.7 3.0 %collective-permute-start.2 = (bf16[272,768]{1,0:T(8,128)(2,1)S(1)}, bf16[272,768]{1,0:T(8,128)(2,1)S(1)}, u32[]{:S(2)}, u32[]{:S(2)}) collective-permute-start(bf16[272,768]{1,0:T(8,128)(2,1)S(1)} %get-tuple-element.24), channel_id=1, source_target_pairs={{0,8},{8,16},{16,24},{24,32},{32,40},{40,48},{48,56},{56,64},{64,7... | collective-permute-start | bytes 1253384 | tf_op jit(solution)/shard_map/ppermute | solution.py:239
  81.7 4.9 %collective-permute-start.3 = (bf16[272,768]{1,0:T(8,128)(2,1)S(1)}, bf16[272,768]{1,0:T(8,128)(2,1)S(1)}, u32[]{:S(2)}, u32[]{:S(2)}) collective-permute-start(bf16[272,768]{1,0:T(8,128)(2,1)S(1)} %get-tuple-element.25), channel_id=1, source_target_pairs={{8,0},{16,8},{24,16},{32,24},{40,32},{48,40},{56,48},{64,56},{72,6... | collective-permute-start | bytes 1253384 | tf_op jit(solution)/shard_map/ppermute | solution.py:240
  86.6 0.0 copy-start.7
  86.6 0.0 copy-start.9
  86.7 0.7 shard_map.61
  87.4 7.1 %collective-permute-done.2.below_ref = bf16[272,768]{1,0:T(8,128)(2,1)S(1)} collective-permute-done((bf16[272,768]{1,0:T(8,128)(2,1)S(1)}, bf16[272,768]{1,0:T(8,128)(2,1)S(1)}, u32[]{:S(2)}, u32[]{:S(2)}) %collective-permute-start.2) | collective-permute-done | bytes 417824 | tf_op jit(solution)/shard_map/ppermute | solution.py:239
  94.5 1.2 %collective-permute-done.3.above_ref = bf16[272,768]{1,0:T(8,128)(2,1)S(1)} collective-permute-done((bf16[272,768]{1,0:T(8,128)(2,1)S(1)}, bf16[272,768]{1,0:T(8,128)(2,1)S(1)}, u32[]{:S(2)}, u32[]{:S(2)}) %collective-permute-start.3) | collective-permute-done | bytes 417824 | tf_op jit(solution)/shard_map/ppermute | solution.py:240
  95.6 0.0 copy-done.7
  95.6 0.0 copy-done.9
  95.6 3.7 %shard_map.62 = (bf16[2,128,768]{2,1,0:T(8,128)(2,1)S(1)}, bf16[768,1024]{1,0:T(8,128)(2,1)S(1)}, f32[768,1]{1,0:T(8,128)S(1)}, f32[1,1024]{1,0:T(1,128)S(1)}, b...) custom-call(bf16[1024,768]{1,0:T(8,128)(2,1)S(1)} %get-tuple-element.18.rows_ref, s32[4,1024]{1,0:T(4,128)S(1)} %bitcast.27, ...), custom_call_target="tpu_custom_call" | custom-call | flops 1610612736 | bytes 1048576 | tf_op jit(solution)/shard_map/pallas_call | solution.py:281
  99.3 0.0 copy-start.4
  99.3 1.2 copy-done.4
  100.5 0.0 copy-start.10
  100.5 0.6 copy-done.10
  101.0 2.6 %collective-permute-start.4 = (bf16[144,768]{1,0:T(8,128)(2,1)}, bf16[144,768]{1,0:T(8,128)(2,1)}, u32[]{:S(2)}, u32[]{:S(2)}) collective-permute-start(bf16[144,768]{1,0:T(8,128)(2,1)} %get-tuple-element.31), channel_id=1, source_target_pairs={{0,8},{8,16},{16,24},{24,32},{32,40},{40,48},{48,56},{56,64},{64,7... | collective-permute-start | bytes 663560 | tf_op jit(solution)/shard_map/ppermute | solution.py:239
  103.7 5.8 %collective-permute-start.5 = (bf16[144,768]{1,0:T(8,128)(2,1)}, bf16[144,768]{1,0:T(8,128)(2,1)}, u32[]{:S(2)}, u32[]{:S(2)}) collective-permute-start(bf16[144,768]{1,0:T(8,128)(2,1)} %get-tuple-element.32), channel_id=1, source_target_pairs={{8,0},{16,8},{24,16},{32,24},{40,32},{48,40},{56,48},{64,56},{72,6... | collective-permute-start | bytes 663560 | tf_op jit(solution)/shard_map/ppermute | solution.py:240
  109.5 0.6 broadcast.16
  110.1 1.4 %reduce.3 = f32[1024]{0:T(1024)S(1)} reduce(f32[1,1024]{1,0:T(1,128)} %copy-done.10, f32[]{:T(128)} %broadcast.16), dimensions={0}, to_apply=%get-tuple-element.33.reduce_sub_computation.3 | reduce | bytes 8196 | tf_op jit(solution)/shard_map/pallas_call | solution.py:281
  111.4 0.1 copy.10
  111.6 0.8 reshape.43
  112.4 0.0 copy-start.5
  112.4 1.4 %copy-done.5 = bf16[768,1024]{1,0:T(8,128)(2,1)S(1)} copy-done((bf16[768,1024]{1,0:T(8,128)(2,1)S(1)}, bf16[768,1024]{1,0:T(8,128)(2,1)}, u32[]{:S(2)}) %copy-start.5) | copy-done | bytes 1572888
  113.8 1.0 shard_map.63
  114.8 0.0 collective-permute-done.4.below_ref
  114.8 0.0 collective-permute-done.5.above_ref
  114.8 2.2 %shard_map.64 = bf16[4,128,768]{2,1,0:T(8,128)(2,1)} custom-call(bf16[2,128,768]{2,1,0:T(8,128)(2,1)S(1)} %get-tuple-element.29.done_ref, f32[2,128,768]{2,1,0:T(8,128)S(1)} %get-tuple-element.30.part_ref, f32[768,1]{1,0:T(8,128)S(1)} %get-tuple-element.27.mass_ref, bf16[2,128,768]{2,1,0:T(8,128)(2,1)S(1)} %get-tuple-element.28.edge_ref, ...), custom_call_target="tpu_custom_call" | custom-call | bytes 1048576 | tf_op jit(solution)/shard_map/pallas_call | solution.py:291
  (2 shorter events, 0.0 us)
Async XLA Ops:
  0.6 1.4 %copy-start.11 = (bf16[1024,768]{1,0:T(8,128)(2,1)S(1)}, bf16[1024,768]{1,0:T(8,128)(2,1)}, u32[]{:S(2)}) copy-start(bf16[1024,768]{1,0:T(8,128)(2,1)} %rows_ref.1) | copy-start | bytes 4718596
  2.0 0.7 copy-start.12
  4.6 1.2 copy-start.3
  5.8 21.1 %copy-start = (bf16[4,1,128,768]{3,2,1,0:T(8,128)(2,1)S(1)}, bf16[4,1,128,768]{3,2,1,0:T(8,128)(2,1)}, u32[]{:S(2)}) copy-start(bf16[4,1,128,768]{3,2,1,0:T(8,128)(2,1)} %param.7) | copy-start | bytes 2359300
  5.8 32.0 %copy-start.13 = (s32[1024,4]{0,1:T(4,128)S(1)}, s32[1024,4]{0,1:T(4,128)}, u32[]{:S(2)}) copy-start(s32[1024,4]{0,1:T(4,128)} %param.6) | copy-start | bytes 49156
  5.8 65.4 %all-to-all-start = ((bf16[512,3,4,128]{3,2,1,0:T(4,128)(2,1)}), bf16[512,3,4,128]{3,2,1,0:T(4,128)(2,1)S(1)}, u32[]{:S(2)}, u32[]{:S(2)}) async-start(bf16[512,3,4,128]{3,2,1,0:T(4,128)(2,1)} %bitcast.25), calls=%async_computation | async-start | bytes 3145728 | tf_op jit(solution)/shard_map/all_to_all | solution.py:264
  27.6 42.1 %collective-permute-start = (bf16[128,768]{1,0:T(8,128)(2,1)}, bf16[128,768]{1,0:T(8,128)(2,1)S(1)}, u32[]{:S(2)}, u32[]{:S(2)}) collective-permute-start(bf16[128,768]{1,0:T(8,128)(2,1)} %get-tuple-element.39), channel_id=1, source_target_pairs={{0,8},{8,16},{16,24},{24,32},{32,40},{40,48},{48,56},{56,64},{64,7... | collective-permute-start | bytes 589832 | tf_op jit(solution)/shard_map/ppermute | solution.py:239
  31.4 38.3 %collective-permute-start.1 = (bf16[128,768]{1,0:T(8,128)(2,1)S(1)}, bf16[128,768]{1,0:T(8,128)(2,1)S(1)}, u32[]{:S(2)}, u32[]{:S(2)}) collective-permute-start(bf16[128,768]{1,0:T(8,128)(2,1)S(1)} %get-tuple-element.38), channel_id=1, source_target_pairs={{8,0},{16,8},{24,16},{32,24},{40,32},{48,40},{56,48},{64,56},{72,6... | collective-permute-start | bytes 589832 | tf_op jit(solution)/shard_map/ppermute | solution.py:240
  71.2 1.2 copy-start.1
  72.3 1.4 %copy-start.2 = (bf16[512,3,4,128]{3,2,1,0:T(4,128)(2,1)S(1)}, bf16[512,3,4,128]{3,2,1,0:T(4,128)(2,1)}, u32[]{:S(2)}) copy-start(bf16[512,3,4,128]{3,2,1,0:T(4,128)(2,1)} %copy-done.1) | copy-start | bytes 4718596
  77.3 0.7 copy-start.6
  78.0 0.7 copy-start.8
  78.7 15.8 %collective-permute-start.2 = (bf16[272,768]{1,0:T(8,128)(2,1)S(1)}, bf16[272,768]{1,0:T(8,128)(2,1)S(1)}, u32[]{:S(2)}, u32[]{:S(2)}) collective-permute-start(bf16[272,768]{1,0:T(8,128)(2,1)S(1)} %get-tuple-element.24), channel_id=1, source_target_pairs={{0,8},{8,16},{16,24},{24,32},{32,40},{40,48},{48,56},{56,64},{64,7... | collective-permute-start | bytes 1253384 | tf_op jit(solution)/shard_map/ppermute | solution.py:239
  81.7 13.9 %collective-permute-start.3 = (bf16[272,768]{1,0:T(8,128)(2,1)S(1)}, bf16[272,768]{1,0:T(8,128)(2,1)S(1)}, u32[]{:S(2)}, u32[]{:S(2)}) collective-permute-start(bf16[272,768]{1,0:T(8,128)(2,1)S(1)} %get-tuple-element.25), channel_id=1, source_target_pairs={{8,0},{16,8},{24,16},{32,24},{40,32},{48,40},{56,48},{64,56},{72,6... | collective-permute-start | bytes 1253384 | tf_op jit(solution)/shard_map/ppermute | solution.py:240
  86.6 9.0 %copy-start.7 = (bf16[128,768]{1,0:T(8,128)(2,1)S(1)}, bf16[128,768]{1,0:T(8,128)(2,1)}, u32[]{:S(2)}) copy-start(bf16[128,768]{1,0:T(8,128)(2,1)} %copy-done.6) | copy-start | bytes 589828
  86.6 9.0 %copy-start.9 = (bf16[128,768]{1,0:T(8,128)(2,1)S(1)}, bf16[128,768]{1,0:T(8,128)(2,1)}, u32[]{:S(2)}) copy-start(bf16[128,768]{1,0:T(8,128)(2,1)} %copy-done.8) | copy-start | bytes 589828
  99.3 1.2 copy-start.4
  100.5 0.6 copy-start.10
  101.0 13.7 %collective-permute-start.4 = (bf16[144,768]{1,0:T(8,128)(2,1)}, bf16[144,768]{1,0:T(8,128)(2,1)}, u32[]{:S(2)}, u32[]{:S(2)}) collective-permute-start(bf16[144,768]{1,0:T(8,128)(2,1)} %get-tuple-element.31), channel_id=1, source_target_pairs={{0,8},{8,16},{16,24},{24,32},{32,40},{40,48},{48,56},{56,64},{64,7... | collective-permute-start | bytes 663560 | tf_op jit(solution)/shard_map/ppermute | solution.py:239
  103.7 11.1 %collective-permute-start.5 = (bf16[144,768]{1,0:T(8,128)(2,1)}, bf16[144,768]{1,0:T(8,128)(2,1)}, u32[]{:S(2)}, u32[]{:S(2)}) collective-permute-start(bf16[144,768]{1,0:T(8,128)(2,1)} %get-tuple-element.32), channel_id=1, source_target_pairs={{8,0},{16,8},{24,16},{32,24},{40,32},{48,40},{56,48},{64,56},{72,6... | collective-permute-start | bytes 663560 | tf_op jit(solution)/shard_map/ppermute | solution.py:240
  112.4 1.4 %copy-start.5 = (bf16[768,1024]{1,0:T(8,128)(2,1)S(1)}, bf16[768,1024]{1,0:T(8,128)(2,1)}, u32[]{:S(2)}) copy-start(bf16[768,1024]{1,0:T(8,128)(2,1)} %copy-done.4) | copy-start | bytes 4718596

commit v2 on v1

v2 whole, which is shorter than its diff:
```python
import functools
import math

import jax
import jax.numpy as jnp
from jax import lax
from jax.experimental import pallas as pl
from jax.experimental.pallas import tpu as pltpu
from jax.sharding import PartitionSpec as P

PRIOR = 1.0
LOG2E = 1.4426950408889634
LANES = 128
MASS_ROWS = 16
VMEM = pltpu.VMEM
HBM = pltpu.HBM
ANY = pl.ANY
F32 = jnp.float32
BF16 = jnp.bfloat16


def call(kernel, ins, outs, scratch=(), flops=0, limit=24, aliases=None):
    arrays = [x if space is ANY else pltpu.with_memory_space_constraint(x, space) for x, space in ins]
    made = pl.pallas_call(
        kernel,
        in_specs=[pl.BlockSpec(memory_space=space) for _, space in ins],
        out_shape=[space(*x) if space is not ANY else sds(*x) for x, space in outs],
        out_specs=[pl.BlockSpec(memory_space=space) for _, space in outs],
        scratch_shapes=list(scratch),
        input_output_aliases=aliases or {},
        compiler_params=pltpu.CompilerParams(vmem_limit_bytes=limit << 20),
        cost_estimate=pl.CostEstimate(flops=flops, bytes_accessed=1 << 20, transcendentals=0),
    )(*arrays)
    return made[0] if len(outs) == 1 else made


def sds(shape, dtype):
    return jax.ShapeDtypeStruct(shape, dtype)


def matmul(a, b, contract):
    return lax.dot_general(a, b, (contract, ((), ())), preferred_element_type=F32)


def regroup_kernel(pairs, dest_hbm, rows_hbm, out_hbm, dest_ref, rows_ref, wide, out_ref, in_sems, out_sems):
    count, features = rows_ref.shape
    per_pair = count // pairs
    chunks = features // LANES
    fetch_dest = pltpu.make_async_copy(dest_hbm, dest_ref, in_sems.at[0])
    fetch_rows = pltpu.make_async_copy(rows_hbm, rows_ref, in_sems.at[1])
    fetch_dest.start()
    fetch_rows.start()
    fetch_dest.wait()
    dest = dest_ref[...]
    place = lax.rem(dest, per_pair) * pairs + lax.div(dest, count)
    parts = 4
    step = pairs // parts
    span = step * per_pair * chunks
    rows = None
    stores = []
    for part in range(parts):
        first = part * step
        picks = []
        for slot in range(per_pair):
            ids = lax.broadcasted_iota(jnp.int32, (step, count), 0) + (slot * pairs + first)
            picks.append(jnp.where(ids == place, 1.0, 0.0).astype(BF16))
        pick = jnp.concatenate(picks, axis=0)
        if rows is None:
            fetch_rows.wait()
            rows = rows_ref[...]
        moved = matmul(pick, rows, ((1,), (0,)))
        for slot in range(per_pair):
            for f in range(chunks):
                line = (first * chunks + f) * per_pair + slot
                wide[pl.ds(line, step, stride=chunks * per_pair), :] = moved[
                    slot * step : (slot + 1) * step, f * LANES : (f + 1) * LANES
                ]
        here = pl.ds(part * span, span)
        out_ref[here, :] = wide[here, :].astype(BF16)
        store = pltpu.make_async_copy(out_ref.at[here], out_hbm.at[here], out_sems.at[part])
        store.start()
        stores.append(store)
    for store in stores:
        store.wait()


def unpack_rows(lines_ref, rows_ref, wide, pairs):
    count, features = rows_ref.shape
    per_pair = count // pairs
    chunks = features // LANES
    parts = 4
    step = pairs // parts
    span = step * per_pair * chunks
    for part in range(parts):
        here = pl.ds(part * span, span)
        wide[here, :] = lines_ref[here, :].astype(F32)
        for slot in range(per_pair):
            for f in range(chunks):
                got = wide[pl.ds(part * span + f * per_pair + slot, step, stride=chunks * per_pair), :]
                rows_ref[pl.ds(slot * pairs + part * step, step), f * LANES : (f + 1) * LANES] = got.astype(BF16)


def assign(rows_ref, ids_ref, blocks, norms, resp_ref, tops_ref=None):
    count, features = rows_ref.shape
    window = len(blocks)
    half = 0.5 * LOG2E / math.sqrt(features)
    bias = [norm * half for norm in norms]
    flat = jnp.concatenate(blocks, axis=0)
    per_block = blocks[0].shape[0]
    mass = [0.0] * window
    step = 256
    for start in range(0, count, step):
        rows = rows_ref[pl.ds(start, step), :]
        ids = ids_ref[:, start : start + step]
        cross = matmul(flat, rows, ((1,), (1,)))
        scores = []
        top = None
        for w in range(window):
            hit = jnp.max(jnp.where(ids == w, 0.0, -jnp.inf), axis=0, keepdims=True)
            score = cross[w * per_block : (w + 1) * per_block] * (2.0 * half) - bias[w] + hit
            scores.append(score)
            here = jnp.max(score, axis=0, keepdims=True)
            top = here if top is None else jnp.maximum(top, here)
        total = None
        for w in range(window):
            scores[w] = jnp.exp2(scores[w] - top)
            here = jnp.sum(scores[w], axis=0, keepdims=True)
            total = here if total is None else total + here
        scale = 1.0 / total
        for w in range(window):
            resp = scores[w] * scale
            resp_ref[w * per_block : (w + 1) * per_block, start : start + step] = resp.astype(BF16)
            mass[w] = mass[w] + resp
        if tops_ref is not None:
            tops_ref[:, start : start + step] = top * (1.0 / LOG2E) + jnp.log(total)
    return [jnp.sum(m, axis=1, keepdims=True) for m in mass]


def square_norms(blocks):
    wide = [block.astype(F32) for block in blocks]
    return [jnp.sum(w * w, axis=1, keepdims=True) for w in wide]


def diagonal(size):
    across = lax.broadcasted_iota(jnp.int32, (size, size), 0)
    return across == lax.broadcasted_iota(jnp.int32, (size, size), 1)


def pack_mass(masses):
    size = masses[0].shape[0]
    eye = diagonal(size)
    lines = [jnp.sum(jnp.where(eye, m, 0.0), axis=0, keepdims=True) for m in masses]
    line = jnp.concatenate(lines, axis=1)
    high = line.astype(BF16).astype(F32)
    row = lax.broadcasted_iota(jnp.int32, (MASS_ROWS, line.shape[1]), 0)
    return jnp.where(row == 0, high, jnp.where(row == 1, line - high, 0.0)).astype(BF16)


def unpack_mass(packed, which, size):
    line = packed[:, which * size : (which + 1) * size].astype(F32)
    line = jnp.sum(line, axis=0, keepdims=True)
    return jnp.sum(jnp.where(diagonal(size), line, 0.0), axis=1, keepdims=True)


def package(pkg_ref, sums, masses):
    size = masses[0].shape[0]
    blocks = len(sums)
    for k in range(blocks):
        pkg_ref[k * size : (k + 1) * size, :] = sums[k].astype(BF16)
    packed = pack_mass(masses)
    pkg_ref[blocks * size :, : blocks * size] = packed
    rest = pkg_ref.shape[1] - blocks * size
    pkg_ref[blocks * size :, blocks * size :] = jnp.zeros((MASS_ROWS, rest), BF16)


def refresh(total, tally, previous):
    return ((total + PRIOR * previous.astype(F32)) / (tally + PRIOR)).astype(BF16)


def first_kernel(
    pairs, lines_ref, ids_ref, left_ref, own_ref, right_ref,
    rows_ref, resp_ref, sums_ref, mass_ref, up_ref, down_ref, wide,
):
    blocks = [left_ref[...]] + [own_ref[k] for k in range(own_ref.shape[0])] + [right_ref[...]]
    norms = square_norms(blocks)
    unpack_rows(lines_ref, rows_ref, wide, pairs)
    mass = assign(rows_ref, ids_ref, blocks, norms, resp_ref)
    size = own_ref.shape[1]
    last = len(blocks) - 1
    rows = rows_ref[...]
    sums = []
    for k, w in enumerate((0, 1, last - 1, last)):
        total = matmul(resp_ref[w * size : (w + 1) * size, :], rows, ((1,), (0,)))
        sums_ref[k] = total + PRIOR * blocks[w].astype(F32)
        sums.append(total)
    for w in range(last + 1):
        mass_ref[w * size : (w + 1) * size, :] = mass[w] + PRIOR
    package(up_ref, sums[2:], mass[last - 1 :])
    package(down_ref, sums[:2], mass[:2])


def ratio(total, tally):
    return (total * (1.0 / tally)).astype(BF16)


def inner_kernel(rows_ref, resp_ref, mass_ref, own_ref, fresh_ref, norm_ref):
    blocks, size, _ = own_ref.shape
    rows = rows_ref[...]
    for k in range(1, blocks - 1):
        w = k + 1
        total = matmul(resp_ref[w * size : (w + 1) * size, :], rows, ((1,), (0,)))
        total = total + PRIOR * own_ref[k].astype(F32)
        fresh_ref[k - 1] = ratio(total, mass_ref[w * size : (w + 1) * size, :])
    eye = diagonal(LANES)
    for start in range(0, rows_ref.shape[0], LANES):
        wide = rows_ref[pl.ds(start, LANES), :].astype(F32)
        norm = jnp.sum(wide * wide, axis=1, keepdims=True)
        norm_ref[:, start : start + LANES] = jnp.sum(jnp.where(eye, norm, 0.0), axis=0, keepdims=True)


def second_kernel(
    rows_ref, ids_ref, sums_ref, mass_ref, fresh_ref, norm_ref, below_ref, above_ref,
    edge_ref, resp_ref, mass_out, cost_ref, up_ref, down_ref,
):
    inner, size, _ = fresh_ref.shape
    last = inner + 3
    new = []
    for p, (pkg, ws) in enumerate(((below_ref, (0, 1)), (above_ref, (last - 1, last)))):
        packed = pkg[2 * size :, : 2 * size]
        for k, w in enumerate(ws):
            total = sums_ref[2 * p + k] + pkg[k * size : (k + 1) * size, :].astype(F32)
            tally = mass_ref[w * size : (w + 1) * size, :] + unpack_mass(packed, k, size)
            new.append(ratio(total, tally))
    edge_ref[0] = new[1]
    edge_ref[1] = new[2]
    blocks = new[:2] + [fresh_ref[k] for k in range(inner)] + new[2:]
    mass = assign(rows_ref, ids_ref, blocks, square_norms(blocks), resp_ref, cost_ref)
    half = 0.5 / math.sqrt(rows_ref.shape[1])
    cost_ref[...] = norm_ref[...] * half - cost_ref[...]
    for w in range(last + 1):
        mass_out[w * size : (w + 1) * size, :] = mass[w] + PRIOR
    rows = rows_ref[...]
    for pkg, w in ((up_ref, last), (down_ref, 0)):
        total = matmul(resp_ref[w * size : (w + 1) * size, :], rows, ((1,), (0,)))
        package(pkg, [total], [mass[w]])


def interleave(lines_ref, out_ref, slots):
    count = lines_ref.shape[1]
    pairs = count // slots
    width = LANES * slots
    groups = pairs // LANES
    row = lax.broadcasted_iota(jnp.int32, (width, width), 0)
    lane = lax.broadcasted_iota(jnp.int32, (width, width), 1)
    pick = jnp.where(row == lax.rem(lane, slots) * LANES + lax.div(lane, slots), 1.0, 0.0).astype(BF16)
    pieces = []
    for g in range(groups):
        cuts = [lines_ref[:, s * pairs + g * LANES : s * pairs + (g + 1) * LANES] for s in range(slots)]
        left = jnp.concatenate(cuts, axis=1)
        for _ in range(3):
            piece = left.astype(BF16).astype(F32)
            pieces.append(piece)
            left = left - piece
    pieces += [jnp.zeros_like(pieces[0])] * (-len(pieces) % 16)
    moved = matmul(jnp.concatenate(pieces, axis=0).astype(BF16), pick, ((1,), (0,)))
    for g in range(groups):
        line = moved[3 * g : 3 * g + 1] + moved[3 * g + 1 : 3 * g + 2] + moved[3 * g + 2 : 3 * g + 3]
        for s in range(slots):
            out_ref[g * slots + s : g * slots + s + 1, :] = line[:, s * LANES : (s + 1) * LANES]


def own_kernel(
    slots, rows_ref, resp_ref, mass_ref, edge_ref, fresh_ref, cost_ref, out_hbm, part_ref, placed_ref, done_ref, sem
):
    inner, size, _ = fresh_ref.shape
    rows = rows_ref[...]
    for k in range(inner):
        w = k + 2
        total = matmul(resp_ref[w * size : (w + 1) * size, :], rows, ((1,), (0,)))
        total = total + PRIOR * fresh_ref[k].astype(F32)
        done_ref[k] = ratio(total, mass_ref[w * size : (w + 1) * size, :])
    store = pltpu.make_async_copy(done_ref, out_hbm.at[pl.ds(1, inner)], sem)
    store.start()
    for e, w in ((0, 1), (1, inner + 2)):
        total = matmul(resp_ref[w * size : (w + 1) * size, :], rows, ((1,), (0,)))
        part_ref[e] = total + PRIOR * edge_ref[e].astype(F32)
    interleave(cost_ref, placed_ref, slots)
    store.wait()


def last_kernel(given_hbm, part_ref, mass_ref, below_ref, above_ref, out_hbm, done_ref, sems):
    blocks, size, _ = out_hbm.shape
    stores = []
    for e, (k, pkg) in enumerate(((0, below_ref), (blocks - 1, above_ref))):
        w = k + 1
        total = part_ref[e] + pkg[:size, :].astype(F32)
        tally = mass_ref[w * size : (w + 1) * size, :] + unpack_mass(pkg[size:, :size], 0, size)
        done_ref[e] = ratio(total, tally)
        stores.append(pltpu.make_async_copy(done_ref.at[e], out_hbm.at[k], sems.at[e]))
        stores[-1].start()
    for store in stores:
        store.wait()


def swap(up, down, axis):
    devices = lax.axis_size(axis)
    pairs = [(i, i + 1) for i in range(devices - 1)]
    below = lax.ppermute(up, axis, pairs)
    above = lax.ppermute(down, axis, [(j, i) for i, j in pairs])
    return below, above


def per_device(sample_rows, destination, neighbours, centroids):
    own_count, rep_count = lax.axis_size("own"), lax.axis_size("rep")
    pairs = own_count * rep_count
    count, features = sample_rows.shape
    per_pair = count // pairs
    chunks = features // LANES
    lines = count * chunks
    blocks, _, size, _ = centroids.shape
    window = blocks + 2
    own = centroids.reshape(blocks, size, features)
    wide = pltpu.VMEM((lines + chunks * per_pair + 4, LANES), F32)
    dma = pltpu.SemaphoreType.DMA
    dot = 2 * count * features
    block = (size, features)

    outgoing = call(
        functools.partial(regroup_kernel, pairs),
        [(destination.reshape(1, count), HBM), (sample_rows, HBM)],
        [(((lines, LANES), BF16), HBM)],
        [VMEM((1, count), jnp.int32), VMEM((count, features), BF16), wide, VMEM((lines, LANES), BF16), dma((2,)), dma((4,))],
        dot * count,
    )
    left, right = swap(own[blocks - 1], own[0], "own")
    first_block = lax.axis_index("own") * blocks - 1
    ids = (neighbours // rep_count - first_block).T
    ids = ids.reshape(-1, pairs, per_pair).swapaxes(1, 2).reshape(-1, count)
    arrived = lax.all_to_all(
        outgoing.reshape(pairs, lines // pairs // 4, 4, LANES), ("own", "rep"), split_axis=0, concat_axis=0, tiled=True
    ).reshape(lines, LANES)

    resp = (((window * size, count), BF16), VMEM)
    mass = (((window * size, 1), F32), VMEM)
    two = (((2 * size + MASS_ROWS, features), BF16), VMEM)
    one = (((size + MASS_ROWS, features), BF16), VMEM)
    line = (((1, count), F32), VMEM)
    rows, resp1, sums1, mass1, up1, down1 = call(
        functools.partial(first_kernel, pairs),
        [(arrived, VMEM), (ids, VMEM), (left, VMEM), (own, VMEM), (right, VMEM)],
        [(((count, features), BF16), VMEM), resp, (((4,) + block, F32), VMEM), mass, two, two],
        [wide],
        dot * (window + 4) * size,
    )
    below1, above1 = swap(up1, down1, "own")
    fresh, norm = call(
        inner_kernel,
        [(rows, VMEM), (resp1, VMEM), (mass1, VMEM), (own, VMEM)],
        [(((blocks - 2,) + block, BF16), VMEM), line],
        flops=dot * 2 * size,
    )
    edge, resp2, mass2, cost, up2, down2 = call(
        second_kernel,
        [(x, VMEM) for x in (rows, ids, sums1, mass1, fresh, norm, below1, above1)],
        [(((2,) + block, BF16), VMEM), resp, mass, line, one, one],
        flops=dot * (window + 2) * size,
    )
    below2, above2 = swap(up2, down2, "own")
    given, part, placed = call(
        functools.partial(own_kernel, per_pair),
        [(x, VMEM) for x in (rows, resp2, mass2, edge, fresh, cost)],
        [(((blocks,) + block, BF16), HBM), (((2,) + block, F32), VMEM), (((count // LANES, LANES), F32), VMEM)],
        [VMEM((blocks - 2,) + block, BF16), dma],
        dot * blocks * size,
    )
    out = call(
        last_kernel,
        [(given, HBM), (part, VMEM), (mass2, VMEM), (below2, VMEM), (above2, VMEM)],
        [(((blocks,) + block, BF16), HBM)],
        [VMEM((2,) + block, BF16), dma((2,))],
        aliases={0: 0},
    )
    return out.reshape(centroids.shape), placed.reshape(count)


def solution(mesh):
    return jax.shard_map(
        per_device,
        mesh=mesh,
        in_specs=(
            P(("own", "rep"), None),
            P(("own", "rep")),
            P(("own", "rep"), None),
            P("own", "rep", None, None),
        ),
        out_specs=(P("own", "rep", None, None), P(("own", "rep"))),
        check_vma=False,
    )
```

time: 117 us -> 107 us (0.915)
  local copies, waits for them, and re-layouts: 12.9 us -> 1.73 us
  waiting for transfers between devices: 41.2 us -> 43.1 us
  other arithmetic: 1.39 us -> 0.03 us
    ppermute x3, waiting for transfers between devices: 1.19 us -> 28.4 us  [swap(): above = lax.ppermute(down, axis, [(j, i) for i, j in pairs])]
    ppermute x3, waiting for transfers between devices: 38.6 us -> 13.3 us  [swap(): below = lax.ppermute(up, axis, pairs)]
    unnamed x29 -> x6, local copies, waits for them, and re-layouts: 10.5 us -> 0.81 us
    ppermute x3, starting transfers between devices: 17 us -> 18.9 us  [swap(): above = lax.ppermute(down, axis, [(j, i) for i, j in pairs])]
    ppermute x3, starting transfers between devices: 9.44 us -> 7.56 us  [swap(): below = lax.ppermute(up, axis, pairs)]
    pallas_call x1 -> x0, other arithmetic: 1.37 us -> none  [per_device(): call(second_kernel, (sds((2, size, features), BF16), resp, mass, sds((1,...]
  transfers between devices with their start and end apart: 7 -> 7, of which waited for: 4 -> 7; matrix products, arithmetic and copies ran while one was open for 3% -> 2% of each run, Pallas kernels for 1% -> 2%
where the time goes in v2:
time: 107 us
  starting transfers between devices  47.6 us (44%)
  waiting for transfers between devices  43.1 us (40%)
  Pallas kernels  13.9 us (13%)
  local copies, waits for them, and re-layouts  1.73 us (2%)
    ppermute x3, waiting for transfers between devices, swap(): above = lax.ppermute(down, axis, [(j, i) for i, j in pairs])  28.4 us
    all_to_all x1, starting transfers between devices, per_device(): lax.all_to_all(outgoing.reshape(pairs, lines // pairs // 4, 4, LANES), ('...  21.1 us
    ppermute x3, starting transfers between devices, swap(): above = lax.ppermute(down, axis, [(j, i) for i, j in pairs])  18.9 us
    pallas_call x6, Pallas kernels, call(): pl.pallas_call(kernel, in_specs=[pl.BlockSpec(memory_space=space) for _,...  13.9 us
    ppermute x3, waiting for transfers between devices, swap(): below = lax.ppermute(up, axis, pairs)  13.3 us
    ppermute x3, starting transfers between devices, swap(): below = lax.ppermute(up, axis, pairs)  7.56 us
  transfers between devices with their start and end apart: 7, of which 7 were waited for; matrix products, arithmetic and copies ran while one was open for 2% of the time, Pallas kernels for 2%

profile of v2, /device:TPU:8, one launch (start us, length us, event | category | flops | bytes accessed | tf_op | source)
XLA Modules:
  0.0 107.1 jit_solution(2041640832310317841)
XLA Ops:
  0.6 4.2 %shard_map.59 = bf16[6144,128]{1,0:T(8,128)(2,1)} custom-call(s32[1,1024]{1,0:T(1,128)} %bitcast.30, bf16[1024,768]{1,0:T(8,128)(2,1)} %rows_hbm.1), custom_call_target="tpu_custom_call" | custom-call | flops 1610612736 | bytes 1048576 | tf_op jit(solution)/shard_map/pallas_call | solution.py:24
  4.8 0.0 copy-start
  4.8 0.0 copy-start.1
  4.8 21.1 %all-to-all-start = ((bf16[512,3,4,128]{3,2,1,0:T(4,128)(2,1)}), bf16[512,3,4,128]{3,2,1,0:T(4,128)(2,1)S(1)}, u32[]{:S(2)}, u32[]{:S(2)}) async-start(bf16[512,3,4,128]{3,2,1,0:T(4,128)(2,1)} %bitcast.28), calls=%async_computation | async-start | bytes 3145728 | tf_op jit(solution)/shard_map/all_to_all | solution.py:339
  26.0 0.0 copy-done
  26.0 0.7 slice_bitcast_fusion
  26.7 8.2 %collective-permute-start.1 = (bf16[128,768]{1,0:T(8,128)(2,1)}, bf16[128,768]{1,0:T(8,128)(2,1)S(1)}, u32[]{:S(2)}, u32[]{:S(2)}) collective-permute-start(bf16[128,768]{1,0:T(8,128)(2,1)} %get-tuple-element.40), channel_id=1, source_target_pairs={{8,0},{16,8},{24,16},{32,24},{40,32},{48,40},{56,48},{64,56},{72,6... | collective-permute-start | bytes 589832 | tf_op jit(solution)/shard_map/ppermute | solution.py:309
  34.9 1.9 %collective-permute-start = (bf16[128,768]{1,0:T(8,128)(2,1)S(1)}, bf16[128,768]{1,0:T(8,128)(2,1)S(1)}, u32[]{:S(2)}, u32[]{:S(2)}) collective-permute-start(bf16[128,768]{1,0:T(8,128)(2,1)S(1)} %get-tuple-element.41), channel_id=1, source_target_pairs={{0,8},{8,16},{16,24},{24,32},{32,40},{40,48},{48,56},{56,64},{64,7... | collective-permute-start | bytes 589832 | tf_op jit(solution)/shard_map/ppermute | solution.py:308
  36.8 0.0 copy-done.1
  36.8 0.2 copy.9
  37.1 0.2 copy.12
  37.3 26.0 %collective-permute-done.1.right_ref = bf16[128,768]{1,0:T(8,128)(2,1)S(1)} collective-permute-done((bf16[128,768]{1,0:T(8,128)(2,1)}, bf16[128,768]{1,0:T(8,128)(2,1)S(1)}, u32[]{:S(2)}, u32[]{:S(2)}) %collective-permute-start.1) | collective-permute-done | bytes 196640 | tf_op jit(solution)/shard_map/ppermute | solution.py:309
  63.3 5.5 %collective-permute-done.left_ref = bf16[128,768]{1,0:T(8,128)(2,1)S(1)} collective-permute-done((bf16[128,768]{1,0:T(8,128)(2,1)S(1)}, bf16[128,768]{1,0:T(8,128)(2,1)S(1)}, u32[]{:S(2)}, u32[]{:S(2)}) %collective-permute-start) | collective-permute-done | bytes 196640 | tf_op jit(solution)/shard_map/ppermute | solution.py:308
  68.8 1.5 %all-to-all-done = bf16[512,3,4,128]{3,2,1,0:T(4,128)(2,1)S(1)} async-done(((bf16[512,3,4,128]{3,2,1,0:T(4,128)(2,1)}), bf16[512,3,4,128]{3,2,1,0:T(4,128)(2,1)S(1)}, u32[]{:S(2)}, u32[]{:S(2)}) %all-to-all-start) | async-done | bytes 1572896 | tf_op jit(solution)/shard_map/all_to_all | solution.py:339
  70.2 3.6 %shard_map.60 = (bf16[1024,768]{1,0:T(8,128)(2,1)S(1)}, bf16[768,1024]{1,0:T(8,128)(2,1)S(1)}, f32[4,128,768]{2,1,0:T(8,128)S(1)}, f32[768,1]{1,0:T(8,128)S(1)},...) custom-call(bf16[6144,128]{1,0:T(8,128)(2,1)S(1)} %bitcast.24, s32[4,1024]{1,0:T(4,128)S(1)} %bitcast.25, ...), custom_call_target="tpu_custom_call" | custom-call | flops 2013265920 | bytes 1048576 | tf_op jit(solution)/shard_map/pallas_call | solution.py:24
  73.9 3.0 %collective-permute-start.2 = (bf16[272,768]{1,0:T(8,128)(2,1)S(1)}, bf16[272,768]{1,0:T(8,128)(2,1)S(1)}, u32[]{:S(2)}, u32[]{:S(2)}) collective-permute-start(bf16[272,768]{1,0:T(8,128)(2,1)S(1)} %get-tuple-element.25), channel_id=1, source_target_pairs={{0,8},{8,16},{16,24},{24,32},{32,40},{40,48},{48,56},{56,64},{64,7... | collective-permute-start | bytes 1253384 | tf_op jit(solution)/shard_map/ppermute | solution.py:308
  76.9 4.9 %collective-permute-start.3 = (bf16[272,768]{1,0:T(8,128)(2,1)S(1)}, bf16[272,768]{1,0:T(8,128)(2,1)S(1)}, u32[]{:S(2)}, u32[]{:S(2)}) collective-permute-start(bf16[272,768]{1,0:T(8,128)(2,1)S(1)} %get-tuple-element.26), channel_id=1, source_target_pairs={{8,0},{16,8},{24,16},{32,24},{40,32},{48,40},{56,48},{64,56},{72,6... | collective-permute-start | bytes 1253384 | tf_op jit(solution)/shard_map/ppermute | solution.py:309
  81.8 0.7 shard_map.61
  82.6 7.1 %collective-permute-done.2.below_ref = bf16[272,768]{1,0:T(8,128)(2,1)S(1)} collective-permute-done((bf16[272,768]{1,0:T(8,128)(2,1)S(1)}, bf16[272,768]{1,0:T(8,128)(2,1)S(1)}, u32[]{:S(2)}, u32[]{:S(2)}) %collective-permute-start.2) | collective-permute-done | bytes 417824 | tf_op jit(solution)/shard_map/ppermute | solution.py:308
  89.7 1.2 %collective-permute-done.3.above_ref = bf16[272,768]{1,0:T(8,128)(2,1)S(1)} collective-permute-done((bf16[272,768]{1,0:T(8,128)(2,1)S(1)}, bf16[272,768]{1,0:T(8,128)(2,1)S(1)}, u32[]{:S(2)}, u32[]{:S(2)}) %collective-permute-start.3) | collective-permute-done | bytes 417824 | tf_op jit(solution)/shard_map/ppermute | solution.py:309
  90.8 3.0 %shard_map.62 = (bf16[2,128,768]{2,1,0:T(8,128)(2,1)S(1)}, bf16[768,1024]{1,0:T(8,128)(2,1)S(1)}, f32[768,1]{1,0:T(8,128)S(1)}, f32[1,1024]{1,0:T(1,128)S(1)}, b...) custom-call(bf16[1024,768]{1,0:T(8,128)(2,1)S(1)} %get-tuple-element.19.rows_ref, s32[4,1024]{1,0:T(4,128)S(1)} %bitcast.26, ...), custom_call_target="tpu_custom_call" | custom-call | flops 1610612736 | bytes 1048576 | tf_op jit(solution)/shard_map/pallas_call | solution.py:24
  93.8 2.6 %collective-permute-start.4 = (bf16[144,768]{1,0:T(8,128)(2,1)S(1)}, bf16[144,768]{1,0:T(8,128)(2,1)S(1)}, u32[]{:S(2)}, u32[]{:S(2)}) collective-permute-start(bf16[144,768]{1,0:T(8,128)(2,1)S(1)} %get-tuple-element.33), channel_id=1, source_target_pairs={{0,8},{8,16},{16,24},{24,32},{32,40},{40,48},{48,56},{56,64},{64,7... | collective-permute-start | bytes 663560 | tf_op jit(solution)/shard_map/ppermute | solution.py:308
  96.4 5.8 %collective-permute-start.5 = (bf16[144,768]{1,0:T(8,128)(2,1)S(1)}, bf16[144,768]{1,0:T(8,128)(2,1)S(1)}, u32[]{:S(2)}, u32[]{:S(2)}) collective-permute-start(bf16[144,768]{1,0:T(8,128)(2,1)S(1)} %get-tuple-element.34), channel_id=1, source_target_pairs={{8,0},{16,8},{24,16},{32,24},{40,32},{48,40},{56,48},{64,56},{72,6... | collective-permute-start | bytes 663560 | tf_op jit(solution)/shard_map/ppermute | solution.py:309
  102.2 1.4 %shard_map.63 = (bf16[4,128,768]{2,1,0:T(8,128)(2,1)}, f32[2,128,768]{2,1,0:T(8,128)S(1)}, f32[8,128]{1,0:T(8,128)S(1)}) custom-call(bf16[1024,768]{1,0:T(8,128)(2,1)S(1)} %get-tuple-element.19.rows_ref, bf16[768,1024]{1,0:T(8,128)(2,1)S(1)} %get-tuple-element.27.resp_ref, f32[768,1]{1,0:T(8,128)S(1)} %get-tuple-element.28.mass_ref, ...), custom_call_target="tpu_custom_call" | custom-call | flops 805306368 | bytes 1048576 | tf_op jit(solution)/shard_map/pallas_call | solution.py:24
  103.6 0.6 copy.15
  104.2 0.8 collective-permute-done.4.below_ref
  105.0 1.2 %collective-permute-done.5.above_ref = bf16[144,768]{1,0:T(8,128)(2,1)S(1)} collective-permute-done((bf16[144,768]{1,0:T(8,128)(2,1)S(1)}, bf16[144,768]{1,0:T(8,128)(2,1)S(1)}, u32[]{:S(2)}, u32[]{:S(2)}) %collective-permute-start.5) | collective-permute-done | bytes 221216 | tf_op jit(solution)/shard_map/ppermute | solution.py:309
  106.2 1.0 shard_map.64
  (1 shorter events, 0.0 us)
Async XLA Ops:
  4.8 21.1 %copy-start = (bf16[4,1,128,768]{3,2,1,0:T(8,128)(2,1)S(1)}, bf16[4,1,128,768]{3,2,1,0:T(8,128)(2,1)}, u32[]{:S(2)}) copy-start(bf16[4,1,128,768]{3,2,1,0:T(8,128)(2,1)} %param.7) | copy-start | bytes 2359300
  4.8 32.0 %copy-start.1 = (s32[1024,4]{0,1:T(4,128)S(1)}, s32[1024,4]{0,1:T(4,128)}, u32[]{:S(2)}) copy-start(s32[1024,4]{0,1:T(4,128)} %param.6) | copy-start | bytes 49156
  4.8 65.4 %all-to-all-start = ((bf16[512,3,4,128]{3,2,1,0:T(4,128)(2,1)}), bf16[512,3,4,128]{3,2,1,0:T(4,128)(2,1)S(1)}, u32[]{:S(2)}, u32[]{:S(2)}) async-start(bf16[512,3,4,128]{3,2,1,0:T(4,128)(2,1)} %bitcast.28), calls=%async_computation | async-start | bytes 3145728 | tf_op jit(solution)/shard_map/all_to_all | solution.py:339
  26.7 36.6 %collective-permute-start.1 = (bf16[128,768]{1,0:T(8,128)(2,1)}, bf16[128,768]{1,0:T(8,128)(2,1)S(1)}, u32[]{:S(2)}, u32[]{:S(2)}) collective-permute-start(bf16[128,768]{1,0:T(8,128)(2,1)} %get-tuple-element.40), channel_id=1, source_target_pairs={{8,0},{16,8},{24,16},{32,24},{40,32},{48,40},{56,48},{64,56},{72,6... | collective-permute-start | bytes 589832 | tf_op jit(solution)/shard_map/ppermute | solution.py:309
  34.9 33.9 %collective-permute-start = (bf16[128,768]{1,0:T(8,128)(2,1)S(1)}, bf16[128,768]{1,0:T(8,128)(2,1)S(1)}, u32[]{:S(2)}, u32[]{:S(2)}) collective-permute-start(bf16[128,768]{1,0:T(8,128)(2,1)S(1)} %get-tuple-element.41), channel_id=1, source_target_pairs={{0,8},{8,16},{16,24},{24,32},{32,40},{40,48},{48,56},{56,64},{64,7... | collective-permute-start | bytes 589832 | tf_op jit(solution)/shard_map/ppermute | solution.py:308
  73.9 15.8 %collective-permute-start.2 = (bf16[272,768]{1,0:T(8,128)(2,1)S(1)}, bf16[272,768]{1,0:T(8,128)(2,1)S(1)}, u32[]{:S(2)}, u32[]{:S(2)}) collective-permute-start(bf16[272,768]{1,0:T(8,128)(2,1)S(1)} %get-tuple-element.25), channel_id=1, source_target_pairs={{0,8},{8,16},{16,24},{24,32},{32,40},{40,48},{48,56},{56,64},{64,7... | collective-permute-start | bytes 1253384 | tf_op jit(solution)/shard_map/ppermute | solution.py:308
  76.9 13.9 %collective-permute-start.3 = (bf16[272,768]{1,0:T(8,128)(2,1)S(1)}, bf16[272,768]{1,0:T(8,128)(2,1)S(1)}, u32[]{:S(2)}, u32[]{:S(2)}) collective-permute-start(bf16[272,768]{1,0:T(8,128)(2,1)S(1)} %get-tuple-element.26), channel_id=1, source_target_pairs={{8,0},{16,8},{24,16},{32,24},{40,32},{48,40},{56,48},{64,56},{72,6... | collective-permute-start | bytes 1253384 | tf_op jit(solution)/shard_map/ppermute | solution.py:309
  93.8 11.2 %collective-permute-start.4 = (bf16[144,768]{1,0:T(8,128)(2,1)S(1)}, bf16[144,768]{1,0:T(8,128)(2,1)S(1)}, u32[]{:S(2)}, u32[]{:S(2)}) collective-permute-start(bf16[144,768]{1,0:T(8,128)(2,1)S(1)} %get-tuple-element.33), channel_id=1, source_target_pairs={{0,8},{8,16},{16,24},{24,32},{32,40},{40,48},{48,56},{56,64},{64,7... | collective-permute-start | bytes 663560 | tf_op jit(solution)/shard_map/ppermute | solution.py:308
  96.4 9.7 %collective-permute-start.5 = (bf16[144,768]{1,0:T(8,128)(2,1)S(1)}, bf16[144,768]{1,0:T(8,128)(2,1)S(1)}, u32[]{:S(2)}, u32[]{:S(2)}) collective-permute-start(bf16[144,768]{1,0:T(8,128)(2,1)S(1)} %get-tuple-element.34), channel_id=1, source_target_pairs={{8,0},{16,8},{24,16},{32,24},{40,32},{48,40},{56,48},{64,56},{72,6... | collective-permute-start | bytes 663560 | tf_op jit(solution)/shard_map/ppermute | solution.py:309

commit v3 on v2

v3 whole, which is shorter than its diff:
```python
import functools
import math

import jax
import jax.numpy as jnp
from jax import lax
from jax.experimental import pallas as pl
from jax.experimental.pallas import tpu as pltpu
from jax.sharding import PartitionSpec as P

PRIOR = 1.0
LOG2E = 1.4426950408889634
LANES = 128
MASS_ROWS = 16
VMEM = pltpu.VMEM
HBM = pltpu.HBM
ANY = pl.ANY
F32 = jnp.float32
BF16 = jnp.bfloat16


def call(kernel, ins, outs, scratch=(), flops=0, limit=24, aliases=None):
    arrays = [x if space is ANY else pltpu.with_memory_space_constraint(x, space) for x, space in ins]
    made = pl.pallas_call(
        kernel,
        in_specs=[pl.BlockSpec(memory_space=space) for _, space in ins],
        out_shape=[space(*x) if space is not ANY else sds(*x) for x, space in outs],
        out_specs=[pl.BlockSpec(memory_space=space) for _, space in outs],
        scratch_shapes=list(scratch),
        input_output_aliases=aliases or {},
        compiler_params=pltpu.CompilerParams(vmem_limit_bytes=limit << 20),
        cost_estimate=pl.CostEstimate(flops=flops, bytes_accessed=1 << 20, transcendentals=0),
    )(*arrays)
    return made[0] if len(outs) == 1 else made


def sds(shape, dtype):
    return jax.ShapeDtypeStruct(shape, dtype)


def matmul(a, b, contract):
    return lax.dot_general(a, b, (contract, ((), ())), preferred_element_type=F32)


def regroup_kernel(pairs, dest_hbm, rows_hbm, out_hbm, dest_ref, rows_ref, wide, out_ref, in_sems, out_sems):
    count, features = rows_ref.shape
    per_pair = count // pairs
    chunks = features // LANES
    fetch_dest = pltpu.make_async_copy(dest_hbm, dest_ref, in_sems.at[0])
    fetch_rows = pltpu.make_async_copy(rows_hbm, rows_ref, in_sems.at[1])
    fetch_dest.start()
    fetch_rows.start()
    fetch_dest.wait()
    dest = dest_ref[...]
    place = lax.rem(dest, per_pair) * pairs + lax.div(dest, count)
    parts = 4
    step = pairs // parts
    span = step * per_pair * chunks
    rows = None
    stores = []
    for part in range(parts):
        first = part * step
        picks = []
        for slot in range(per_pair):
            ids = lax.broadcasted_iota(jnp.int32, (step, count), 0) + (slot * pairs + first)
            picks.append(jnp.where(ids == place, 1.0, 0.0).astype(BF16))
        pick = jnp.concatenate(picks, axis=0)
        if rows is None:
            fetch_rows.wait()
            rows = rows_ref[...]
        moved = matmul(pick, rows, ((1,), (0,)))
        for slot in range(per_pair):
            for f in range(chunks):
                line = (first * chunks + f) * per_pair + slot
                wide[pl.ds(line, step, stride=chunks * per_pair), :] = moved[
                    slot * step : (slot + 1) * step, f * LANES : (f + 1) * LANES
                ]
        here = pl.ds(part * span, span)
        out_ref[here, :] = wide[here, :].astype(BF16)
        store = pltpu.make_async_copy(out_ref.at[here], out_hbm.at[here], out_sems.at[part])
        store.start()
        stores.append(store)
    for store in stores:
        store.wait()


def unpack_rows(lines_ref, rows_ref, wide, pairs):
    count, features = rows_ref.shape
    per_pair = count // pairs
    chunks = features // LANES
    parts = 4
    step = pairs // parts
    span = step * per_pair * chunks
    for part in range(parts):
        here = pl.ds(part * span, span)
        wide[here, :] = lines_ref[here, :].astype(F32)
        for slot in range(per_pair):
            for f in range(chunks):
                got = wide[pl.ds(part * span + f * per_pair + slot, step, stride=chunks * per_pair), :]
                rows_ref[pl.ds(slot * pairs + part * step, step), f * LANES : (f + 1) * LANES] = got.astype(BF16)


STEP = 256


def half_scale(features):
    return 0.5 * LOG2E / math.sqrt(features)


def scored(flat, biases, slots, rows, ids):
    cross = matmul(flat, rows, ((1,), (1,)))
    size = flat.shape[0] // len(slots)
    factor = 2.0 * half_scale(flat.shape[1])
    scores = []
    for k, w in enumerate(slots):
        hit = jnp.max(jnp.where(ids == w, 0.0, -jnp.inf), axis=0, keepdims=True)
        scores.append(cross[k * size : (k + 1) * size] * factor + (hit - biases[k]))
    return scores


def highest(scores):
    return functools.reduce(jnp.maximum, [jnp.max(s, axis=0, keepdims=True) for s in scores])


def added(parts):
    return functools.reduce(jnp.add, [jnp.sum(p, axis=0, keepdims=True) for p in parts])


def square_biases(blocks):
    half = half_scale(blocks[0].shape[1])
    wide = [block.astype(F32) for block in blocks]
    return [jnp.sum(w * w, axis=1, keepdims=True) * half for w in wide]


def row_sums(parts):
    return [jnp.sum(p, axis=1, keepdims=True) for p in parts]


def diagonal(size):
    across = lax.broadcasted_iota(jnp.int32, (size, size), 0)
    return across == lax.broadcasted_iota(jnp.int32, (size, size), 1)


def pack_mass(masses):
    size = masses[0].shape[0]
    eye = diagonal(size)
    lines = [jnp.sum(jnp.where(eye, m, 0.0), axis=0, keepdims=True) for m in masses]
    line = jnp.concatenate(lines, axis=1)
    high = line.astype(BF16).astype(F32)
    row = lax.broadcasted_iota(jnp.int32, (MASS_ROWS, line.shape[1]), 0)
    return jnp.where(row == 0, high, jnp.where(row == 1, line - high, 0.0)).astype(BF16)


def unpack_mass(packed, which, size):
    line = packed[:, which * size : (which + 1) * size].astype(F32)
    line = jnp.sum(line, axis=0, keepdims=True)
    return jnp.sum(jnp.where(diagonal(size), line, 0.0), axis=1, keepdims=True)


def package(pkg_ref, sums, masses):
    size = masses[0].shape[0]
    blocks = len(sums)
    for k in range(blocks):
        pkg_ref[k * size : (k + 1) * size, :] = sums[k].astype(BF16)
    packed = pack_mass(masses)
    pkg_ref[blocks * size :, : blocks * size] = packed
    rest = pkg_ref.shape[1] - blocks * size
    pkg_ref[blocks * size :, blocks * size :] = jnp.zeros((MASS_ROWS, rest), BF16)


def refresh(total, tally, previous):
    return ((total + PRIOR * previous.astype(F32)) / (tally + PRIOR)).astype(BF16)


def first_kernel(
    pairs, lines_ref, ids_ref, left_ref, own_ref, right_ref,
    rows_ref, inner_ref, scale_ref, sums_ref, mass_ref, up_ref, down_ref, wide, resp_ref,
):
    blocks = [left_ref[...]] + [own_ref[k] for k in range(own_ref.shape[0])] + [right_ref[...]]
    last = len(blocks) - 1
    size = own_ref.shape[1]
    biases = square_biases(blocks)
    flat = jnp.concatenate(blocks, axis=0)
    unpack_rows(lines_ref, rows_ref, wide, pairs)
    edges = (0, 1, last - 1, last)
    mass = [0.0] * len(edges)
    count = rows_ref.shape[0]
    for start in range(0, count, STEP):
        here = slice(start, start + STEP)
        scores = scored(flat, biases, range(last + 1), rows_ref[here, :], ids_ref[:, here])
        top = highest(scores)
        weights = [jnp.exp2(score - top) for score in scores]
        scale = 1.0 / added(weights)
        scale_ref[:, here] = scale
        for k in range(2, last - 1):
            inner_ref[(k - 2) * size : (k - 1) * size, here] = weights[k]
        for k, w in enumerate(edges):
            resp = weights[w] * scale
            resp_ref[k * size : (k + 1) * size, here] = resp.astype(BF16)
            mass[k] = mass[k] + resp
    mass = row_sums(mass)
    rows = rows_ref[...]
    sums = []
    for k, w in enumerate(edges):
        total = matmul(resp_ref[k * size : (k + 1) * size, :], rows, ((1,), (0,)))
        sums_ref[k] = total + PRIOR * blocks[w].astype(F32)
        sums.append(total)
        mass_ref[k * size : (k + 1) * size, :] = mass[k] + PRIOR
    package(up_ref, sums[2:], mass[2:])
    package(down_ref, sums[:2], mass[:2])


def ratio(total, tally):
    return (total * (1.0 / tally)).astype(BF16)


def inner_kernel(
    rows_ref, ids_ref, inner_ref, scale_ref, own_ref, fresh_ref, norm_ref, next_ref, top_ref, total_ref, resp_ref
):
    blocks, size, _ = own_ref.shape
    inner = blocks - 2
    count = rows_ref.shape[0]
    mass = [0.0] * inner
    for start in range(0, count, STEP):
        here = slice(start, start + STEP)
        for k in range(inner):
            there = slice(k * size, (k + 1) * size)
            resp = inner_ref[there, here] * scale_ref[:, here]
            resp_ref[there, here] = resp.astype(BF16)
            mass[k] = mass[k] + resp
    mass = row_sums(mass)
    rows = rows_ref[...]
    new = []
    for k in range(inner):
        total = matmul(resp_ref[k * size : (k + 1) * size, :], rows, ((1,), (0,)))
        new.append(ratio(total + PRIOR * own_ref[k + 1].astype(F32), mass[k] + PRIOR))
        fresh_ref[k] = new[k]
    biases = square_biases(new)
    flat = jnp.concatenate(new, axis=0)
    for start in range(0, count, STEP):
        here = slice(start, start + STEP)
        scores = scored(flat, biases, range(2, inner + 2), rows_ref[here, :], ids_ref[:, here])
        top = highest(scores)
        top_ref[:, here] = top
        safe = jnp.where(top == -jnp.inf, 0.0, top)
        weights = [jnp.exp2(score - safe) for score in scores]
        total_ref[:, here] = added(weights)
        for k in range(inner):
            next_ref[k * size : (k + 1) * size, here] = weights[k]
    eye = diagonal(LANES)
    for start in range(0, count, LANES):
        wide = rows_ref[start : start + LANES, :].astype(F32)
        norm = jnp.sum(wide * wide, axis=1, keepdims=True)
        norm_ref[:, start : start + LANES] = jnp.sum(jnp.where(eye, norm, 0.0), axis=0, keepdims=True)


def second_kernel(
    rows_ref, ids_ref, sums_ref, mass_ref, norm_ref, top_ref, total_ref, below_ref, above_ref,
    edge_ref, outer_ref, scale_ref, ratio_ref, cost_ref, up_ref, down_ref, resp_ref,
):
    size = sums_ref.shape[1]
    inner = 2
    last = inner + 3
    edges = (0, 1, last - 1, last)
    new = []
    for p, pkg in enumerate((below_ref, above_ref)):
        packed = pkg[2 * size :, : 2 * size]
        for k in range(2):
            e = 2 * p + k
            total = sums_ref[e] + pkg[k * size : (k + 1) * size, :].astype(F32)
            new.append(ratio(total, mass_ref[e * size : (e + 1) * size, :] + unpack_mass(packed, k, size)))
    edge_ref[0] = new[1]
    edge_ref[1] = new[2]
    biases = square_biases(new)
    flat = jnp.concatenate(new, axis=0)
    mass = [0.0, 0.0]
    half = 0.5 / math.sqrt(rows_ref.shape[1])
    for start in range(0, rows_ref.shape[0], STEP):
        here = slice(start, start + STEP)
        scores = scored(flat, biases, edges, rows_ref[here, :], ids_ref[:, here])
        top = jnp.maximum(highest(scores), top_ref[:, here])
        shrink = jnp.exp2(top_ref[:, here] - top)
        weights = [jnp.exp2(score - top) for score in scores]
        total = added(weights) + shrink * total_ref[:, here]
        scale = 1.0 / total
        scale_ref[:, here] = scale
        ratio_ref[:, here] = scale * shrink
        cost_ref[:, here] = norm_ref[:, here] * half - (top * (1.0 / LOG2E) + jnp.log(total))
        for k in range(2):
            outer_ref[k * size : (k + 1) * size, here] = weights[k + 1]
            resp = weights[3 * k] * scale
            resp_ref[k * size : (k + 1) * size, here] = resp.astype(BF16)
            mass[k] = mass[k] + resp
    mass = row_sums(mass)
    rows = rows_ref[...]
    for k, pkg in enumerate((down_ref, up_ref)):
        total = matmul(resp_ref[k * size : (k + 1) * size, :], rows, ((1,), (0,)))
        package(pkg, [total], [mass[k]])


def interleave(lines_ref, out_ref, slots):
    count = lines_ref.shape[1]
    pairs = count // slots
    width = LANES * slots
    groups = pairs // LANES
    row = lax.broadcasted_iota(jnp.int32, (width, width), 0)
    lane = lax.broadcasted_iota(jnp.int32, (width, width), 1)
    pick = jnp.where(row == lax.rem(lane, slots) * LANES + lax.div(lane, slots), 1.0, 0.0).astype(BF16)
    pieces = []
    for g in range(groups):
        cuts = [lines_ref[:, s * pairs + g * LANES : s * pairs + (g + 1) * LANES] for s in range(slots)]
        left = jnp.concatenate(cuts, axis=1)
        for _ in range(3):
            piece = left.astype(BF16).astype(F32)
            pieces.append(piece)
            left = left - piece
    pieces += [jnp.zeros_like(pieces[0])] * (-len(pieces) % 16)
    moved = matmul(jnp.concatenate(pieces, axis=0).astype(BF16), pick, ((1,), (0,)))
    for g in range(groups):
        line = moved[3 * g : 3 * g + 1] + moved[3 * g + 1 : 3 * g + 2] + moved[3 * g + 2 : 3 * g + 3]
        for s in range(slots):
            out_ref[g * slots + s : g * slots + s + 1, :] = line[:, s * LANES : (s + 1) * LANES]


def own_kernel(
    slots, rows_ref, inner_ref, ratio_ref, outer_ref, scale_ref, edge_ref, fresh_ref, cost_ref,
    out_hbm, part_ref, mass_ref, placed_ref, done_ref, resp_ref, sem,
):
    inner, size, _ = fresh_ref.shape
    rows = rows_ref[...]

    def summed(weights_ref, by_ref, blocks):
        mass = [0.0] * blocks
        for start in range(0, rows_ref.shape[0], STEP):
            here = slice(start, start + STEP)
            for k in range(blocks):
                there = slice(k * size, (k + 1) * size)
                resp = weights_ref[there, here] * by_ref[:, here]
                resp_ref[there, here] = resp.astype(BF16)
                mass[k] = mass[k] + resp
        sums = [matmul(resp_ref[k * size : (k + 1) * size, :], rows, ((1,), (0,))) for k in range(blocks)]
        return sums, row_sums(mass)

    sums, mass = summed(inner_ref, ratio_ref, inner)
    for k in range(inner):
        done_ref[k] = ratio(sums[k] + PRIOR * fresh_ref[k].astype(F32), mass[k] + PRIOR)
    store = pltpu.make_async_copy(done_ref, out_hbm.at[pl.ds(1, inner)], sem)
    store.start()
    sums, mass = summed(outer_ref, scale_ref, 2)
    for k in range(2):
        part_ref[k] = sums[k] + PRIOR * edge_ref[k].astype(F32)
        mass_ref[k * size : (k + 1) * size, :] = mass[k] + PRIOR
    interleave(cost_ref, placed_ref, slots)
    store.wait()


def last_kernel(given_hbm, part_ref, mass_ref, below_ref, above_ref, out_hbm, done_ref, sems):
    blocks, size, _ = out_hbm.shape
    stores = []
    for e, (k, pkg) in enumerate(((0, below_ref), (blocks - 1, above_ref))):
        total = part_ref[e] + pkg[:size, :].astype(F32)
        tally = mass_ref[e * size : (e + 1) * size, :] + unpack_mass(pkg[size:, :size], 0, size)
        done_ref[e] = ratio(total, tally)
        stores.append(pltpu.make_async_copy(done_ref.at[e], out_hbm.at[k], sems.at[e]))
        stores[-1].start()
    for store in stores:
        store.wait()


def wide_lines(lines, stride):
    return pltpu.VMEM((lines + stride + 4, LANES), F32)


def run_regroup(pairs, dest, rows):
    count, features = rows.shape
    lines = count * features // LANES
    dma = pltpu.SemaphoreType.DMA
    return call(
        functools.partial(regroup_kernel, pairs),
        [(dest, HBM), (rows, HBM)],
        [(((lines, LANES), BF16), HBM)],
        [
            VMEM((1, count), jnp.int32),
            VMEM((count, features), BF16),
            wide_lines(lines, lines // pairs),
            VMEM((lines, LANES), BF16),
            dma((2,)),
            dma((4,)),
        ],
        2 * count * features * count,
    )


def run_first(pairs, arrived, ids, left, own, right):
    lines, count = arrived.shape[0], ids.shape[1]
    blocks, size, features = own.shape
    window = blocks + 2
    two = (((2 * size + MASS_ROWS, features), BF16), VMEM)
    return call(
        functools.partial(first_kernel, pairs),
        [(arrived, VMEM), (ids, VMEM), (left, VMEM), (own, VMEM), (right, VMEM)],
        [
            (((count, features), BF16), VMEM),
            ((((blocks - 2) * size, count), F32), VMEM),
            (((1, count), F32), VMEM),
            (((4, size, features), F32), VMEM),
            (((4 * size, 1), F32), VMEM),
            two,
            two,
        ],
        [wide_lines(lines, lines // pairs), VMEM((4 * size, count), BF16)],
        2 * count * features * (window + 4) * size,
    )


def run_inner(rows, ids, inner, scale, own):
    blocks, size, features = own.shape
    count = rows.shape[0]
    line = (((1, count), F32), VMEM)
    return call(
        inner_kernel,
        [(x, VMEM) for x in (rows, ids, inner, scale, own)],
        [(((blocks - 2, size, features), BF16), VMEM), line, ((inner.shape, F32), VMEM), line, line],
        [VMEM(inner.shape, BF16)],
        2 * count * features * 4 * size,
    )


def run_second(rows, ids, sums, mass, norm, top, total, below, above):
    _, size, features = sums.shape
    count = rows.shape[0]
    line = (((1, count), F32), VMEM)
    one = (((size + MASS_ROWS, features), BF16), VMEM)
    return call(
        second_kernel,
        [(x, VMEM) for x in (rows, ids, sums, mass, norm, top, total, below, above)],
        [(((2, size, features), BF16), VMEM), (((2 * size, count), F32), VMEM), line, line, line, one, one],
        [VMEM((2 * size, count), BF16)],
        2 * count * features * 6 * size,
    )


def run_own(slots, rows, inner, ratios, outer, scale, edge, fresh, cost):
    blocks, size, features = fresh.shape[0] + 2, fresh.shape[1], fresh.shape[2]
    count = rows.shape[0]
    return call(
        functools.partial(own_kernel, slots),
        [(x, VMEM) for x in (rows, inner, ratios, outer, scale, edge, fresh, cost)],
        [
            (((blocks, size, features), BF16), HBM),
            (((2, size, features), F32), VMEM),
            (((2 * size, 1), F32), VMEM),
            (((count // LANES, LANES), F32), VMEM),
        ],
        [VMEM((blocks - 2, size, features), BF16), VMEM((2 * size, count), BF16), pltpu.SemaphoreType.DMA],
        2 * count * features * blocks * size,
    )


def run_last(given, part, mass, below, above):
    return call(
        last_kernel,
        [(given, HBM)] + [(x, VMEM) for x in (part, mass, below, above)],
        [((given.shape, BF16), HBM)],
        [VMEM(part.shape, BF16), pltpu.SemaphoreType.DMA((2,))],
        aliases={0: 0},
    )


def swap(up, down, axis):
    devices = lax.axis_size(axis)
    pairs = [(i, i + 1) for i in range(devices - 1)]
    below = lax.ppermute(up, axis, pairs)
    above = lax.ppermute(down, axis, [(j, i) for i, j in pairs])
    return below, above


def per_device(sample_rows, destination, neighbours, centroids):
    own_count, rep_count = lax.axis_size("own"), lax.axis_size("rep")
    pairs = own_count * rep_count
    count, features = sample_rows.shape
    per_pair = count // pairs
    chunks = features // LANES
    lines = count * chunks
    blocks, _, size, _ = centroids.shape
    own = centroids.reshape(blocks, size, features)
    outgoing = run_regroup(pairs, destination.reshape(1, count), sample_rows)
    left, right = swap(own[blocks - 1], own[0], "own")
    first_block = lax.axis_index("own") * blocks - 1
    ids = (neighbours // rep_count - first_block).T
    ids = ids.reshape(-1, pairs, per_pair).swapaxes(1, 2).reshape(-1, count)
    arrived = lax.all_to_all(
        outgoing.reshape(pairs, lines // pairs // 4, 4, LANES), ("own", "rep"), split_axis=0, concat_axis=0, tiled=True
    ).reshape(lines, LANES)

    rows, inner1, scale1, sums1, mass1, up1, down1 = run_first(pairs, arrived, ids, left, own, right)
    below1, above1 = swap(up1, down1, "own")
    fresh, norm, inner2, top, total = run_inner(rows, ids, inner1, scale1, own)
    edge, outer, scale2, ratio2, cost, up2, down2 = run_second(rows, ids, sums1, mass1, norm, top, total, below1, above1)
    below2, above2 = swap(up2, down2, "own")
    given, part, mass2, placed = run_own(per_pair, rows, inner2, ratio2, outer, scale2, edge, fresh, cost)
    out = run_last(given, part, mass2, below2, above2)
    return out.reshape(centroids.shape), placed.reshape(count)


def solution(mesh):
    return jax.shard_map(
        per_device,
        mesh=mesh,
        in_specs=(
            P(("own", "rep"), None),
            P(("own", "rep")),
            P(("own", "rep"), None),
            P("own", "rep", None, None),
        ),
        out_specs=(P("own", "rep", None, None), P(("own", "rep"))),
        check_vma=False,
    )
```

time: 107 us -> 107 us (level)
  transfers between devices with their start and end apart: 7 -> 7, of which waited for: 7 -> 7; matrix products, arithmetic and copies ran while one was open for 2% -> 2% of each run, Pallas kernels for 2% -> 3%
where the time goes in v3:
time: 107 us; the launch traced here: 106 us
  starting transfers between devices  47.6 us (44%)
  waiting for transfers between devices  42.4 us (40%)
  Pallas kernels  13.6 us (13%)
  local copies, waits for them, and re-layouts  1.73 us (2%)
    ppermute x3, waiting for transfers between devices, swap(): above = lax.ppermute(down, axis, [(j, i) for i, j in pairs])  28.4 us
    all_to_all x1, starting transfers between devices, per_device(): lax.all_to_all(outgoing.reshape(pairs, lines // pairs // 4, 4, LANES), ('...  21.1 us
    ppermute x3, starting transfers between devices, swap(): above = lax.ppermute(down, axis, [(j, i) for i, j in pairs])  18.9 us
    pallas_call x6, Pallas kernels, call(): pl.pallas_call(kernel, in_specs=[pl.BlockSpec(memory_space=space) for _,...  13.6 us
    ppermute x3, waiting for transfers between devices, swap(): below = lax.ppermute(up, axis, pairs)  12.6 us
    ppermute x3, starting transfers between devices, swap(): below = lax.ppermute(up, axis, pairs)  7.56 us
  transfers between devices with their start and end apart: 7, of which 7 were waited for; matrix products, arithmetic and copies ran while one was open for 2% of the time, Pallas kernels for 3%

profile of v3, /device:TPU:8, one launch (start us, length us, event | category | flops | bytes accessed | tf_op | source)
XLA Modules:
  0.0 106.2 jit_solution(13977079392835884487)
XLA Ops:
  0.6 4.2 %shard_map.59 = bf16[6144,128]{1,0:T(8,128)(2,1)} custom-call(s32[1,1024]{1,0:T(1,128)} %bitcast.31, bf16[1024,768]{1,0:T(8,128)(2,1)} %rows_hbm.1), custom_call_target="tpu_custom_call" | custom-call | flops 1610612736 | bytes 1048576 | tf_op jit(solution)/shard_map/pallas_call | solution.py:24
  4.8 0.0 copy-start
  4.8 0.0 copy-start.1
  4.8 21.1 %all-to-all-start = ((bf16[512,3,4,128]{3,2,1,0:T(4,128)(2,1)}), bf16[512,3,4,128]{3,2,1,0:T(4,128)(2,1)S(1)}, u32[]{:S(2)}, u32[]{:S(2)}) async-start(bf16[512,3,4,128]{3,2,1,0:T(4,128)(2,1)} %bitcast.29), calls=%async_computation | async-start | bytes 3145728 | tf_op jit(solution)/shard_map/all_to_all | solution.py:492
  26.0 0.0 copy-done
  26.0 0.7 slice_bitcast_fusion
  26.7 8.2 %collective-permute-start.1 = (bf16[128,768]{1,0:T(8,128)(2,1)}, bf16[128,768]{1,0:T(8,128)(2,1)S(1)}, u32[]{:S(2)}, u32[]{:S(2)}) collective-permute-start(bf16[128,768]{1,0:T(8,128)(2,1)} %get-tuple-element.52), channel_id=1, source_target_pairs={{8,0},{16,8},{24,16},{32,24},{40,32},{48,40},{56,48},{64,56},{72,6... | collective-permute-start | bytes 589832 | tf_op jit(solution)/shard_map/ppermute | solution.py:474
  34.9 1.9 %collective-permute-start = (bf16[128,768]{1,0:T(8,128)(2,1)S(1)}, bf16[128,768]{1,0:T(8,128)(2,1)S(1)}, u32[]{:S(2)}, u32[]{:S(2)}) collective-permute-start(bf16[128,768]{1,0:T(8,128)(2,1)S(1)} %get-tuple-element.53), channel_id=1, source_target_pairs={{0,8},{8,16},{16,24},{24,32},{32,40},{40,48},{48,56},{56,64},{64,7... | collective-permute-start | bytes 589832 | tf_op jit(solution)/shard_map/ppermute | solution.py:473
  36.8 0.0 copy-done.1
  36.8 0.2 copy.9
  37.1 0.2 copy.12
  37.3 26.0 %collective-permute-done.1.right_ref = bf16[128,768]{1,0:T(8,128)(2,1)S(1)} collective-permute-done((bf16[128,768]{1,0:T(8,128)(2,1)}, bf16[128,768]{1,0:T(8,128)(2,1)S(1)}, u32[]{:S(2)}, u32[]{:S(2)}) %collective-permute-start.1) | collective-permute-done | bytes 196640 | tf_op jit(solution)/shard_map/ppermute | solution.py:474
  63.3 5.5 %collective-permute-done.left_ref = bf16[128,768]{1,0:T(8,128)(2,1)S(1)} collective-permute-done((bf16[128,768]{1,0:T(8,128)(2,1)S(1)}, bf16[128,768]{1,0:T(8,128)(2,1)S(1)}, u32[]{:S(2)}, u32[]{:S(2)}) %collective-permute-start) | collective-permute-done | bytes 196640 | tf_op jit(solution)/shard_map/ppermute | solution.py:473
  68.8 1.5 %all-to-all-done = bf16[512,3,4,128]{3,2,1,0:T(4,128)(2,1)S(1)} async-done(((bf16[512,3,4,128]{3,2,1,0:T(4,128)(2,1)}), bf16[512,3,4,128]{3,2,1,0:T(4,128)(2,1)S(1)}, u32[]{:S(2)}, u32[]{:S(2)}) %all-to-all-start) | async-done | bytes 1572896 | tf_op jit(solution)/shard_map/all_to_all | solution.py:492
  70.2 3.4 %shard_map.60 = (bf16[1024,768]{1,0:T(8,128)(2,1)S(1)}, f32[256,1024]{1,0:T(8,128)S(1)}, f32[1,1024]{1,0:T(1,128)S(1)}, f32[4,128,768]{2,1,0:T(8,128)S(1)}, f32[...) custom-call(bf16[6144,128]{1,0:T(8,128)(2,1)S(1)} %bitcast.24, ...), custom_call_target="tpu_custom_call" | custom-call | flops 2013265920 | bytes 1048576 | tf_op jit(solution)/shard_map/pallas_call | solution.py:24
  73.7 3.0 %collective-permute-start.2 = (bf16[272,768]{1,0:T(8,128)(2,1)S(1)}, bf16[272,768]{1,0:T(8,128)(2,1)S(1)}, u32[]{:S(2)}, u32[]{:S(2)}) collective-permute-start(bf16[272,768]{1,0:T(8,128)(2,1)S(1)} %get-tuple-element.34), channel_id=1, source_target_pairs={{0,8},{8,16},{16,24},{24,32},{32,40},{40,48},{48,56},{56,64},{64,7... | collective-permute-start | bytes 1253384 | tf_op jit(solution)/shard_map/ppermute | solution.py:473
  76.7 5.0 %collective-permute-start.3 = (bf16[272,768]{1,0:T(8,128)(2,1)S(1)}, bf16[272,768]{1,0:T(8,128)(2,1)S(1)}, u32[]{:S(2)}, u32[]{:S(2)}) collective-permute-start(bf16[272,768]{1,0:T(8,128)(2,1)S(1)} %get-tuple-element.35), channel_id=1, source_target_pairs={{8,0},{16,8},{24,16},{32,24},{40,32},{48,40},{56,48},{64,56},{72,6... | collective-permute-start | bytes 1253384 | tf_op jit(solution)/shard_map/ppermute | solution.py:474
  81.6 1.5 %shard_map.61 = (bf16[2,128,768]{2,1,0:T(8,128)(2,1)S(1)}, f32[1,1024]{1,0:T(1,128)S(1)}, f32[256,1024]{1,0:T(8,128)S(1)}, f32[1,1024]{1,0:T(1,128)S(1)}, f32[1,1024]{1,0:T(1,128)S(1)}) custom-call(bf16[1024,768]{1,0:T(8,128)(2,1)S(1)} %get-tuple-element.25.rows_ref, s32[4,1024]{1,0:T(4,128)S(1)} %bitcast.26, f32[256,1024]{1,0:T(8,128)S(1)} %get-tuple-element.26.inner_ref, ...), custom_call_target="tpu_custom_call" | custom-call | flops 805306368 | bytes 1048576 | tf_op jit(solution)/shard_map/pallas_call | solution.py:24
  83.1 6.4 %collective-permute-done.2.below_ref = bf16[272,768]{1,0:T(8,128)(2,1)S(1)} collective-permute-done((bf16[272,768]{1,0:T(8,128)(2,1)S(1)}, bf16[272,768]{1,0:T(8,128)(2,1)S(1)}, u32[]{:S(2)}, u32[]{:S(2)}) %collective-permute-start.2) | collective-permute-done | bytes 417824 | tf_op jit(solution)/shard_map/ppermute | solution.py:473
  89.5 1.2 %collective-permute-done.3.above_ref = bf16[272,768]{1,0:T(8,128)(2,1)S(1)} collective-permute-done((bf16[272,768]{1,0:T(8,128)(2,1)S(1)}, bf16[272,768]{1,0:T(8,128)(2,1)S(1)}, u32[]{:S(2)}, u32[]{:S(2)}) %collective-permute-start.3) | collective-permute-done | bytes 417824 | tf_op jit(solution)/shard_map/ppermute | solution.py:474
  90.6 2.2 %shard_map.62 = (bf16[2,128,768]{2,1,0:T(8,128)(2,1)S(1)}, f32[256,1024]{1,0:T(8,128)S(1)}, f32[1,1024]{1,0:T(1,128)S(1)}, f32[1,1024]{1,0:T(1,128)S(1)}, f32[1,...) custom-call(bf16[1024,768]{1,0:T(8,128)(2,1)S(1)} %get-tuple-element.25.rows_ref, ...), custom_call_target="tpu_custom_call" | custom-call | flops 1207959552 | bytes 1048576 | tf_op jit(solution)/shard_map/pallas_call | solution.py:24
  92.9 2.6 %collective-permute-start.4 = (bf16[144,768]{1,0:T(8,128)(2,1)S(1)}, bf16[144,768]{1,0:T(8,128)(2,1)S(1)}, u32[]{:S(2)}, u32[]{:S(2)}) collective-permute-start(bf16[144,768]{1,0:T(8,128)(2,1)S(1)} %get-tuple-element.45), channel_id=1, source_target_pairs={{0,8},{8,16},{16,24},{24,32},{32,40},{40,48},{48,56},{56,64},{64,7... | collective-permute-start | bytes 663560 | tf_op jit(solution)/shard_map/ppermute | solution.py:473
  95.5 5.8 %collective-permute-start.5 = (bf16[144,768]{1,0:T(8,128)(2,1)S(1)}, bf16[144,768]{1,0:T(8,128)(2,1)S(1)}, u32[]{:S(2)}, u32[]{:S(2)}) collective-permute-start(bf16[144,768]{1,0:T(8,128)(2,1)S(1)} %get-tuple-element.46), channel_id=1, source_target_pairs={{8,0},{16,8},{24,16},{32,24},{40,32},{48,40},{56,48},{64,56},{72,6... | collective-permute-start | bytes 663560 | tf_op jit(solution)/shard_map/ppermute | solution.py:474
  101.3 1.4 %shard_map.63 = (bf16[4,128,768]{2,1,0:T(8,128)(2,1)}, f32[2,128,768]{2,1,0:T(8,128)S(1)}, f32[256,1]{1,0:T(8,128)S(1)}, f32[8,128]{1,0:T(8,128)S(1)}) custom-call(bf16[1024,768]{1,0:T(8,128)(2,1)S(1)} %get-tuple-element.25.rows_ref, f32[256,1024]{1,0:T(8,128)S(1)} %get-tuple-element.28.inner_ref, f32[1,1024]{1,0:T(1,128)S(1)} %get-tuple-element.36.ratio_ref, ...), custom_call_target="tpu_custom_call" | custom-call | flops 805306368 | bytes 1048576 | tf_op jit(solution)/shard_map/pallas_call | solution.py:24
  102.7 0.6 copy.15
  103.3 0.7 collective-permute-done.4.below_ref
  104.0 1.2 %collective-permute-done.5.above_ref = bf16[144,768]{1,0:T(8,128)(2,1)S(1)} collective-permute-done((bf16[144,768]{1,0:T(8,128)(2,1)S(1)}, bf16[144,768]{1,0:T(8,128)(2,1)S(1)}, u32[]{:S(2)}, u32[]{:S(2)}) %collective-permute-start.5) | collective-permute-done | bytes 221216 | tf_op jit(solution)/shard_map/ppermute | solution.py:474
  105.2 1.0 shard_map.64
  (1 shorter events, 0.0 us)
Async XLA Ops:
  4.8 21.1 %copy-start = (bf16[4,1,128,768]{3,2,1,0:T(8,128)(2,1)S(1)}, bf16[4,1,128,768]{3,2,1,0:T(8,128)(2,1)}, u32[]{:S(2)}) copy-start(bf16[4,1,128,768]{3,2,1,0:T(8,128)(2,1)} %param.7) | copy-start | bytes 2359300
  4.8 32.0 %copy-start.1 = (s32[1024,4]{0,1:T(4,128)S(1)}, s32[1024,4]{0,1:T(4,128)}, u32[]{:S(2)}) copy-start(s32[1024,4]{0,1:T(4,128)} %param.6) | copy-start | bytes 49156
  4.8 65.4 %all-to-all-start = ((bf16[512,3,4,128]{3,2,1,0:T(4,128)(2,1)}), bf16[512,3,4,128]{3,2,1,0:T(4,128)(2,1)S(1)}, u32[]{:S(2)}, u32[]{:S(2)}) async-start(bf16[512,3,4,128]{3,2,1,0:T(4,128)(2,1)} %bitcast.29), calls=%async_computation | async-start | bytes 3145728 | tf_op jit(solution)/shard_map/all_to_all | solution.py:492
  26.7 36.6 %collective-permute-start.1 = (bf16[128,768]{1,0:T(8,128)(2,1)}, bf16[128,768]{1,0:T(8,128)(2,1)S(1)}, u32[]{:S(2)}, u32[]{:S(2)}) collective-permute-start(bf16[128,768]{1,0:T(8,128)(2,1)} %get-tuple-element.52), channel_id=1, source_target_pairs={{8,0},{16,8},{24,16},{32,24},{40,32},{48,40},{56,48},{64,56},{72,6... | collective-permute-start | bytes 589832 | tf_op jit(solution)/shard_map/ppermute | solution.py:474
  34.9 33.9 %collective-permute-start = (bf16[128,768]{1,0:T(8,128)(2,1)S(1)}, bf16[128,768]{1,0:T(8,128)(2,1)S(1)}, u32[]{:S(2)}, u32[]{:S(2)}) collective-permute-start(bf16[128,768]{1,0:T(8,128)(2,1)S(1)} %get-tuple-element.53), channel_id=1, source_target_pairs={{0,8},{8,16},{16,24},{24,32},{32,40},{40,48},{48,56},{56,64},{64,7... | collective-permute-start | bytes 589832 | tf_op jit(solution)/shard_map/ppermute | solution.py:473
  73.7 15.8 %collective-permute-start.2 = (bf16[272,768]{1,0:T(8,128)(2,1)S(1)}, bf16[272,768]{1,0:T(8,128)(2,1)S(1)}, u32[]{:S(2)}, u32[]{:S(2)}) collective-permute-start(bf16[272,768]{1,0:T(8,128)(2,1)S(1)} %get-tuple-element.34), channel_id=1, source_target_pairs={{0,8},{8,16},{16,24},{24,32},{32,40},{40,48},{48,56},{56,64},{64,7... | collective-permute-start | bytes 1253384 | tf_op jit(solution)/shard_map/ppermute | solution.py:473
  76.7 13.9 %collective-permute-start.3 = (bf16[272,768]{1,0:T(8,128)(2,1)S(1)}, bf16[272,768]{1,0:T(8,128)(2,1)S(1)}, u32[]{:S(2)}, u32[]{:S(2)}) collective-permute-start(bf16[272,768]{1,0:T(8,128)(2,1)S(1)} %get-tuple-element.35), channel_id=1, source_target_pairs={{8,0},{16,8},{24,16},{32,24},{40,32},{48,40},{56,48},{64,56},{72,6... | collective-permute-start | bytes 1253384 | tf_op jit(solution)/shard_map/ppermute | solution.py:474
  92.9 11.2 %collective-permute-start.4 = (bf16[144,768]{1,0:T(8,128)(2,1)S(1)}, bf16[144,768]{1,0:T(8,128)(2,1)S(1)}, u32[]{:S(2)}, u32[]{:S(2)}) collective-permute-start(bf16[144,768]{1,0:T(8,128)(2,1)S(1)} %get-tuple-element.45), channel_id=1, source_target_pairs={{0,8},{8,16},{16,24},{24,32},{32,40},{40,48},{48,56},{56,64},{64,7... | collective-permute-start | bytes 663560 | tf_op jit(solution)/shard_map/ppermute | solution.py:473
  95.5 9.7 %collective-permute-start.5 = (bf16[144,768]{1,0:T(8,128)(2,1)S(1)}, bf16[144,768]{1,0:T(8,128)(2,1)S(1)}, u32[]{:S(2)}, u32[]{:S(2)}) collective-permute-start(bf16[144,768]{1,0:T(8,128)(2,1)S(1)} %get-tuple-element.46), channel_id=1, source_target_pairs={{8,0},{16,8},{24,16},{32,24},{40,32},{48,40},{56,48},{64,56},{72,6... | collective-permute-start | bytes 663560 | tf_op jit(solution)/shard_map/ppermute | solution.py:474

commit v4 on v3

--- a/solution.py
+++ b/solution.py
@@ -172,38 +172,60 @@
     return ((total + PRIOR * previous.astype(F32)) / (tally + PRIOR)).astype(BF16)
 
 
+def arrival_kernel(
+    pairs, lines_ref, ids_ref, own_ref, rows_ref, weights_ref, top_ref, total_ref, wide
+):
+    blocks, size, _ = own_ref.shape
+    own = [own_ref[k] for k in range(blocks)]
+    biases = square_biases(own)
+    flat = jnp.concatenate(own, axis=0)
+    unpack_rows(lines_ref, rows_ref, wide, pairs)
+    for start in range(0, rows_ref.shape[0], STEP):
+        here = slice(start, start + STEP)
+        scores = scored(flat, biases, range(1, blocks + 1), rows_ref[here, :], ids_ref[:, here])
+        top = highest(scores)
+        top_ref[:, here] = top
+        weights = [jnp.exp2(score - top) for score in scores]
+        total_ref[:, here] = added(weights)
+        for k in range(blocks):
+            weights_ref[k * size : (k + 1) * size, here] = weights[k]
+
+
 def first_kernel(
-    pairs, lines_ref, ids_ref, left_ref, own_ref, right_ref,
-    rows_ref, inner_ref, scale_ref, sums_ref, mass_ref, up_ref, down_ref, wide, resp_ref,
+    rows_ref, ids_ref, weights_ref, top_ref, total_ref, left_ref, own_ref, right_ref,
+    scale_ref, sums_ref, mass_ref, up_ref, down_ref, resp_ref,
 ):
-    blocks = [left_ref[...]] + [own_ref[k] for k in range(own_ref.shape[0])] + [right_ref[...]]
-    last = len(blocks) - 1
-    size = own_ref.shape[1]
-    biases = square_biases(blocks)
-    flat = jnp.concatenate(blocks, axis=0)
-    unpack_rows(lines_ref, rows_ref, wide, pairs)
-    edges = (0, 1, last - 1, last)
+    count_own, size, _ = own_ref.shape
+    last = count_own + 1
+    halo = [left_ref[...], right_ref[...]]
+    biases = square_biases(halo)
+    flat = jnp.concatenate(halo, axis=0)
+    edges = (halo[0], own_ref[0], own_ref[count_own - 1], halo[1])
     mass = [0.0] * len(edges)
-    count = rows_ref.shape[0]
-    for start in range(0, count, STEP):
+    for start in range(0, rows_ref.shape[0], STEP):
         here = slice(start, start + STEP)
-        scores = scored(flat, biases, range(last + 1), rows_ref[here, :], ids_ref[:, here])
-        top = highest(scores)
+        scores = scored(flat, biases, (0, last), rows_ref[here, :], ids_ref[:, here])
+        top = jnp.maximum(highest(scores), top_ref[:, here])
+        shrink = jnp.exp2(top_ref[:, here] - top)
         weights = [jnp.exp2(score - top) for score in scores]
-        scale = 1.0 / added(weights)
-        scale_ref[:, here] = scale
-        for k in range(2, last - 1):
-            inner_ref[(k - 2) * size : (k - 1) * size, here] = weights[k]
-        for k, w in enumerate(edges):
-            resp = weights[w] * scale
+        scale = 1.0 / (added(weights) + shrink * total_ref[:, here])
+        own_scale = shrink * scale
+        scale_ref[:, here] = own_scale
+        resps = (
+            weights[0] * scale,
+            weights_ref[:size, here] * own_scale,
+            weights_ref[(count_own - 1) * size :, here] * own_scale,
+            weights[1] * scale,
+        )
+        for k, resp in enumerate(resps):
             resp_ref[k * size : (k + 1) * size, here] = resp.astype(BF16)
             mass[k] = mass[k] + resp
     mass = row_sums(mass)
     rows = rows_ref[...]
     sums = []
-    for k, w in enumerate(edges):
+    for k, block in enumerate(edges):
         total = matmul(resp_ref[k * size : (k + 1) * size, :], rows, ((1,), (0,)))
-        sums_ref[k] = total + PRIOR * blocks[w].astype(F32)
+        sums_ref[k] = total + PRIOR * block.astype(F32)
         sums.append(total)
         mass_ref[k * size : (k + 1) * size, :] = mass[k] + PRIOR
     package(up_ref, sums[2:], mass[2:])
@@ -215,7 +237,7 @@
 
 
 def inner_kernel(
-    rows_ref, ids_ref, inner_ref, scale_ref, own_ref, fresh_ref, norm_ref, next_ref, top_ref, total_ref, resp_ref
+    rows_ref, ids_ref, weights_ref, scale_ref, own_ref, fresh_ref, norm_ref, next_ref, top_ref, total_ref, resp_ref
 ):
     blocks, size, _ = own_ref.shape
     inner = blocks - 2
@@ -225,7 +247,7 @@
         here = slice(start, start + STEP)
         for k in range(inner):
             there = slice(k * size, (k + 1) * size)
-            resp = inner_ref[there, here] * scale_ref[:, here]
+            resp = weights_ref[(k + 1) * size : (k + 2) * size, here] * scale_ref[:, here]
             resp_ref[there, here] = resp.astype(BF16)
             mass[k] = mass[k] + resp
     mass = row_sums(mass)
@@ -254,41 +276,70 @@
         norm_ref[:, start : start + LANES] = jnp.sum(jnp.where(eye, norm, 0.0), axis=0, keepdims=True)
 
 
-def second_kernel(
-    rows_ref, ids_ref, sums_ref, mass_ref, norm_ref, top_ref, total_ref, below_ref, above_ref,
-    edge_ref, outer_ref, scale_ref, ratio_ref, cost_ref, up_ref, down_ref, resp_ref,
+def renewed(pkg_ref, sums, masses):
+    size = sums[0].shape[0]
+    packed = pkg_ref[2 * size :, : 2 * size]
+    new = []
+    for k in range(2):
+        total = sums[k] + pkg_ref[k * size : (k + 1) * size, :].astype(F32)
+        new.append(ratio(total, masses[k] + unpack_mass(packed, k, size)))
+    return new
+
+
+def below_kernel(
+    rows_ref, ids_ref, sums_ref, mass_ref, top_ref, total_ref, below_ref,
+    edge_ref, weights_ref, new_top_ref, new_total_ref, shrink_ref,
 ):
     size = sums_ref.shape[1]
-    inner = 2
-    last = inner + 3
-    edges = (0, 1, last - 1, last)
-    new = []
-    for p, pkg in enumerate((below_ref, above_ref)):
-        packed = pkg[2 * size :, : 2 * size]
+    new = renewed(below_ref, [sums_ref[k] for k in range(2)], [mass_ref[k * size : (k + 1) * size, :] for k in range(2)])
+    edge_ref[...] = new[1]
+    biases = square_biases(new)
+    flat = jnp.concatenate(new, axis=0)
+    for start in range(0, rows_ref.shape[0], STEP):
+        here = slice(start, start + STEP)
+        scores = scored(flat, biases, (0, 1), rows_ref[here, :], ids_ref[:, here])
+        before = top_ref[:, here]
+        top = jnp.maximum(highest(scores), before)
+        safe = jnp.where(top == -jnp.inf, 0.0, top)
+        shrink = jnp.exp2(before - safe)
+        weights = [jnp.exp2(score - safe) for score in scores]
+        new_top_ref[:, here] = top
+        shrink_ref[:, here] = shrink
+        new_total_ref[:, here] = added(weights) + shrink * total_ref[:, here]
         for k in range(2):
-            e = 2 * p + k
-            total = sums_ref[e] + pkg[k * size : (k + 1) * size, :].astype(F32)
-            new.append(ratio(total, mass_ref[e * size : (e + 1) * size, :] + unpack_mass(packed, k, size)))
-    edge_ref[0] = new[1]
-    edge_ref[1] = new[2]
+            weights_ref[k * size : (k + 1) * size, here] = weights[k]
+
+
+def above_kernel(
+    rows_ref, ids_ref, sums_ref, mass_ref, norm_ref, top_ref, total_ref, shrink_ref, weights_ref, above_ref,
+    edge_ref, outer_ref, above_scale_ref, below_scale_ref, inner_scale_ref, cost_ref, up_ref, down_ref, resp_ref,
+):
+    size = sums_ref.shape[1]
+    last = 5
+    new = renewed(
+        above_ref, [sums_ref[k] for k in range(2, 4)], [mass_ref[k * size : (k + 1) * size, :] for k in range(2, 4)]
+    )
+    edge_ref[...] = new[0]
     biases = square_biases(new)
     flat = jnp.concatenate(new, axis=0)
     mass = [0.0, 0.0]
     half = 0.5 / math.sqrt(rows_ref.shape[1])
     for start in range(0, rows_ref.shape[0], STEP):
         here = slice(start, start + STEP)
-        scores = scored(flat, biases, edges, rows_ref[here, :], ids_ref[:, here])
-        top = jnp.maximum(highest(scores), top_ref[:, here])
-        shrink = jnp.exp2(top_ref[:, here] - top)
+        scores = scored(flat, biases, (last - 1, last), rows_ref[here, :], ids_ref[:, here])
+        before = top_ref[:, here]
+        top = jnp.maximum(highest(scores), before)
+        fade = jnp.exp2(before - top)
         weights = [jnp.exp2(score - top) for score in scores]
-        total = added(weights) + shrink * total_ref[:, here]
+        total = added(weights) + fade * total_ref[:, here]
         scale = 1.0 / total
-        scale_ref[:, here] = scale
-        ratio_ref[:, here] = scale * shrink
+        below_scale = scale * fade
+        above_scale_ref[:, here] = scale
+        below_scale_ref[:, here] = below_scale
+        inner_scale_ref[:, here] = below_scale * shrink_ref[:, here]
         cost_ref[:, here] = norm_ref[:, here] * half - (top * (1.0 / LOG2E) + jnp.log(total))
-        for k in range(2):
-            outer_ref[k * size : (k + 1) * size, here] = weights[k + 1]
-            resp = weights[3 * k] * scale
+        outer_ref[:, here] = weights[0]
+        for k, resp in enumerate((weights_ref[:size, here] * below_scale, weights[1] * scale)):
             resp_ref[k * size : (k + 1) * size, here] = resp.astype(BF16)
             mass[k] = mass[k] + resp
     mass = row_sums(mass)
@@ -323,32 +374,34 @@
 
 
 def own_kernel(
-    slots, rows_ref, inner_ref, ratio_ref, outer_ref, scale_ref, edge_ref, fresh_ref, cost_ref,
+    slots, rows_ref, inner_ref, inner_scale_ref, below_ref, below_scale_ref, above_ref, above_scale_ref,
+    below_edge_ref, above_edge_ref, fresh_ref, cost_ref,
     out_hbm, part_ref, mass_ref, placed_ref, done_ref, resp_ref, sem,
 ):
     inner, size, _ = fresh_ref.shape
     rows = rows_ref[...]
 
-    def summed(weights_ref, by_ref, blocks):
-        mass = [0.0] * blocks
+    def summed(weights):
+        mass = [0.0] * len(weights)
         for start in range(0, rows_ref.shape[0], STEP):
             here = slice(start, start + STEP)
-            for k in range(blocks):
-                there = slice(k * size, (k + 1) * size)
-                resp = weights_ref[there, here] * by_ref[:, here]
-                resp_ref[there, here] = resp.astype(BF16)
+            for k, (ref, first, by_ref) in enumerate(weights):
+                resp = ref[first : first + size, here] * by_ref[:, here]
+                resp_ref[k * size : (k + 1) * size, here] = resp.astype(BF16)
                 mass[k] = mass[k] + resp
-        sums = [matmul(resp_ref[k * size : (k + 1) * size, :], rows, ((1,), (0,))) for k in range(blocks)]
+        sums = [
+            matmul(resp_ref[k * size : (k + 1) * size, :], rows, ((1,), (0,))) for k in range(len(weights))
+        ]
         return sums, row_sums(mass)
 
-    sums, mass = summed(inner_ref, ratio_ref, inner)
+    sums, mass = summed([(inner_ref, k * size, inner_scale_ref) for k in range(inner)])
     for k in range(inner):
         done_ref[k] = ratio(sums[k] + PRIOR * fresh_ref[k].astype(F32), mass[k] + PRIOR)
     store = pltpu.make_async_copy(done_ref, out_hbm.at[pl.ds(1, inner)], sem)
     store.start()
-    sums, mass = summed(outer_ref, scale_ref, 2)
-    for k in range(2):
-        part_ref[k] = sums[k] + PRIOR * edge_ref[k].astype(F32)
+    sums, mass = summed([(below_ref, size, below_scale_ref), (above_ref, 0, above_scale_ref)])
+    for k, edge_ref in enumerate((below_edge_ref, above_edge_ref)):
+        part_ref[k] = sums[k] + PRIOR * edge_ref[...].astype(F32)
         mass_ref[k * size : (k + 1) * size, :] = mass[k] + PRIOR
     interleave(cost_ref, placed_ref, slots)
     store.wait()
@@ -391,61 +444,79 @@
     )
 
 
-def run_first(pairs, arrived, ids, left, own, right):
+def run_arrival(pairs, arrived, ids, own):
     lines, count = arrived.shape[0], ids.shape[1]
     blocks, size, features = own.shape
-    window = blocks + 2
-    two = (((2 * size + MASS_ROWS, features), BF16), VMEM)
-    return call(
-        functools.partial(first_kernel, pairs),
-        [(arrived, VMEM), (ids, VMEM), (left, VMEM), (own, VMEM), (right, VMEM)],
-        [
-            (((count, features), BF16), VMEM),
-            ((((blocks - 2) * size, count), F32), VMEM),
-            (((1, count), F32), VMEM),
-            (((4, size, features), F32), VMEM),
-            (((4 * size, 1), F32), VMEM),
-            two,
-            two,
-        ],
-        [wide_lines(lines, lines // pairs), VMEM((4 * size, count), BF16)],
-        2 * count * features * (window + 4) * size,
-    )
-
-
-def run_inner(rows, ids, inner, scale, own):
+    line = (((1, count), F32), VMEM)
+    return call(
+        functools.partial(arrival_kernel, pairs),
+        [(arrived, VMEM), (ids, VMEM), (own, VMEM)],
+        [(((count, features), BF16), VMEM), (((blocks * size, count), F32), VMEM), line, line],
+        [wide_lines(lines, lines // pairs)],
+        2 * count * features * blocks * size,
+    )
+
+
+def run_first(rows, ids, weights, top, total, left, own, right):
     blocks, size, features = own.shape
     count = rows.shape[0]
+    two = (((2 * size + MASS_ROWS, features), BF16), VMEM)
+    return call(
+        first_kernel,
+        [(x, VMEM) for x in (rows, ids, weights, top, total, left, own, right)],
+        [(((1, count), F32), VMEM), (((4, size, features), F32), VMEM), (((4 * size, 1), F32), VMEM), two, two],
+        [VMEM((4 * size, count), BF16)],
+        2 * count * features * 6 * size,
+    )
+
+
+def run_inner(rows, ids, weights, scale, own):
+    blocks, size, features = own.shape
+    count = rows.shape[0]
+    inner = (blocks - 2) * size
     line = (((1, count), F32), VMEM)
     return call(
         inner_kernel,
-        [(x, VMEM) for x in (rows, ids, inner, scale, own)],
-        [(((blocks - 2, size, features), BF16), VMEM), line, ((inner.shape, F32), VMEM), line, line],
-        [VMEM(inner.shape, BF16)],
+        [(x, VMEM) for x in (rows, ids, weights, scale, own)],
+        [(((blocks - 2, size, features), BF16), VMEM), line, (((inner, count), F32), VMEM), line, line],
+        [VMEM((inner, count), BF16)],
         2 * count * features * 4 * size,
     )
 
 
-def run_second(rows, ids, sums, mass, norm, top, total, below, above):
+def run_below(rows, ids, sums, mass, top, total, below):
+    _, size, features = sums.shape
+    count = rows.shape[0]
+    line = (((1, count), F32), VMEM)
+    return call(
+        below_kernel,
+        [(x, VMEM) for x in (rows, ids, sums, mass, top, total, below)],
+        [(((size, features), BF16), VMEM), (((2 * size, count), F32), VMEM), line, line, line],
+        flops=2 * count * features * 2 * size,
+    )
+
+
+def run_above(rows, ids, sums, mass, norm, top, total, shrink, weights, above):
     _, size, features = sums.shape
     count = rows.shape[0]
     line = (((1, count), F32), VMEM)
     one = (((size + MASS_ROWS, features), BF16), VMEM)
     return call(
-        second_kernel,
-        [(x, VMEM) for x in (rows, ids, sums, mass, norm, top, total, below, above)],
-        [(((2, size, features), BF16), VMEM), (((2 * size, count), F32), VMEM), line, line, line, one, one],
+        above_kernel,
+        [(x, VMEM) for x in (rows, ids, sums, mass, norm, top, total, shrink, weights, above)],
+        [(((size, features), BF16), VMEM), (((size, count), F32), VMEM), line, line, line, line, one, one],
         [VMEM((2 * size, count), BF16)],
-        2 * count * features * 6 * size,
-    )
-
-
-def run_own(slots, rows, inner, ratios, outer, scale, edge, fresh, cost):
+        2 * count * features * 4 * size,
+    )
+
+
+def run_own(slots, rows, inner, inner_scale, below, below_scale, above, above_scale, below_edge, above_edge, fresh, cost):
     blocks, size, features = fresh.shape[0] + 2, fresh.shape[1], fresh.shape[2]
     count = rows.shape[0]
+    ins = (rows, inner, inner_scale, below, below_scale, above, above_scale, below_edge, above_edge, fresh, cost)
     return call(
         functools.partial(own_kernel, slots),
-        [(x, VMEM) for x in (rows, inner, ratios, outer, scale, edge, fresh, cost)],
+        [(x, VMEM) for x in ins],
         [
             (((blocks, size, features), BF16), HBM),
             (((2, size, features), F32), VMEM),
@@ -493,12 +564,18 @@
         outgoing.reshape(pairs, lines // pairs // 4, 4, LANES), ("own", "rep"), split_axis=0, concat_axis=0, tiled=True
     ).reshape(lines, LANES)
 
-    rows, inner1, scale1, sums1, mass1, up1, down1 = run_first(pairs, arrived, ids, left, own, right)
+    rows, weights1, top1, total1 = run_arrival(pairs, arrived, ids, own)
+    scale1, sums1, mass1, up1, down1 = run_first(rows, ids, weights1, top1, total1, left, own, right)
     below1, above1 = swap(up1, down1, "own")
-    fresh, norm, inner2, top, total = run_inner(rows, ids, inner1, scale1, own)
-    edge, outer, scale2, ratio2, cost, up2, down2 = run_second(rows, ids, sums1, mass1, norm, top, total, below1, above1)
+    fresh, norm, inner2, top, total = run_inner(rows, ids, weights1, scale1, own)
+    below_edge, below_w, top, total, shrink = run_below(rows, ids, sums1, mass1, top, total, below1)
+    above_edge, above_w, above_by, below_by, inner_by, cost, up2, down2 = run_above(
+        rows, ids, sums1, mass1, norm, top, total, shrink, below_w, above1
+    )
     below2, above2 = swap(up2, down2, "own")
-    given, part, mass2, placed = run_own(per_pair, rows, inner2, ratio2, outer, scale2, edge, fresh, cost)
+    given, part, mass2, placed = run_own(
+        per_pair, rows, inner2, inner_by, below_w, below_by, above_w, above_by, below_edge, above_edge, fresh, cost
+    )
     out = run_last(given, part, mass2, below2, above2)
     return out.reshape(centroids.shape), placed.reshape(count)
 

time: 107 us -> 106 us (level)
  waiting for transfers between devices: 42.4 us -> 41.2 us
    all_to_all x1, waiting for transfers between devices: 1.47 us -> 33 us  [per_device(): lax.all_to_all(outgoing.reshape(pairs, lines // pairs // 4, 4, LANES), ('...]
    ppermute x3, waiting for transfers between devices: 28.4 us -> 1.43 us  [swap(): above = lax.ppermute(down, axis, [(j, i) for i, j in pairs])]
    ppermute x3, waiting for transfers between devices: 12.6 us -> 6.85 us  [swap(): below = lax.ppermute(up, axis, pairs)]
    pallas_call x6 -> x8, Pallas kernels: 13.6 us -> 14.1 us  [call(): pl.pallas_call(kernel, in_specs=[pl.BlockSpec(memory_space=space) for _,...]
  transfers between devices with their start and end apart: 7 -> 7, of which waited for: 7 -> 5; matrix products, arithmetic and copies ran while one was open for 2% -> 2% of each run, Pallas kernels for 3% -> 6%
where the time goes in v4:
time: 106 us
  starting transfers between devices  47.6 us (45%)
  waiting for transfers between devices  41.2 us (39%)
  Pallas kernels  14.1 us (13%)
  local copies, waits for them, and re-layouts  1.73 us (2%)
    all_to_all x1, waiting for transfers between devices, per_device(): lax.all_to_all(outgoing.reshape(pairs, lines // pairs // 4, 4, LANES), ('...  33 us
    all_to_all x1, starting transfers between devices, per_device(): lax.all_to_all(outgoing.reshape(pairs, lines // pairs // 4, 4, LANES), ('...  21.1 us
    ppermute x3, starting transfers between devices, swap(): above = lax.ppermute(down, axis, [(j, i) for i, j in pairs])  18.9 us
    pallas_call x8, Pallas kernels, call(): pl.pallas_call(kernel, in_specs=[pl.BlockSpec(memory_space=space) for _,...  14.1 us
    ppermute x3, starting transfers between devices, swap(): below = lax.ppermute(up, axis, pairs)  7.56 us
    ppermute x3, waiting for transfers between devices, swap(): below = lax.ppermute(up, axis, pairs)  6.85 us
  transfers between devices with their start and end apart: 7, of which 5 were waited for; matrix products, arithmetic and copies ran while one was open for 2% of the time, Pallas kernels for 6%

profile of v4, /device:TPU:8, one launch (start us, length us, event | category | flops | bytes accessed | tf_op | source)
XLA Modules:
  0.0 105.5 jit_solution(13329280818838918959)
XLA Ops:
  0.6 4.2 %shard_map.59 = bf16[6144,128]{1,0:T(8,128)(2,1)} custom-call(s32[1,1024]{1,0:T(1,128)} %bitcast.34, bf16[1024,768]{1,0:T(8,128)(2,1)} %rows_hbm.1), custom_call_target="tpu_custom_call" | custom-call | flops 1610612736 | bytes 1048576 | tf_op jit(solution)/shard_map/pallas_call | solution.py:24
  4.8 0.0 copy-start
  4.8 0.0 copy-start.1
  4.8 21.1 %all-to-all-start = ((bf16[512,3,4,128]{3,2,1,0:T(4,128)(2,1)}), bf16[512,3,4,128]{3,2,1,0:T(4,128)(2,1)S(1)}, u32[]{:S(2)}, u32[]{:S(2)}) async-start(bf16[512,3,4,128]{3,2,1,0:T(4,128)(2,1)} %bitcast.32), calls=%async_computation | async-start | bytes 3145728 | tf_op jit(solution)/shard_map/all_to_all | solution.py:563
  26.0 0.0 copy-done
  26.0 0.7 slice_bitcast_fusion
  26.7 8.2 %collective-permute-start.1 = (bf16[128,768]{1,0:T(8,128)(2,1)}, bf16[128,768]{1,0:T(8,128)(2,1)S(1)}, u32[]{:S(2)}, u32[]{:S(2)}) collective-permute-start(bf16[128,768]{1,0:T(8,128)(2,1)} %get-tuple-element.68), channel_id=1, source_target_pairs={{8,0},{16,8},{24,16},{32,24},{40,32},{48,40},{56,48},{64,56},{72,6... | collective-permute-start | bytes 589832 | tf_op jit(solution)/shard_map/ppermute | solution.py:545
  34.9 1.9 %collective-permute-start = (bf16[128,768]{1,0:T(8,128)(2,1)S(1)}, bf16[128,768]{1,0:T(8,128)(2,1)S(1)}, u32[]{:S(2)}, u32[]{:S(2)}) collective-permute-start(bf16[128,768]{1,0:T(8,128)(2,1)S(1)} %get-tuple-element.69), channel_id=1, source_target_pairs={{0,8},{8,16},{16,24},{24,32},{32,40},{40,48},{48,56},{56,64},{64,7... | collective-permute-start | bytes 589832 | tf_op jit(solution)/shard_map/ppermute | solution.py:544
  36.8 0.0 copy-done.1
  36.8 0.2 copy.9
  37.1 0.2 copy.12
  37.3 33.0 %all-to-all-done = bf16[512,3,4,128]{3,2,1,0:T(4,128)(2,1)S(1)} async-done(((bf16[512,3,4,128]{3,2,1,0:T(4,128)(2,1)}), bf16[512,3,4,128]{3,2,1,0:T(4,128)(2,1)S(1)}, u32[]{:S(2)}, u32[]{:S(2)}) %all-to-all-start) | async-done | bytes 1572896 | tf_op jit(solution)/shard_map/all_to_all | solution.py:563
  70.2 1.8 %shard_map.60 = (bf16[1024,768]{1,0:T(8,128)(2,1)S(1)}, f32[512,1024]{1,0:T(8,128)S(1)}, f32[1,1024]{1,0:T(1,128)S(1)}, f32[1,1024]{1,0:T(1,128)S(1)}) custom-call(bf16[6144,128]{1,0:T(8,128)(2,1)S(1)} %bitcast.25, s32[4,1024]{1,0:T(4,128)S(1)} %bitcast.26, bf16[4,128,768]{2,1,0:T(8,128)(2,1)S(1)} %bitcast.22), custom_call_target="tpu_custom_call" | custom-call | flops 805306368 | bytes 1048576 | tf_op jit(solution)/shard_map/pallas_call | solution.py:24
  72.0 0.0 collective-permute-done.1.right_ref
  72.0 0.0 collective-permute-done.left_ref
  72.0 1.7 %shard_map.61 = (f32[1,1024]{1,0:T(1,128)S(1)}, f32[4,128,768]{2,1,0:T(8,128)S(1)}, f32[512,1]{1,0:T(8,128)S(1)}, bf16[272,768]{1,0:T(8,128)(2,1)S(1)}, bf16[272,768]{1,0:T(8,128)(2,1)S(1)}) custom-call(bf16[1024,768]{1,0:T(8,128)(2,1)S(1)} %get-tuple-element.33.rows_ref, s32[4,1024]{1,0:T(4,128)S(1)} %bitcast.27, ...), custom_call_target="tpu_custom_call" | custom-call | flops 1207959552 | bytes 1048576 | tf_op jit(solution)/shard_map/pallas_call | solution.py:24
  73.8 3.0 %collective-permute-start.2 = (bf16[272,768]{1,0:T(8,128)(2,1)S(1)}, bf16[272,768]{1,0:T(8,128)(2,1)S(1)}, u32[]{:S(2)}, u32[]{:S(2)}) collective-permute-start(bf16[272,768]{1,0:T(8,128)(2,1)S(1)} %get-tuple-element.44), channel_id=1, source_target_pairs={{0,8},{8,16},{16,24},{24,32},{32,40},{40,48},{48,56},{56,64},{64,7... | collective-permute-start | bytes 1253384 | tf_op jit(solution)/shard_map/ppermute | solution.py:544
  76.8 4.9 %collective-permute-start.3 = (bf16[272,768]{1,0:T(8,128)(2,1)S(1)}, bf16[272,768]{1,0:T(8,128)(2,1)S(1)}, u32[]{:S(2)}, u32[]{:S(2)}) collective-permute-start(bf16[272,768]{1,0:T(8,128)(2,1)S(1)} %get-tuple-element.49), channel_id=1, source_target_pairs={{8,0},{16,8},{24,16},{32,24},{40,32},{48,40},{56,48},{64,56},{72,6... | collective-permute-start | bytes 1253384 | tf_op jit(solution)/shard_map/ppermute | solution.py:545
  81.7 1.5 %shard_map.62 = (bf16[2,128,768]{2,1,0:T(8,128)(2,1)S(1)}, f32[1,1024]{1,0:T(1,128)S(1)}, f32[256,1024]{1,0:T(8,128)S(1)}, f32[1,1024]{1,0:T(1,128)S(1)}, f32[1,1024]{1,0:T(1,128)S(1)}) custom-call(bf16[1024,768]{1,0:T(8,128)(2,1)S(1)} %get-tuple-element.33.rows_ref, s32[4,1024]{1,0:T(4,128)S(1)} %bitcast.28, f32[512,1024]{1,0:T(8,128)S(1)} %get-tuple-element.34.weights_ref, ...), custom_call_target="tpu_custom_call" | custom-call | flops 805306368 | bytes 1048576 | tf_op jit(solution)/shard_map/pallas_call | solution.py:24
  83.2 6.4 %collective-permute-done.2.below_ref = bf16[272,768]{1,0:T(8,128)(2,1)S(1)} collective-permute-done((bf16[272,768]{1,0:T(8,128)(2,1)S(1)}, bf16[272,768]{1,0:T(8,128)(2,1)S(1)}, u32[]{:S(2)}, u32[]{:S(2)}) %collective-permute-start.2) | collective-permute-done | bytes 417824 | tf_op jit(solution)/shard_map/ppermute | solution.py:544
  89.6 0.9 shard_map.63
  90.5 0.2 collective-permute-done.3.above_ref
  90.7 1.4 %shard_map.64 = (bf16[128,768]{1,0:T(8,128)(2,1)S(1)}, f32[128,1024]{1,0:T(8,128)S(1)}, f32[1,1024]{1,0:T(1,128)S(1)}, f32[1,1024]{1,0:T(1,128)S(1)}, f32[1,1024...) custom-call(bf16[1024,768]{1,0:T(8,128)(2,1)S(1)} %get-tuple-element.33.rows_r, ...), custom_call_target="tpu_custom_call" | custom-call | flops 805306368 | bytes 1048576 | tf_op jit(solution)/shard_map/pallas_call | solution.py:24
  92.2 2.6 %collective-permute-start.4 = (bf16[144,768]{1,0:T(8,128)(2,1)S(1)}, bf16[144,768]{1,0:T(8,128)(2,1)S(1)}, u32[]{:S(2)}, u32[]{:S(2)}) collective-permute-start(bf16[144,768]{1,0:T(8,128)(2,1)S(1)} %get-tuple-element.61), channel_id=1, source_target_pairs={{0,8},{8,16},{16,24},{24,32},{32,40},{40,48},{48,56},{56,64},{64,7... | collective-permute-start | bytes 663560 | tf_op jit(solution)/shard_map/ppermute | solution.py:544
  94.8 5.8 %collective-permute-start.5 = (bf16[144,768]{1,0:T(8,128)(2,1)S(1)}, bf16[144,768]{1,0:T(8,128)(2,1)S(1)}, u32[]{:S(2)}, u32[]{:S(2)}) collective-permute-start(bf16[144,768]{1,0:T(8,128)(2,1)S(1)} %get-tuple-element.62), channel_id=1, source_target_pairs={{8,0},{16,8},{24,16},{32,24},{40,32},{48,40},{56,48},{64,56},{72,6... | collective-permute-start | bytes 663560 | tf_op jit(solution)/shard_map/ppermute | solution.py:545
  100.6 1.7 %shard_map.65 = (bf16[4,128,768]{2,1,0:T(8,128)(2,1)}, f32[2,128,768]{2,1,0:T(8,128)S(1)}, f32[256,1]{1,0:T(8,128)S(1)}, f32[8,128]{1,0:T(8,128)S(1)}) custom-call(bf16[1024,768]{1,0:T(8,128)(2,1)S(1)} %get-tuple-element.33.rows_ref, f32[256,1024]{1,0:T(8,128)S(1)} %get-tuple-element.38.inner_ref, f32[1,1024]{1,0:T(1,128)S(1)} %get-tuple-element.50.inner_scale_ref, ...), custom_call_target="tpu_custom_call" | custom-call | flops 805306368 | bytes 1048576 | tf_op jit(solution)/shard_map/pallas_call | solution.py:24
  102.3 0.6 copy.15
  102.9 0.5 collective-permute-done.4.below_ref
  103.4 1.2 %collective-permute-done.5.above_ref = bf16[144,768]{1,0:T(8,128)(2,1)S(1)} collective-permute-done((bf16[144,768]{1,0:T(8,128)(2,1)S(1)}, bf16[144,768]{1,0:T(8,128)(2,1)S(1)}, u32[]{:S(2)}, u32[]{:S(2)}) %collective-permute-start.5) | collective-permute-done | bytes 221216 | tf_op jit(solution)/shard_map/ppermute | solution.py:545
  104.5 1.0 shard_map.66
  (1 shorter events, 0.0 us)
Async XLA Ops:
  4.8 21.1 %copy-start = (bf16[4,1,128,768]{3,2,1,0:T(8,128)(2,1)S(1)}, bf16[4,1,128,768]{3,2,1,0:T(8,128)(2,1)}, u32[]{:S(2)}) copy-start(bf16[4,1,128,768]{3,2,1,0:T(8,128)(2,1)} %param.7) | copy-start | bytes 2359300
  4.8 32.0 %copy-start.1 = (s32[1024,4]{0,1:T(4,128)S(1)}, s32[1024,4]{0,1:T(4,128)}, u32[]{:S(2)}) copy-start(s32[1024,4]{0,1:T(4,128)} %param.6) | copy-start | bytes 49156
  4.8 65.4 %all-to-all-start = ((bf16[512,3,4,128]{3,2,1,0:T(4,128)(2,1)}), bf16[512,3,4,128]{3,2,1,0:T(4,128)(2,1)S(1)}, u32[]{:S(2)}, u32[]{:S(2)}) async-start(bf16[512,3,4,128]{3,2,1,0:T(4,128)(2,1)} %bitcast.32), calls=%async_computation | async-start | bytes 3145728 | tf_op jit(solution)/shard_map/all_to_all | solution.py:563
  26.7 45.3 %collective-permute-start.1 = (bf16[128,768]{1,0:T(8,128)(2,1)}, bf16[128,768]{1,0:T(8,128)(2,1)S(1)}, u32[]{:S(2)}, u32[]{:S(2)}) collective-permute-start(bf16[128,768]{1,0:T(8,128)(2,1)} %get-tuple-element.68), channel_id=1, source_target_pairs={{8,0},{16,8},{24,16},{32,24},{40,32},{48,40},{56,48},{64,56},{72,6... | collective-permute-start | bytes 589832 | tf_op jit(solution)/shard_map/ppermute | solution.py:545
  34.9 37.2 %collective-permute-start = (bf16[128,768]{1,0:T(8,128)(2,1)S(1)}, bf16[128,768]{1,0:T(8,128)(2,1)S(1)}, u32[]{:S(2)}, u32[]{:S(2)}) collective-permute-start(bf16[128,768]{1,0:T(8,128)(2,1)S(1)} %get-tuple-element.69), channel_id=1, source_target_pairs={{0,8},{8,16},{16,24},{24,32},{32,40},{40,48},{48,56},{56,64},{64,7... | collective-permute-start | bytes 589832 | tf_op jit(solution)/shard_map/ppermute | solution.py:544
  73.8 15.8 %collective-permute-start.2 = (bf16[272,768]{1,0:T(8,128)(2,1)S(1)}, bf16[272,768]{1,0:T(8,128)(2,1)S(1)}, u32[]{:S(2)}, u32[]{:S(2)}) collective-permute-start(bf16[272,768]{1,0:T(8,128)(2,1)S(1)} %get-tuple-element.44), channel_id=1, source_target_pairs={{0,8},{8,16},{16,24},{24,32},{32,40},{40,48},{48,56},{56,64},{64,7... | collective-permute-start | bytes 1253384 | tf_op jit(solution)/shard_map/ppermute | solution.py:544
  76.8 13.9 %collective-permute-start.3 = (bf16[272,768]{1,0:T(8,128)(2,1)S(1)}, bf16[272,768]{1,0:T(8,128)(2,1)S(1)}, u32[]{:S(2)}, u32[]{:S(2)}) collective-permute-start(bf16[272,768]{1,0:T(8,128)(2,1)S(1)} %get-tuple-element.49), channel_id=1, source_target_pairs={{8,0},{16,8},{24,16},{32,24},{40,32},{48,40},{56,48},{64,56},{72,6... | collective-permute-start | bytes 1253384 | tf_op jit(solution)/shard_map/ppermute | solution.py:545
  92.2 11.2 %collective-permute-start.4 = (bf16[144,768]{1,0:T(8,128)(2,1)S(1)}, bf16[144,768]{1,0:T(8,128)(2,1)S(1)}, u32[]{:S(2)}, u32[]{:S(2)}) collective-permute-start(bf16[144,768]{1,0:T(8,128)(2,1)S(1)} %get-tuple-element.61), channel_id=1, source_target_pairs={{0,8},{8,16},{16,24},{24,32},{32,40},{40,48},{48,56},{56,64},{64,7... | collective-permute-start | bytes 663560 | tf_op jit(solution)/shard_map/ppermute | solution.py:544
  94.8 9.7 %collective-permute-start.5 = (bf16[144,768]{1,0:T(8,128)(2,1)S(1)}, bf16[144,768]{1,0:T(8,128)(2,1)S(1)}, u32[]{:S(2)}, u32[]{:S(2)}) collective-permute-start(bf16[144,768]{1,0:T(8,128)(2,1)S(1)} %get-tuple-element.62), channel_id=1, source_target_pairs={{8,0},{16,8},{24,16},{32,24},{40,32},{48,40},{56,48},{64,56},{72,6... | collective-permute-start | bytes 663560 | tf_op jit(solution)/shard_map/ppermute | solution.py:545

commit v5 on v4

--- a/solution.py
+++ b/solution.py
@@ -144,32 +144,41 @@
 def pack_mass(masses):
     size = masses[0].shape[0]
     eye = diagonal(size)
-    lines = [jnp.sum(jnp.where(eye, m, 0.0), axis=0, keepdims=True) for m in masses]
-    line = jnp.concatenate(lines, axis=1)
-    high = line.astype(BF16).astype(F32)
-    row = lax.broadcasted_iota(jnp.int32, (MASS_ROWS, line.shape[1]), 0)
-    return jnp.where(row == 0, high, jnp.where(row == 1, line - high, 0.0)).astype(BF16)
-
-
-def unpack_mass(packed, which, size):
-    line = packed[:, which * size : (which + 1) * size].astype(F32)
-    line = jnp.sum(line, axis=0, keepdims=True)
+    row = lax.broadcasted_iota(jnp.int32, (MASS_ROWS, size), 0)
+    packed = jnp.zeros((MASS_ROWS, size), F32)
+    for k, mass in enumerate(masses):
+        line = jnp.sum(jnp.where(eye, mass, 0.0), axis=0, keepdims=True)
+        high = line.astype(BF16).astype(F32)
+        packed = jnp.where(row == 2 * k, high, jnp.where(row == 2 * k + 1, line - high, packed))
+    return packed.astype(BF16)
+
+
+def unpack_mass(packed, which):
+    size = packed.shape[1]
+    row = lax.broadcasted_iota(jnp.int32, packed.shape, 0)
+    line = jnp.sum(jnp.where(lax.div(row, 2) == which, packed.astype(F32), 0.0), axis=0, keepdims=True)
     return jnp.sum(jnp.where(diagonal(size), line, 0.0), axis=1, keepdims=True)
 
 
 def package(pkg_ref, sums, masses):
-    size = masses[0].shape[0]
+    size, features = sums[0].shape
     blocks = len(sums)
-    for k in range(blocks):
-        pkg_ref[k * size : (k + 1) * size, :] = sums[k].astype(BF16)
-    packed = pack_mass(masses)
-    pkg_ref[blocks * size :, : blocks * size] = packed
-    rest = pkg_ref.shape[1] - blocks * size
-    pkg_ref[blocks * size :, blocks * size :] = jnp.zeros((MASS_ROWS, rest), BF16)
-
-
-def refresh(total, tally, previous):
-    return ((total + PRIOR * previous.astype(F32)) / (tally + PRIOR)).astype(BF16)
+    for f in range(features // LANES):
+        for k in range(blocks):
+            first = (f * blocks + k) * size
+            pkg_ref[first : first + size, :] = sums[k][:, f * LANES : (f + 1) * LANES].astype(BF16)
+    pkg_ref[blocks * size * (features // LANES) :, :] = pack_mass(masses)
+
+
+def unpack(pkg_ref, which, blocks, size):
+    chunks = (pkg_ref.shape[0] - MASS_ROWS) // (blocks * size)
+    firsts = [(f * blocks + which) * size for f in range(chunks)]
+    sums = jnp.concatenate([pkg_ref[first : first + size, :] for first in firsts], axis=1)
+    return sums.astype(F32), unpack_mass(pkg_ref[blocks * size * chunks :, :], which)
+
+
+def package_lines(blocks, size, features):
+    return (((blocks * size * (features // LANES) + MASS_ROWS, LANES), BF16), VMEM)
 
 
 def arrival_kernel(
@@ -277,12 +286,10 @@
 
 
 def renewed(pkg_ref, sums, masses):
-    size = sums[0].shape[0]
-    packed = pkg_ref[2 * size :, : 2 * size]
     new = []
     for k in range(2):
-        total = sums[k] + pkg_ref[k * size : (k + 1) * size, :].astype(F32)
-        new.append(ratio(total, masses[k] + unpack_mass(packed, k, size)))
+        more, tally = unpack(pkg_ref, k, 2, sums[k].shape[0])
+        new.append(ratio(sums[k] + more, masses[k] + tally))
     return new
 
 
@@ -411,9 +418,8 @@
     blocks, size, _ = out_hbm.shape
     stores = []
     for e, (k, pkg) in enumerate(((0, below_ref), (blocks - 1, above_ref))):
-        total = part_ref[e] + pkg[:size, :].astype(F32)
-        tally = mass_ref[e * size : (e + 1) * size, :] + unpack_mass(pkg[size:, :size], 0, size)
-        done_ref[e] = ratio(total, tally)
+        more, tally = unpack(pkg, 0, 1, size)
+        done_ref[e] = ratio(part_ref[e] + more, mass_ref[e * size : (e + 1) * size, :] + tally)
         stores.append(pltpu.make_async_copy(done_ref.at[e], out_hbm.at[k], sems.at[e]))
         stores[-1].start()
     for store in stores:
@@ -460,7 +466,7 @@
 def run_first(rows, ids, weights, top, total, left, own, right):
     blocks, size, features = own.shape
     count = rows.shape[0]
-    two = (((2 * size + MASS_ROWS, features), BF16), VMEM)
+    two = package_lines(2, size, features)
     return call(
         first_kernel,
         [(x, VMEM) for x in (rows, ids, weights, top, total, left, own, right)],
@@ -500,7 +506,7 @@
     _, size, features = sums.shape
     count = rows.shape[0]
     line = (((1, count), F32), VMEM)
-    one = (((size + MASS_ROWS, features), BF16), VMEM)
+    one = package_lines(1, size, features)
     return call(
         above_kernel,
         [(x, VMEM) for x in (rows, ids, sums, mass, norm, top, total, shrink, weights, above)],

time: 106 us -> 105 us (level)
  no operation moved by 1% of the time
where the time goes in v5:
time: 105 us
  starting transfers between devices  47.6 us (45%)
  waiting for transfers between devices  40.3 us (38%)
  Pallas kernels  14.2 us (14%)
  local copies, waits for them, and re-layouts  1.73 us (2%)
    all_to_all x1, waiting for transfers between devices, per_device(): lax.all_to_all(outgoing.reshape(pairs, lines // pairs // 4, 4, LANES), ('...  33 us
    all_to_all x1, starting transfers between devices, per_device(): lax.all_to_all(outgoing.reshape(pairs, lines // pairs // 4, 4, LANES), ('...  21.1 us
    ppermute x3, starting transfers between devices, swap(): above = lax.ppermute(down, axis, [(j, i) for i, j in pairs])  18.9 us
    pallas_call x8, Pallas kernels, call(): pl.pallas_call(kernel, in_specs=[pl.BlockSpec(memory_space=space) for _,...  14.2 us
    ppermute x3, starting transfers between devices, swap(): below = lax.ppermute(up, axis, pairs)  7.56 us
    ppermute x3, waiting for transfers between devices, swap(): below = lax.ppermute(up, axis, pairs)  5.97 us
  transfers between devices with their start and end apart: 7, of which 5 were waited for; matrix products, arithmetic and copies ran while one was open for 2% of the time, Pallas kernels for 6%

profile of v5, /device:TPU:8, one launch (start us, length us, event | category | flops | bytes accessed | tf_op | source)
XLA Modules:
  0.0 104.7 jit_solution(9850024161231631807)
XLA Ops:
  0.6 4.2 %shard_map.59 = bf16[6144,128]{1,0:T(8,128)(2,1)} custom-call(s32[1,1024]{1,0:T(1,128)} %bitcast.34, bf16[1024,768]{1,0:T(8,128)(2,1)} %rows_hbm.1), custom_call_target="tpu_custom_call" | custom-call | flops 1610612736 | bytes 1048576 | tf_op jit(solution)/shard_map/pallas_call | solution.py:24
  4.8 0.0 copy-start
  4.8 0.0 copy-start.1
  4.8 21.1 %all-to-all-start = ((bf16[512,3,4,128]{3,2,1,0:T(4,128)(2,1)}), bf16[512,3,4,128]{3,2,1,0:T(4,128)(2,1)S(1)}, u32[]{:S(2)}, u32[]{:S(2)}) async-start(bf16[512,3,4,128]{3,2,1,0:T(4,128)(2,1)} %bitcast.32), calls=%async_computation | async-start | bytes 3145728 | tf_op jit(solution)/shard_map/all_to_all | solution.py:569
  26.0 0.0 copy-done
  26.0 0.7 slice_bitcast_fusion
  26.7 8.2 %collective-permute-start.1 = (bf16[128,768]{1,0:T(8,128)(2,1)}, bf16[128,768]{1,0:T(8,128)(2,1)S(1)}, u32[]{:S(2)}, u32[]{:S(2)}) collective-permute-start(bf16[128,768]{1,0:T(8,128)(2,1)} %get-tuple-element.68), channel_id=1, source_target_pairs={{8,0},{16,8},{24,16},{32,24},{40,32},{48,40},{56,48},{64,56},{72,6... | collective-permute-start | bytes 589832 | tf_op jit(solution)/shard_map/ppermute | solution.py:551
  34.9 1.9 %collective-permute-start = (bf16[128,768]{1,0:T(8,128)(2,1)S(1)}, bf16[128,768]{1,0:T(8,128)(2,1)S(1)}, u32[]{:S(2)}, u32[]{:S(2)}) collective-permute-start(bf16[128,768]{1,0:T(8,128)(2,1)S(1)} %get-tuple-element.69), channel_id=1, source_target_pairs={{0,8},{8,16},{16,24},{24,32},{32,40},{40,48},{48,56},{56,64},{64,7... | collective-permute-start | bytes 589832 | tf_op jit(solution)/shard_map/ppermute | solution.py:550
  36.8 0.0 copy-done.1
  36.8 0.2 copy.9
  37.1 0.2 copy.12
  37.3 33.0 %all-to-all-done = bf16[512,3,4,128]{3,2,1,0:T(4,128)(2,1)S(1)} async-done(((bf16[512,3,4,128]{3,2,1,0:T(4,128)(2,1)}), bf16[512,3,4,128]{3,2,1,0:T(4,128)(2,1)S(1)}, u32[]{:S(2)}, u32[]{:S(2)}) %all-to-all-start) | async-done | bytes 1572896 | tf_op jit(solution)/shard_map/all_to_all | solution.py:569
  70.2 1.8 %shard_map.60 = (bf16[1024,768]{1,0:T(8,128)(2,1)S(1)}, f32[512,1024]{1,0:T(8,128)S(1)}, f32[1,1024]{1,0:T(1,128)S(1)}, f32[1,1024]{1,0:T(1,128)S(1)}) custom-call(bf16[6144,128]{1,0:T(8,128)(2,1)S(1)} %bitcast.25, s32[4,1024]{1,0:T(4,128)S(1)} %bitcast.26, bf16[4,128,768]{2,1,0:T(8,128)(2,1)S(1)} %bitcast.22), custom_call_target="tpu_custom_call" | custom-call | flops 805306368 | bytes 1048576 | tf_op jit(solution)/shard_map/pallas_call | solution.py:24
  72.0 0.0 collective-permute-done.1.right_ref
  72.0 0.0 collective-permute-done.left_ref
  72.0 1.8 %shard_map.61 = (f32[1,1024]{1,0:T(1,128)S(1)}, f32[4,128,768]{2,1,0:T(8,128)S(1)}, f32[512,1]{1,0:T(8,128)S(1)}, bf16[1552,128]{1,0:T(8,128)(2,1)S(1)}, bf16[1552,128]{1,0:T(8,128)(2,1)S(1)}) custom-call(bf16[1024,768]{1,0:T(8,128)(2,1)S(1)} %get-tuple-element.33.rows_ref, s32[4,1024]{1,0:T(4,128)S(1)} %bitcast.27, ...), custom_call_target="tpu_custom_call" | custom-call | flops 1207959552 | bytes 1048576 | tf_op jit(solution)/shard_map/pallas_call | solution.py:24
  73.8 3.0 %collective-permute-start.2 = (bf16[1552,128]{1,0:T(8,128)(2,1)S(1)}, bf16[1552,128]{1,0:T(8,128)(2,1)S(1)}, u32[]{:S(2)}, u32[]{:S(2)}) collective-permute-start(bf16[1552,128]{1,0:T(8,128)(2,1)S(1)} %get-tuple-element.44), channel_id=1, source_target_pairs={{0,8},{8,16},{16,24},{24,32},{32,40},{40,48},{48,56},{56,64},{64,7... | collective-permute-start | bytes 1191944 | tf_op jit(solution)/shard_map/ppermute | solution.py:550
  76.8 4.9 %collective-permute-start.3 = (bf16[1552,128]{1,0:T(8,128)(2,1)S(1)}, bf16[1552,128]{1,0:T(8,128)(2,1)S(1)}, u32[]{:S(2)}, u32[]{:S(2)}) collective-permute-start(bf16[1552,128]{1,0:T(8,128)(2,1)S(1)} %get-tuple-element.49), channel_id=1, source_target_pairs={{8,0},{16,8},{24,16},{32,24},{40,32},{48,40},{56,48},{64,56},{72,6... | collective-permute-start | bytes 1191944 | tf_op jit(solution)/shard_map/ppermute | solution.py:551
  81.7 1.5 %shard_map.62 = (bf16[2,128,768]{2,1,0:T(8,128)(2,1)S(1)}, f32[1,1024]{1,0:T(1,128)S(1)}, f32[256,1024]{1,0:T(8,128)S(1)}, f32[1,1024]{1,0:T(1,128)S(1)}, f32[1,1024]{1,0:T(1,128)S(1)}) custom-call(bf16[1024,768]{1,0:T(8,128)(2,1)S(1)} %get-tuple-element.33.rows_ref, s32[4,1024]{1,0:T(4,128)S(1)} %bitcast.28, f32[512,1024]{1,0:T(8,128)S(1)} %get-tuple-element.34.weights_ref, ...), custom_call_target="tpu_custom_call" | custom-call | flops 805306368 | bytes 1048576 | tf_op jit(solution)/shard_map/pallas_call | solution.py:24
  83.2 5.9 %collective-permute-done.2.below_ref = bf16[1552,128]{1,0:T(8,128)(2,1)S(1)} collective-permute-done((bf16[1552,128]{1,0:T(8,128)(2,1)S(1)}, bf16[1552,128]{1,0:T(8,128)(2,1)S(1)}, u32[]{:S(2)}, u32[]{:S(2)}) %collective-permute-start.2) | collective-permute-done | bytes 397344 | tf_op jit(solution)/shard_map/ppermute | solution.py:550
  89.1 1.0 shard_map.63
  90.1 0.2 collective-permute-done.3.above_ref
  90.3 1.5 %shard_map.64 = (bf16[128,768]{1,0:T(8,128)(2,1)S(1)}, f32[128,1024]{1,0:T(8,128)S(1)}, f32[1,1024]{1,0:T(1,128)S(1)}, f32[1,1024]{1,0:T(1,128)S(1)}, f32[1,1024...) custom-call(bf16[1024,768]{1,0:T(8,128)(2,1)S(1)} %get-tuple-element.33.rows_r, ...), custom_call_target="tpu_custom_call" | custom-call | flops 805306368 | bytes 1048576 | tf_op jit(solution)/shard_map/pallas_call | solution.py:24
  91.8 2.6 %collective-permute-start.4 = (bf16[784,128]{1,0:T(8,128)(2,1)S(1)}, bf16[784,128]{1,0:T(8,128)(2,1)S(1)}, u32[]{:S(2)}, u32[]{:S(2)}) collective-permute-start(bf16[784,128]{1,0:T(8,128)(2,1)S(1)} %get-tuple-element.61), channel_id=1, source_target_pairs={{0,8},{8,16},{16,24},{24,32},{32,40},{40,48},{48,56},{56,64},{64,7... | collective-permute-start | bytes 602120 | tf_op jit(solution)/shard_map/ppermute | solution.py:550
  94.4 5.8 %collective-permute-start.5 = (bf16[784,128]{1,0:T(8,128)(2,1)S(1)}, bf16[784,128]{1,0:T(8,128)(2,1)S(1)}, u32[]{:S(2)}, u32[]{:S(2)}) collective-permute-start(bf16[784,128]{1,0:T(8,128)(2,1)S(1)} %get-tuple-element.62), channel_id=1, source_target_pairs={{8,0},{16,8},{24,16},{32,24},{40,32},{48,40},{56,48},{64,56},{72,6... | collective-permute-start | bytes 602120 | tf_op jit(solution)/shard_map/ppermute | solution.py:551
  100.2 1.6 %shard_map.65 = (bf16[4,128,768]{2,1,0:T(8,128)(2,1)}, f32[2,128,768]{2,1,0:T(8,128)S(1)}, f32[256,1]{1,0:T(8,128)S(1)}, f32[8,128]{1,0:T(8,128)S(1)}) custom-call(bf16[1024,768]{1,0:T(8,128)(2,1)S(1)} %get-tuple-element.33.rows_ref, f32[256,1024]{1,0:T(8,128)S(1)} %get-tuple-element.38.inner_ref, f32[1,1024]{1,0:T(1,128)S(1)} %get-tuple-element.50.inner_scale_ref, ...), custom_call_target="tpu_custom_call" | custom-call | flops 805306368 | bytes 1048576 | tf_op jit(solution)/shard_map/pallas_call | solution.py:24
  101.9 0.6 copy.15
  102.5 0.1 collective-permute-done.4.below_ref
  102.5 1.2 %collective-permute-done.5.above_ref = bf16[784,128]{1,0:T(8,128)(2,1)S(1)} collective-permute-done((bf16[784,128]{1,0:T(8,128)(2,1)S(1)}, bf16[784,128]{1,0:T(8,128)(2,1)S(1)}, u32[]{:S(2)}, u32[]{:S(2)}) %collective-permute-start.5) | collective-permute-done | bytes 200736 | tf_op jit(solution)/shard_map/ppermute | solution.py:551
  103.7 1.0 shard_map.66
  (1 shorter events, 0.0 us)
Async XLA Ops:
  4.8 21.1 %copy-start = (bf16[4,1,128,768]{3,2,1,0:T(8,128)(2,1)S(1)}, bf16[4,1,128,768]{3,2,1,0:T(8,128)(2,1)}, u32[]{:S(2)}) copy-start(bf16[4,1,128,768]{3,2,1,0:T(8,128)(2,1)} %param.7) | copy-start | bytes 2359300
  4.8 32.0 %copy-start.1 = (s32[1024,4]{0,1:T(4,128)S(1)}, s32[1024,4]{0,1:T(4,128)}, u32[]{:S(2)}) copy-start(s32[1024,4]{0,1:T(4,128)} %param.6) | copy-start | bytes 49156
  4.8 65.4 %all-to-all-start = ((bf16[512,3,4,128]{3,2,1,0:T(4,128)(2,1)}), bf16[512,3,4,128]{3,2,1,0:T(4,128)(2,1)S(1)}, u32[]{:S(2)}, u32[]{:S(2)}) async-start(bf16[512,3,4,128]{3,2,1,0:T(4,128)(2,1)} %bitcast.32), calls=%async_computation | async-start | bytes 3145728 | tf_op jit(solution)/shard_map/all_to_all | solution.py:569
  26.7 45.3 %collective-permute-start.1 = (bf16[128,768]{1,0:T(8,128)(2,1)}, bf16[128,768]{1,0:T(8,128)(2,1)S(1)}, u32[]{:S(2)}, u32[]{:S(2)}) collective-permute-start(bf16[128,768]{1,0:T(8,128)(2,1)} %get-tuple-element.68), channel_id=1, source_target_pairs={{8,0},{16,8},{24,16},{32,24},{40,32},{48,40},{56,48},{64,56},{72,6... | collective-permute-start | bytes 589832 | tf_op jit(solution)/shard_map/ppermute | solution.py:551
  34.9 37.1 %collective-permute-start = (bf16[128,768]{1,0:T(8,128)(2,1)S(1)}, bf16[128,768]{1,0:T(8,128)(2,1)S(1)}, u32[]{:S(2)}, u32[]{:S(2)}) collective-permute-start(bf16[128,768]{1,0:T(8,128)(2,1)S(1)} %get-tuple-element.69), channel_id=1, source_target_pairs={{0,8},{8,16},{16,24},{24,32},{32,40},{40,48},{48,56},{56,64},{64,7... | collective-permute-start | bytes 589832 | tf_op jit(solution)/shard_map/ppermute | solution.py:550
  73.8 15.3 %collective-permute-start.2 = (bf16[1552,128]{1,0:T(8,128)(2,1)S(1)}, bf16[1552,128]{1,0:T(8,128)(2,1)S(1)}, u32[]{:S(2)}, u32[]{:S(2)}) collective-permute-start(bf16[1552,128]{1,0:T(8,128)(2,1)S(1)} %get-tuple-element.44), channel_id=1, source_target_pairs={{0,8},{8,16},{16,24},{24,32},{32,40},{40,48},{48,56},{56,64},{64,7... | collective-permute-start | bytes 1191944 | tf_op jit(solution)/shard_map/ppermute | solution.py:550
  76.8 13.5 %collective-permute-start.3 = (bf16[1552,128]{1,0:T(8,128)(2,1)S(1)}, bf16[1552,128]{1,0:T(8,128)(2,1)S(1)}, u32[]{:S(2)}, u32[]{:S(2)}) collective-permute-start(bf16[1552,128]{1,0:T(8,128)(2,1)S(1)} %get-tuple-element.49), channel_id=1, source_target_pairs={{8,0},{16,8},{24,16},{32,24},{40,32},{48,40},{56,48},{64,56},{72,6... | collective-permute-start | bytes 1191944 | tf_op jit(solution)/shard_map/ppermute | solution.py:551
  91.8 10.8 %collective-permute-start.4 = (bf16[784,128]{1,0:T(8,128)(2,1)S(1)}, bf16[784,128]{1,0:T(8,128)(2,1)S(1)}, u32[]{:S(2)}, u32[]{:S(2)}) collective-permute-start(bf16[784,128]{1,0:T(8,128)(2,1)S(1)} %get-tuple-element.61), channel_id=1, source_target_pairs={{0,8},{8,16},{16,24},{24,32},{32,40},{40,48},{48,56},{56,64},{64,7... | collective-permute-start | bytes 602120 | tf_op jit(solution)/shard_map/ppermute | solution.py:550
  94.4 9.3 %collective-permute-start.5 = (bf16[784,128]{1,0:T(8,128)(2,1)S(1)}, bf16[784,128]{1,0:T(8,128)(2,1)S(1)}, u32[]{:S(2)}, u32[]{:S(2)}) collective-permute-start(bf16[784,128]{1,0:T(8,128)(2,1)S(1)} %get-tuple-element.62), channel_id=1, source_target_pairs={{8,0},{16,8},{24,16},{32,24},{40,32},{48,40},{56,48},{64,56},{72,6... | collective-permute-start | bytes 602120 | tf_op jit(solution)/shard_map/ppermute | solution.py:551

commit v6 on v5

--- a/solution.py
+++ b/solution.py
@@ -100,20 +100,20 @@
                 rows_ref[pl.ds(slot * pairs + part * step, step), f * LANES : (f + 1) * LANES] = got.astype(BF16)
 
 
-STEP = 256
+STEP = 512
 
 
 def half_scale(features):
     return 0.5 * LOG2E / math.sqrt(features)
 
 
-def scored(flat, biases, slots, rows, ids):
+def scored(flat, biases, slots, rows, hits):
     cross = matmul(flat, rows, ((1,), (1,)))
     size = flat.shape[0] // len(slots)
     factor = 2.0 * half_scale(flat.shape[1])
     scores = []
     for k, w in enumerate(slots):
-        hit = jnp.max(jnp.where(ids == w, 0.0, -jnp.inf), axis=0, keepdims=True)
+        hit = hits[w : w + 1, :]
         scores.append(cross[k * size : (k + 1) * size] * factor + (hit - biases[k]))
     return scores
 
@@ -181,17 +181,27 @@
     return (((blocks * size * (features // LANES) + MASS_ROWS, LANES), BF16), VMEM)
 
 
+def prepare_kernel(ids_ref, own_ref, hits_ref, bias_ref):
+    ids = ids_ref[...]
+    hits_ref[...] = jnp.full(hits_ref.shape, -jnp.inf, F32)
+    blocks, size, _ = own_ref.shape
+    for w in range(blocks + 2):
+        hits_ref[w : w + 1, :] = jnp.max(jnp.where(ids == w, 0.0, -jnp.inf), axis=0, keepdims=True)
+    for k, bias in enumerate(square_biases([own_ref[k] for k in range(blocks)])):
+        bias_ref[k * size : (k + 1) * size, :] = bias
+
+
 def arrival_kernel(
-    pairs, lines_ref, ids_ref, own_ref, rows_ref, weights_ref, top_ref, total_ref, wide
+    pairs, lines_ref, hits_ref, own_ref, bias_ref, rows_ref, weights_ref, top_ref, total_ref, wide
 ):
     blocks, size, _ = own_ref.shape
     own = [own_ref[k] for k in range(blocks)]
-    biases = square_biases(own)
+    biases = [bias_ref[k * size : (k + 1) * size, :] for k in range(blocks)]
     flat = jnp.concatenate(own, axis=0)
     unpack_rows(lines_ref, rows_ref, wide, pairs)
     for start in range(0, rows_ref.shape[0], STEP):
         here = slice(start, start + STEP)
-        scores = scored(flat, biases, range(1, blocks + 1), rows_ref[here, :], ids_ref[:, here])
+        scores = scored(flat, biases, range(1, blocks + 1), rows_ref[here, :], hits_ref[:, here])
         top = highest(scores)
         top_ref[:, here] = top
         weights = [jnp.exp2(score - top) for score in scores]
@@ -201,7 +211,7 @@
 
 
 def first_kernel(
-    rows_ref, ids_ref, weights_ref, top_ref, total_ref, left_ref, own_ref, right_ref,
+    rows_ref, hits_ref, weights_ref, top_ref, total_ref, left_ref, own_ref, right_ref,
     scale_ref, sums_ref, mass_ref, up_ref, down_ref, resp_ref,
 ):
     count_own, size, _ = own_ref.shape
@@ -213,7 +223,7 @@
     mass = [0.0] * len(edges)
     for start in range(0, rows_ref.shape[0], STEP):
         here = slice(start, start + STEP)
-        scores = scored(flat, biases, (0, last), rows_ref[here, :], ids_ref[:, here])
+        scores = scored(flat, biases, (0, last), rows_ref[here, :], hits_ref[:, here])
         top = jnp.maximum(highest(scores), top_ref[:, here])
         shrink = jnp.exp2(top_ref[:, here] - top)
         weights = [jnp.exp2(score - top) for score in scores]
@@ -246,7 +256,7 @@
 
 
 def inner_kernel(
-    rows_ref, ids_ref, weights_ref, scale_ref, own_ref, fresh_ref, norm_ref, next_ref, top_ref, total_ref, resp_ref
+    rows_ref, hits_ref, weights_ref, scale_ref, own_ref, fresh_ref, norm_ref, next_ref, top_ref, total_ref, resp_ref
 ):
     blocks, size, _ = own_ref.shape
     inner = blocks - 2
@@ -270,7 +280,7 @@
     flat = jnp.concatenate(new, axis=0)
     for start in range(0, count, STEP):
         here = slice(start, start + STEP)
-        scores = scored(flat, biases, range(2, inner + 2), rows_ref[here, :], ids_ref[:, here])
+        scores = scored(flat, biases, range(2, inner + 2), rows_ref[here, :], hits_ref[:, here])
         top = highest(scores)
         top_ref[:, here] = top
         safe = jnp.where(top == -jnp.inf, 0.0, top)
@@ -294,7 +304,7 @@
 
 
 def below_kernel(
-    rows_ref, ids_ref, sums_ref, mass_ref, top_ref, total_ref, below_ref,
+    rows_ref, hits_ref, sums_ref, mass_ref, top_ref, total_ref, below_ref,
     edge_ref, weights_ref, new_top_ref, new_total_ref, shrink_ref,
 ):
     size = sums_ref.shape[1]
@@ -304,7 +314,7 @@
     flat = jnp.concatenate(new, axis=0)
     for start in range(0, rows_ref.shape[0], STEP):
         here = slice(start, start + STEP)
-        scores = scored(flat, biases, (0, 1), rows_ref[here, :], ids_ref[:, here])
+        scores = scored(flat, biases, (0, 1), rows_ref[here, :], hits_ref[:, here])
         before = top_ref[:, here]
         top = jnp.maximum(highest(scores), before)
         safe = jnp.where(top == -jnp.inf, 0.0, top)
@@ -318,7 +328,7 @@
 
 
 def above_kernel(
-    rows_ref, ids_ref, sums_ref, mass_ref, norm_ref, top_ref, total_ref, shrink_ref, weights_ref, above_ref,
+    rows_ref, hits_ref, sums_ref, mass_ref, norm_ref, top_ref, total_ref, shrink_ref, weights_ref, above_ref,
     edge_ref, outer_ref, above_scale_ref, below_scale_ref, inner_scale_ref, cost_ref, up_ref, down_ref, resp_ref,
 ):
     size = sums_ref.shape[1]
@@ -333,7 +343,7 @@
     half = 0.5 / math.sqrt(rows_ref.shape[1])
     for start in range(0, rows_ref.shape[0], STEP):
         here = slice(start, start + STEP)
-        scores = scored(flat, biases, (last - 1, last), rows_ref[here, :], ids_ref[:, here])
+        scores = scored(flat, biases, (last - 1, last), rows_ref[here, :], hits_ref[:, here])
         before = top_ref[:, here]
         top = jnp.maximum(highest(scores), before)
         fade = jnp.exp2(before - top)
@@ -383,7 +393,7 @@
 def own_kernel(
     slots, rows_ref, inner_ref, inner_scale_ref, below_ref, below_scale_ref, above_ref, above_scale_ref,
     below_edge_ref, above_edge_ref, fresh_ref, cost_ref,
-    out_hbm, part_ref, mass_ref, placed_ref, done_ref, resp_ref, sem,
+    out_hbm, part_ref, mass_ref, placed_hbm, done_ref, resp_ref, placed_ref, sems,
 ):
     inner, size, _ = fresh_ref.shape
     rows = rows_ref[...]
@@ -404,14 +414,17 @@
     sums, mass = summed([(inner_ref, k * size, inner_scale_ref) for k in range(inner)])
     for k in range(inner):
         done_ref[k] = ratio(sums[k] + PRIOR * fresh_ref[k].astype(F32), mass[k] + PRIOR)
-    store = pltpu.make_async_copy(done_ref, out_hbm.at[pl.ds(1, inner)], sem)
+    store = pltpu.make_async_copy(done_ref, out_hbm.at[pl.ds(1, inner)], sems.at[0])
     store.start()
+    interleave(cost_ref, placed_ref, slots)
+    place = pltpu.make_async_copy(placed_ref, placed_hbm, sems.at[1])
+    place.start()
     sums, mass = summed([(below_ref, size, below_scale_ref), (above_ref, 0, above_scale_ref)])
     for k, edge_ref in enumerate((below_edge_ref, above_edge_ref)):
         part_ref[k] = sums[k] + PRIOR * edge_ref[...].astype(F32)
         mass_ref[k * size : (k + 1) * size, :] = mass[k] + PRIOR
-    interleave(cost_ref, placed_ref, slots)
     store.wait()
+    place.wait()
 
 
 def last_kernel(given_hbm, part_ref, mass_ref, below_ref, above_ref, out_hbm, done_ref, sems):
@@ -450,13 +463,19 @@
     )
 
 
-def run_arrival(pairs, arrived, ids, own):
+def run_prepare(ids, own):
+    blocks, size, _ = own.shape
+    outs = [(((8, ids.shape[1]), F32), VMEM), (((blocks * size, 1), F32), VMEM)]
+    return call(prepare_kernel, [(ids, VMEM), (own, VMEM)], outs)
+
+
+def run_arrival(pairs, arrived, ids, own, bias):
     lines, count = arrived.shape[0], ids.shape[1]
     blocks, size, features = own.shape
     line = (((1, count), F32), VMEM)
     return call(
         functools.partial(arrival_kernel, pairs),
-        [(arrived, VMEM), (ids, VMEM), (own, VMEM)],
+        [(arrived, VMEM), (ids, VMEM), (own, VMEM), (bias, VMEM)],
         [(((count, features), BF16), VMEM), (((blocks * size, count), F32), VMEM), line, line],
         [wide_lines(lines, lines // pairs)],
         2 * count * features * blocks * size,
@@ -527,9 +546,14 @@
             (((blocks, size, features), BF16), HBM),
             (((2, size, features), F32), VMEM),
             (((2 * size, 1), F32), VMEM),
-            (((count // LANES, LANES), F32), VMEM),
+            (((count // LANES, LANES), F32), HBM),
         ],
-        [VMEM((blocks - 2, size, features), BF16), VMEM((2 * size, count), BF16), pltpu.SemaphoreType.DMA],
+        [
+            VMEM((blocks - 2, size, features), BF16),
+            VMEM((2 * size, count), BF16),
+            VMEM((count // LANES, LANES), F32),
+            pltpu.SemaphoreType.DMA((2,)),
+        ],
         2 * count * features * blocks * size,
     )
 
@@ -570,7 +594,8 @@
         outgoing.reshape(pairs, lines // pairs // 4, 4, LANES), ("own", "rep"), split_axis=0, concat_axis=0, tiled=True
     ).reshape(lines, LANES)
 
-    rows, weights1, top1, total1 = run_arrival(pairs, arrived, ids, own)
+    ids, bias = run_prepare(ids, own)
+    rows, weights1, top1, total1 = run_arrival(pairs, arrived, ids, own, bias)
     scale1, sums1, mass1, up1, down1 = run_first(rows, ids, weights1, top1, total1, left, own, right)
     below1, above1 = swap(up1, down1, "own")
     fresh, norm, inner2, top, total = run_inner(rows, ids, weights1, scale1, own)

time: 105 us -> 105 us (level)
    pallas_call x8 -> x9, Pallas kernels: 14.2 us -> 14.6 us  [call(): pl.pallas_call(kernel, in_specs=[pl.BlockSpec(memory_space=space) for _,...]
  transfers between devices with their start and end apart: 7 -> 7, of which waited for: 5 -> 5; matrix products, arithmetic and copies ran while one was open for 2% -> 1% of each run, Pallas kernels for 6% -> 6%
where the time goes in v6:
time: 105 us
  starting transfers between devices  47.6 us (45%)
  waiting for transfers between devices  40.6 us (39%)
  Pallas kernels  14.6 us (14%)
  local copies, waits for them, and re-layouts  1.14 us (1%)
    all_to_all x1, waiting for transfers between devices, per_device(): lax.all_to_all(outgoing.reshape(pairs, lines // pairs // 4, 4, LANES), ('...  32.7 us
    all_to_all x1, starting transfers between devices, per_device(): lax.all_to_all(outgoing.reshape(pairs, lines // pairs // 4, 4, LANES), ('...  21.1 us
    ppermute x3, starting transfers between devices, swap(): above = lax.ppermute(down, axis, [(j, i) for i, j in pairs])  18.9 us
    pallas_call x9, Pallas kernels, call(): pl.pallas_call(kernel, in_specs=[pl.BlockSpec(memory_space=space) for _,...  14.6 us
    ppermute x3, starting transfers between devices, swap(): below = lax.ppermute(up, axis, pairs)  7.56 us
    ppermute x3, waiting for transfers between devices, swap(): below = lax.ppermute(up, axis, pairs)  6.49 us
  transfers between devices with their start and end apart: 7, of which 5 were waited for; matrix products, arithmetic and copies ran while one was open for 1% of the time, Pallas kernels for 6%

profile of v6, /device:TPU:8, one launch (start us, length us, event | category | flops | bytes accessed | tf_op | source)
XLA Modules:
  0.0 104.7 jit_solution(4070360752978299189)
XLA Ops:
  0.6 4.2 %shard_map.59 = bf16[6144,128]{1,0:T(8,128)(2,1)} custom-call(s32[1,1024]{1,0:T(1,128)} %bitcast.30, bf16[1024,768]{1,0:T(8,128)(2,1)} %rows_hbm.1), custom_call_target="tpu_custom_call" | custom-call | flops 1610612736 | bytes 1048576 | tf_op jit(solution)/shard_map/pallas_call | solution.py:24
  4.8 0.0 copy-start
  4.8 0.0 copy-start.1
  4.8 21.1 %all-to-all-start = ((bf16[512,3,4,128]{3,2,1,0:T(4,128)(2,1)}), bf16[512,3,4,128]{3,2,1,0:T(4,128)(2,1)S(1)}, u32[]{:S(2)}, u32[]{:S(2)}) async-start(bf16[512,3,4,128]{3,2,1,0:T(4,128)(2,1)} %bitcast.28), calls=%async_computation | async-start | bytes 3145728 | tf_op jit(solution)/shard_map/all_to_all | solution.py:593
  25.9 0.0 copy-done
  25.9 0.7 slice_bitcast_fusion
  26.7 8.2 %collective-permute-start.1 = (bf16[128,768]{1,0:T(8,128)(2,1)}, bf16[128,768]{1,0:T(8,128)(2,1)S(1)}, u32[]{:S(2)}, u32[]{:S(2)}) collective-permute-start(bf16[128,768]{1,0:T(8,128)(2,1)} %get-tuple-element.72), channel_id=1, source_target_pairs={{8,0},{16,8},{24,16},{32,24},{40,32},{48,40},{56,48},{64,56},{72,6... | collective-permute-start | bytes 589832 | tf_op jit(solution)/shard_map/ppermute | solution.py:575
  34.8 1.9 %collective-permute-start = (bf16[128,768]{1,0:T(8,128)(2,1)S(1)}, bf16[128,768]{1,0:T(8,128)(2,1)S(1)}, u32[]{:S(2)}, u32[]{:S(2)}) collective-permute-start(bf16[128,768]{1,0:T(8,128)(2,1)S(1)} %get-tuple-element.73), channel_id=1, source_target_pairs={{0,8},{8,16},{16,24},{24,32},{32,40},{40,48},{48,56},{56,64},{64,7... | collective-permute-start | bytes 589832 | tf_op jit(solution)/shard_map/ppermute | solution.py:574
  36.8 0.0 copy-done.1
  36.8 0.2 copy.9
  37.1 0.2 copy.12
  37.3 0.2 shard_map.60
  37.5 32.7 %all-to-all-done = bf16[512,3,4,128]{3,2,1,0:T(4,128)(2,1)S(1)} async-done(((bf16[512,3,4,128]{3,2,1,0:T(4,128)(2,1)}), bf16[512,3,4,128]{3,2,1,0:T(4,128)(2,1)S(1)}, u32[]{:S(2)}, u32[]{:S(2)}) %all-to-all-start) | async-done | bytes 1572896 | tf_op jit(solution)/shard_map/all_to_all | solution.py:593
  70.2 1.7 %shard_map.61 = (bf16[1024,768]{1,0:T(8,128)(2,1)S(1)}, f32[512,1024]{1,0:T(8,128)S(1)}, f32[1,1024]{1,0:T(1,128)S(1)}, f32[1,1024]{1,0:T(1,128)S(1)}) custom-call(bf16[6144,128]{1,0:T(8,128)(2,1)S(1)} %bitcast.25, f32[8,1024]{1,0:T(8,128)S(1)} %get-tuple-element.35.hits_ref, bf16[4,128,768]{2,1,0:T(8,128)(2,1)S(1)} %bitcast.22, ...), custom_call_target="tpu_custom_call" | custom-call | flops 805306368 | bytes 1048576 | tf_op jit(solution)/shard_map/pallas_call | solution.py:24
  71.9 0.0 collective-permute-done.1.right_ref
  71.9 0.0 collective-permute-done.left_ref
  71.9 1.9 %shard_map.62 = (f32[1,1024]{1,0:T(1,128)S(1)}, f32[4,128,768]{2,1,0:T(8,128)S(1)}, f32[512,1]{1,0:T(8,128)S(1)}, bf16[1552,128]{1,0:T(8,128)(2,1)S(1)}, bf16[1552,128]{1,0:T(8,128)(2,1)S(1)}) custom-call(bf16[1024,768]{1,0:T(8,128)(2,1)S(1)} %get-tuple-element.37.rows_ref, f32[8,1024]{1,0:T(8,128)S(1)} %get-tuple-element.35.hits_ref, ...), custom_call_target="tpu_custom_call" | custom-call | flops 1207959552 | bytes 1048576 | tf_op jit(solution)/shard_map/pallas_call | solution.py:24
  73.8 3.0 %collective-permute-start.2 = (bf16[1552,128]{1,0:T(8,128)(2,1)S(1)}, bf16[1552,128]{1,0:T(8,128)(2,1)S(1)}, u32[]{:S(2)}, u32[]{:S(2)}) collective-permute-start(bf16[1552,128]{1,0:T(8,128)(2,1)S(1)} %get-tuple-element.48), channel_id=1, source_target_pairs={{0,8},{8,16},{16,24},{24,32},{32,40},{40,48},{48,56},{56,64},{64,7... | collective-permute-start | bytes 1191944 | tf_op jit(solution)/shard_map/ppermute | solution.py:574
  76.8 4.9 %collective-permute-start.3 = (bf16[1552,128]{1,0:T(8,128)(2,1)S(1)}, bf16[1552,128]{1,0:T(8,128)(2,1)S(1)}, u32[]{:S(2)}, u32[]{:S(2)}) collective-permute-start(bf16[1552,128]{1,0:T(8,128)(2,1)S(1)} %get-tuple-element.53), channel_id=1, source_target_pairs={{8,0},{16,8},{24,16},{32,24},{40,32},{48,40},{56,48},{64,56},{72,6... | collective-permute-start | bytes 1191944 | tf_op jit(solution)/shard_map/ppermute | solution.py:575
  81.7 1.5 %shard_map.63 = (bf16[2,128,768]{2,1,0:T(8,128)(2,1)S(1)}, f32[1,1024]{1,0:T(1,128)S(1)}, f32[256,1024]{1,0:T(8,128)S(1)}, f32[1,1024]{1,0:T(1,128)S(1)}, f32[1,1024]{1,0:T(1,128)S(1)}) custom-call(bf16[1024,768]{1,0:T(8,128)(2,1)S(1)} %get-tuple-element.37.rows_ref, f32[8,1024]{1,0:T(8,128)S(1)} %get-tuple-element.35.hits_ref, ...), custom_call_target="tpu_custom_call" | custom-call | flops 805306368 | bytes 1048576 | tf_op jit(solution)/shard_map/pallas_call | solution.py:24
  83.3 5.9 %collective-permute-done.2.below_ref = bf16[1552,128]{1,0:T(8,128)(2,1)S(1)} collective-permute-done((bf16[1552,128]{1,0:T(8,128)(2,1)S(1)}, bf16[1552,128]{1,0:T(8,128)(2,1)S(1)}, u32[]{:S(2)}, u32[]{:S(2)}) %collective-permute-start.2) | collective-permute-done | bytes 397344 | tf_op jit(solution)/shard_map/ppermute | solution.py:574
  89.1 1.0 shard_map.64
  90.1 0.2 collective-permute-done.3.above_ref
  90.3 1.5 %shard_map.65 = (bf16[128,768]{1,0:T(8,128)(2,1)S(1)}, f32[128,1024]{1,0:T(8,128)S(1)}, f32[1,1024]{1,0:T(1,128)S(1)}, f32[1,1024]{1,0:T(1,128)S(1)}, f32[1,1024...) custom-call(bf16[1024,768]{1,0:T(8,128)(2,1)S(1)} %get-tuple-element.37.rows_r, ...), custom_call_target="tpu_custom_call" | custom-call | flops 805306368 | bytes 1048576 | tf_op jit(solution)/shard_map/pallas_call | solution.py:24
  91.8 2.6 %collective-permute-start.4 = (bf16[784,128]{1,0:T(8,128)(2,1)S(1)}, bf16[784,128]{1,0:T(8,128)(2,1)S(1)}, u32[]{:S(2)}, u32[]{:S(2)}) collective-permute-start(bf16[784,128]{1,0:T(8,128)(2,1)S(1)} %get-tuple-element.65), channel_id=1, source_target_pairs={{0,8},{8,16},{16,24},{24,32},{32,40},{40,48},{48,56},{56,64},{64,7... | collective-permute-start | bytes 602120 | tf_op jit(solution)/shard_map/ppermute | solution.py:574
  94.5 5.8 %collective-permute-start.5 = (bf16[784,128]{1,0:T(8,128)(2,1)S(1)}, bf16[784,128]{1,0:T(8,128)(2,1)S(1)}, u32[]{:S(2)}, u32[]{:S(2)}) collective-permute-start(bf16[784,128]{1,0:T(8,128)(2,1)S(1)} %get-tuple-element.66), channel_id=1, source_target_pairs={{8,0},{16,8},{24,16},{32,24},{40,32},{48,40},{56,48},{64,56},{72,6... | collective-permute-start | bytes 602120 | tf_op jit(solution)/shard_map/ppermute | solution.py:575
  100.3 1.7 %shard_map.66 = (bf16[4,128,768]{2,1,0:T(8,128)(2,1)}, f32[2,128,768]{2,1,0:T(8,128)S(1)}, f32[256,1]{1,0:T(8,128)S(1)}, f32[8,128]{1,0:T(8,128)}) custom-call(bf16[1024,768]{1,0:T(8,128)(2,1)S(1)} %get-tuple-element.37.rows_ref, f32[256,1024]{1,0:T(8,128)S(1)} %get-tuple-element.42.inner_ref, f32[1,1024]{1,0:T(1,128)S(1)} %get-tuple-element.54.inner_scale_ref, ...), custom_call_target="tpu_custom_call" | custom-call | flops 805306368 | bytes 1048576 | tf_op jit(solution)/shard_map/pallas_call | solution.py:24
  102.0 0.6 collective-permute-done.4.below_ref
  102.6 1.2 %collective-permute-done.5.above_ref = bf16[784,128]{1,0:T(8,128)(2,1)S(1)} collective-permute-done((bf16[784,128]{1,0:T(8,128)(2,1)S(1)}, bf16[784,128]{1,0:T(8,128)(2,1)S(1)}, u32[]{:S(2)}, u32[]{:S(2)}) %collective-permute-start.5) | collective-permute-done | bytes 200736 | tf_op jit(solution)/shard_map/ppermute | solution.py:575
  103.8 1.0 shard_map.67
  (1 shorter events, 0.0 us)
Async XLA Ops:
  4.8 21.1 %copy-start = (bf16[4,1,128,768]{3,2,1,0:T(8,128)(2,1)S(1)}, bf16[4,1,128,768]{3,2,1,0:T(8,128)(2,1)}, u32[]{:S(2)}) copy-start(bf16[4,1,128,768]{3,2,1,0:T(8,128)(2,1)} %param.7) | copy-start | bytes 2359300
  4.8 32.0 %copy-start.1 = (s32[1024,4]{0,1:T(4,128)S(1)}, s32[1024,4]{0,1:T(4,128)}, u32[]{:S(2)}) copy-start(s32[1024,4]{0,1:T(4,128)} %param.6) | copy-start | bytes 49156
  4.8 65.4 %all-to-all-start = ((bf16[512,3,4,128]{3,2,1,0:T(4,128)(2,1)}), bf16[512,3,4,128]{3,2,1,0:T(4,128)(2,1)S(1)}, u32[]{:S(2)}, u32[]{:S(2)}) async-start(bf16[512,3,4,128]{3,2,1,0:T(4,128)(2,1)} %bitcast.28), calls=%async_computation | async-start | bytes 3145728 | tf_op jit(solution)/shard_map/all_to_all | solution.py:593
  26.7 45.2 %collective-permute-start.1 = (bf16[128,768]{1,0:T(8,128)(2,1)}, bf16[128,768]{1,0:T(8,128)(2,1)S(1)}, u32[]{:S(2)}, u32[]{:S(2)}) collective-permute-start(bf16[128,768]{1,0:T(8,128)(2,1)} %get-tuple-element.72), channel_id=1, source_target_pairs={{8,0},{16,8},{24,16},{32,24},{40,32},{48,40},{56,48},{64,56},{72,6... | collective-permute-start | bytes 589832 | tf_op jit(solution)/shard_map/ppermute | solution.py:575
  34.8 37.1 %collective-permute-start = (bf16[128,768]{1,0:T(8,128)(2,1)S(1)}, bf16[128,768]{1,0:T(8,128)(2,1)S(1)}, u32[]{:S(2)}, u32[]{:S(2)}) collective-permute-start(bf16[128,768]{1,0:T(8,128)(2,1)S(1)} %get-tuple-element.73), channel_id=1, source_target_pairs={{0,8},{8,16},{16,24},{24,32},{32,40},{40,48},{48,56},{56,64},{64,7... | collective-permute-start | bytes 589832 | tf_op jit(solution)/shard_map/ppermute | solution.py:574
  73.8 15.3 %collective-permute-start.2 = (bf16[1552,128]{1,0:T(8,128)(2,1)S(1)}, bf16[1552,128]{1,0:T(8,128)(2,1)S(1)}, u32[]{:S(2)}, u32[]{:S(2)}) collective-permute-start(bf16[1552,128]{1,0:T(8,128)(2,1)S(1)} %get-tuple-element.48), channel_id=1, source_target_pairs={{0,8},{8,16},{16,24},{24,32},{32,40},{40,48},{48,56},{56,64},{64,7... | collective-permute-start | bytes 1191944 | tf_op jit(solution)/shard_map/ppermute | solution.py:574
  76.8 13.5 %collective-permute-start.3 = (bf16[1552,128]{1,0:T(8,128)(2,1)S(1)}, bf16[1552,128]{1,0:T(8,128)(2,1)S(1)}, u32[]{:S(2)}, u32[]{:S(2)}) collective-permute-start(bf16[1552,128]{1,0:T(8,128)(2,1)S(1)} %get-tuple-element.53), channel_id=1, source_target_pairs={{8,0},{16,8},{24,16},{32,24},{40,32},{48,40},{56,48},{64,56},{72,6... | collective-permute-start | bytes 1191944 | tf_op jit(solution)/shard_map/ppermute | solution.py:575
  91.8 10.7 %collective-permute-start.4 = (bf16[784,128]{1,0:T(8,128)(2,1)S(1)}, bf16[784,128]{1,0:T(8,128)(2,1)S(1)}, u32[]{:S(2)}, u32[]{:S(2)}) collective-permute-start(bf16[784,128]{1,0:T(8,128)(2,1)S(1)} %get-tuple-element.65), channel_id=1, source_target_pairs={{0,8},{8,16},{16,24},{24,32},{32,40},{40,48},{48,56},{56,64},{64,7... | collective-permute-start | bytes 602120 | tf_op jit(solution)/shard_map/ppermute | solution.py:574
  94.5 9.3 %collective-permute-start.5 = (bf16[784,128]{1,0:T(8,128)(2,1)S(1)}, bf16[784,128]{1,0:T(8,128)(2,1)S(1)}, u32[]{:S(2)}, u32[]{:S(2)}) collective-permute-start(bf16[784,128]{1,0:T(8,128)(2,1)S(1)} %get-tuple-element.66), channel_id=1, source_target_pairs={{8,0},{16,8},{24,16},{32,24},{40,32},{48,40},{56,48},{64,56},{72,6... | collective-permute-start | bytes 602120 | tf_op jit(solution)/shard_map/ppermute | solution.py:575

commit v7 on v6

--- a/solution.py
+++ b/solution.py
@@ -100,7 +100,7 @@
                 rows_ref[pl.ds(slot * pairs + part * step, step), f * LANES : (f + 1) * LANES] = got.astype(BF16)
 
 
-STEP = 512
+STEP = 256
 
 
 def half_scale(features):

time: 105 us -> 105 us (level)
  no operation moved by 1% of the time
where the time goes in v7:
time: 105 us
  starting transfers between devices  47.6 us (45%)
  waiting for transfers between devices  40.6 us (39%)
  Pallas kernels  14.6 us (14%)
  local copies, waits for them, and re-layouts  1.14 us (1%)
    all_to_all x1, waiting for transfers between devices, per_device(): lax.all_to_all(outgoing.reshape(pairs, lines // pairs // 4, 4, LANES), ('...  32.7 us
    all_to_all x1, starting transfers between devices, per_device(): lax.all_to_all(outgoing.reshape(pairs, lines // pairs // 4, 4, LANES), ('...  21.1 us
    ppermute x3, starting transfers between devices, swap(): above = lax.ppermute(down, axis, [(j, i) for i, j in pairs])  18.9 us
    pallas_call x9, Pallas kernels, call(): pl.pallas_call(kernel, in_specs=[pl.BlockSpec(memory_space=space) for _,...  14.6 us
    ppermute x3, starting transfers between devices, swap(): below = lax.ppermute(up, axis, pairs)  7.55 us
    ppermute x3, waiting for transfers between devices, swap(): below = lax.ppermute(up, axis, pairs)  6.5 us
  transfers between devices with their start and end apart: 7, of which 5 were waited for; matrix products, arithmetic and copies ran while one was open for 1% of the time, Pallas kernels for 6%

profile of v7, /device:TPU:8, one launch (start us, length us, event | category | flops | bytes accessed | tf_op | source)
XLA Modules:
  0.0 104.8 jit_solution(6265497054770691988)
XLA Ops:
  0.6 4.2 %shard_map.59 = bf16[6144,128]{1,0:T(8,128)(2,1)} custom-call(s32[1,1024]{1,0:T(1,128)} %bitcast.30, bf16[1024,768]{1,0:T(8,128)(2,1)} %rows_hbm.1), custom_call_target="tpu_custom_call" | custom-call | flops 1610612736 | bytes 1048576 | tf_op jit(solution)/shard_map/pallas_call | solution.py:24
  4.8 0.0 copy-start
  4.8 0.0 copy-start.1
  4.8 21.1 %all-to-all-start = ((bf16[512,3,4,128]{3,2,1,0:T(4,128)(2,1)}), bf16[512,3,4,128]{3,2,1,0:T(4,128)(2,1)S(1)}, u32[]{:S(2)}, u32[]{:S(2)}) async-start(bf16[512,3,4,128]{3,2,1,0:T(4,128)(2,1)} %bitcast.28), calls=%async_computation | async-start | bytes 3145728 | tf_op jit(solution)/shard_map/all_to_all | solution.py:593
  25.9 0.0 copy-done
  25.9 0.7 slice_bitcast_fusion
  26.7 8.2 %collective-permute-start.1 = (bf16[128,768]{1,0:T(8,128)(2,1)}, bf16[128,768]{1,0:T(8,128)(2,1)S(1)}, u32[]{:S(2)}, u32[]{:S(2)}) collective-permute-start(bf16[128,768]{1,0:T(8,128)(2,1)} %get-tuple-element.72), channel_id=1, source_target_pairs={{8,0},{16,8},{24,16},{32,24},{40,32},{48,40},{56,48},{64,56},{72,6... | collective-permute-start | bytes 589832 | tf_op jit(solution)/shard_map/ppermute | solution.py:575
  34.8 1.9 %collective-permute-start = (bf16[128,768]{1,0:T(8,128)(2,1)S(1)}, bf16[128,768]{1,0:T(8,128)(2,1)S(1)}, u32[]{:S(2)}, u32[]{:S(2)}) collective-permute-start(bf16[128,768]{1,0:T(8,128)(2,1)S(1)} %get-tuple-element.73), channel_id=1, source_target_pairs={{0,8},{8,16},{16,24},{24,32},{32,40},{40,48},{48,56},{56,64},{64,7... | collective-permute-start | bytes 589832 | tf_op jit(solution)/shard_map/ppermute | solution.py:574
  36.8 0.0 copy-done.1
  36.8 0.2 copy.9
  37.1 0.2 copy.12
  37.3 0.2 shard_map.60
  37.5 32.7 %all-to-all-done = bf16[512,3,4,128]{3,2,1,0:T(4,128)(2,1)S(1)} async-done(((bf16[512,3,4,128]{3,2,1,0:T(4,128)(2,1)}), bf16[512,3,4,128]{3,2,1,0:T(4,128)(2,1)S(1)}, u32[]{:S(2)}, u32[]{:S(2)}) %all-to-all-start) | async-done | bytes 1572896 | tf_op jit(solution)/shard_map/all_to_all | solution.py:593
  70.2 1.7 %shard_map.61 = (bf16[1024,768]{1,0:T(8,128)(2,1)S(1)}, f32[512,1024]{1,0:T(8,128)S(1)}, f32[1,1024]{1,0:T(1,128)S(1)}, f32[1,1024]{1,0:T(1,128)S(1)}) custom-call(bf16[6144,128]{1,0:T(8,128)(2,1)S(1)} %bitcast.25, f32[8,1024]{1,0:T(8,128)S(1)} %get-tuple-element.35.hits_ref, bf16[4,128,768]{2,1,0:T(8,128)(2,1)S(1)} %bitcast.22, ...), custom_call_target="tpu_custom_call" | custom-call | flops 805306368 | bytes 1048576 | tf_op jit(solution)/shard_map/pallas_call | solution.py:24
  71.9 0.0 collective-permute-done.1.right_ref
  71.9 0.0 collective-permute-done.left_ref
  71.9 1.9 %shard_map.62 = (f32[1,1024]{1,0:T(1,128)S(1)}, f32[4,128,768]{2,1,0:T(8,128)S(1)}, f32[512,1]{1,0:T(8,128)S(1)}, bf16[1552,128]{1,0:T(8,128)(2,1)S(1)}, bf16[1552,128]{1,0:T(8,128)(2,1)S(1)}) custom-call(bf16[1024,768]{1,0:T(8,128)(2,1)S(1)} %get-tuple-element.37.rows_ref, f32[8,1024]{1,0:T(8,128)S(1)} %get-tuple-element.35.hits_ref, ...), custom_call_target="tpu_custom_call" | custom-call | flops 1207959552 | bytes 1048576 | tf_op jit(solution)/shard_map/pallas_call | solution.py:24
  73.8 3.0 %collective-permute-start.2 = (bf16[1552,128]{1,0:T(8,128)(2,1)S(1)}, bf16[1552,128]{1,0:T(8,128)(2,1)S(1)}, u32[]{:S(2)}, u32[]{:S(2)}) collective-permute-start(bf16[1552,128]{1,0:T(8,128)(2,1)S(1)} %get-tuple-element.48), channel_id=1, source_target_pairs={{0,8},{8,16},{16,24},{24,32},{32,40},{40,48},{48,56},{56,64},{64,7... | collective-permute-start | bytes 1191944 | tf_op jit(solution)/shard_map/ppermute | solution.py:574
  76.8 4.9 %collective-permute-start.3 = (bf16[1552,128]{1,0:T(8,128)(2,1)S(1)}, bf16[1552,128]{1,0:T(8,128)(2,1)S(1)}, u32[]{:S(2)}, u32[]{:S(2)}) collective-permute-start(bf16[1552,128]{1,0:T(8,128)(2,1)S(1)} %get-tuple-element.53), channel_id=1, source_target_pairs={{8,0},{16,8},{24,16},{32,24},{40,32},{48,40},{56,48},{64,56},{72,6... | collective-permute-start | bytes 1191944 | tf_op jit(solution)/shard_map/ppermute | solution.py:575
  81.8 1.5 %shard_map.63 = (bf16[2,128,768]{2,1,0:T(8,128)(2,1)S(1)}, f32[1,1024]{1,0:T(1,128)S(1)}, f32[256,1024]{1,0:T(8,128)S(1)}, f32[1,1024]{1,0:T(1,128)S(1)}, f32[1,1024]{1,0:T(1,128)S(1)}) custom-call(bf16[1024,768]{1,0:T(8,128)(2,1)S(1)} %get-tuple-element.37.rows_ref, f32[8,1024]{1,0:T(8,128)S(1)} %get-tuple-element.35.hits_ref, ...), custom_call_target="tpu_custom_call" | custom-call | flops 805306368 | bytes 1048576 | tf_op jit(solution)/shard_map/pallas_call | solution.py:24
  83.3 5.9 %collective-permute-done.2.below_ref = bf16[1552,128]{1,0:T(8,128)(2,1)S(1)} collective-permute-done((bf16[1552,128]{1,0:T(8,128)(2,1)S(1)}, bf16[1552,128]{1,0:T(8,128)(2,1)S(1)}, u32[]{:S(2)}, u32[]{:S(2)}) %collective-permute-start.2) | collective-permute-done | bytes 397344 | tf_op jit(solution)/shard_map/ppermute | solution.py:574
  89.1 1.0 shard_map.64
  90.1 0.2 collective-permute-done.3.above_ref
  90.3 1.5 %shard_map.65 = (bf16[128,768]{1,0:T(8,128)(2,1)S(1)}, f32[128,1024]{1,0:T(8,128)S(1)}, f32[1,1024]{1,0:T(1,128)S(1)}, f32[1,1024]{1,0:T(1,128)S(1)}, f32[1,1024...) custom-call(bf16[1024,768]{1,0:T(8,128)(2,1)S(1)} %get-tuple-element.37.rows_r, ...), custom_call_target="tpu_custom_call" | custom-call | flops 805306368 | bytes 1048576 | tf_op jit(solution)/shard_map/pallas_call | solution.py:24
  91.9 2.6 %collective-permute-start.4 = (bf16[784,128]{1,0:T(8,128)(2,1)S(1)}, bf16[784,128]{1,0:T(8,128)(2,1)S(1)}, u32[]{:S(2)}, u32[]{:S(2)}) collective-permute-start(bf16[784,128]{1,0:T(8,128)(2,1)S(1)} %get-tuple-element.65), channel_id=1, source_target_pairs={{0,8},{8,16},{16,24},{24,32},{32,40},{40,48},{48,56},{56,64},{64,7... | collective-permute-start | bytes 602120 | tf_op jit(solution)/shard_map/ppermute | solution.py:574
  94.5 5.8 %collective-permute-start.5 = (bf16[784,128]{1,0:T(8,128)(2,1)S(1)}, bf16[784,128]{1,0:T(8,128)(2,1)S(1)}, u32[]{:S(2)}, u32[]{:S(2)}) collective-permute-start(bf16[784,128]{1,0:T(8,128)(2,1)S(1)} %get-tuple-element.66), channel_id=1, source_target_pairs={{8,0},{16,8},{24,16},{32,24},{40,32},{48,40},{56,48},{64,56},{72,6... | collective-permute-start | bytes 602120 | tf_op jit(solution)/shard_map/ppermute | solution.py:575
  100.3 1.7 %shard_map.66 = (bf16[4,128,768]{2,1,0:T(8,128)(2,1)}, f32[2,128,768]{2,1,0:T(8,128)S(1)}, f32[256,1]{1,0:T(8,128)S(1)}, f32[8,128]{1,0:T(8,128)}) custom-call(bf16[1024,768]{1,0:T(8,128)(2,1)S(1)} %get-tuple-element.37.rows_ref, f32[256,1024]{1,0:T(8,128)S(1)} %get-tuple-element.42.inner_ref, f32[1,1024]{1,0:T(1,128)S(1)} %get-tuple-element.54.inner_scale_ref, ...), custom_call_target="tpu_custom_call" | custom-call | flops 805306368 | bytes 1048576 | tf_op jit(solution)/shard_map/pallas_call | solution.py:24
  102.0 0.6 collective-permute-done.4.below_ref
  102.6 1.2 %collective-permute-done.5.above_ref = bf16[784,128]{1,0:T(8,128)(2,1)S(1)} collective-permute-done((bf16[784,128]{1,0:T(8,128)(2,1)S(1)}, bf16[784,128]{1,0:T(8,128)(2,1)S(1)}, u32[]{:S(2)}, u32[]{:S(2)}) %collective-permute-start.5) | collective-permute-done | bytes 200736 | tf_op jit(solution)/shard_map/ppermute | solution.py:575
  103.8 1.0 shard_map.67
  (1 shorter events, 0.0 us)
Async XLA Ops:
  4.8 21.1 %copy-start = (bf16[4,1,128,768]{3,2,1,0:T(8,128)(2,1)S(1)}, bf16[4,1,128,768]{3,2,1,0:T(8,128)(2,1)}, u32[]{:S(2)}) copy-start(bf16[4,1,128,768]{3,2,1,0:T(8,128)(2,1)} %param.7) | copy-start | bytes 2359300
  4.8 32.0 %copy-start.1 = (s32[1024,4]{0,1:T(4,128)S(1)}, s32[1024,4]{0,1:T(4,128)}, u32[]{:S(2)}) copy-start(s32[1024,4]{0,1:T(4,128)} %param.6) | copy-start | bytes 49156
  4.8 65.4 %all-to-all-start = ((bf16[512,3,4,128]{3,2,1,0:T(4,128)(2,1)}), bf16[512,3,4,128]{3,2,1,0:T(4,128)(2,1)S(1)}, u32[]{:S(2)}, u32[]{:S(2)}) async-start(bf16[512,3,4,128]{3,2,1,0:T(4,128)(2,1)} %bitcast.28), calls=%async_computation | async-start | bytes 3145728 | tf_op jit(solution)/shard_map/all_to_all | solution.py:593
  26.7 45.3 %collective-permute-start.1 = (bf16[128,768]{1,0:T(8,128)(2,1)}, bf16[128,768]{1,0:T(8,128)(2,1)S(1)}, u32[]{:S(2)}, u32[]{:S(2)}) collective-permute-start(bf16[128,768]{1,0:T(8,128)(2,1)} %get-tuple-element.72), channel_id=1, source_target_pairs={{8,0},{16,8},{24,16},{32,24},{40,32},{48,40},{56,48},{64,56},{72,6... | collective-permute-start | bytes 589832 | tf_op jit(solution)/shard_map/ppermute | solution.py:575
  34.8 37.1 %collective-permute-start = (bf16[128,768]{1,0:T(8,128)(2,1)S(1)}, bf16[128,768]{1,0:T(8,128)(2,1)S(1)}, u32[]{:S(2)}, u32[]{:S(2)}) collective-permute-start(bf16[128,768]{1,0:T(8,128)(2,1)S(1)} %get-tuple-element.73), channel_id=1, source_target_pairs={{0,8},{8,16},{16,24},{24,32},{32,40},{40,48},{48,56},{56,64},{64,7... | collective-permute-start | bytes 589832 | tf_op jit(solution)/shard_map/ppermute | solution.py:574
  73.8 15.3 %collective-permute-start.2 = (bf16[1552,128]{1,0:T(8,128)(2,1)S(1)}, bf16[1552,128]{1,0:T(8,128)(2,1)S(1)}, u32[]{:S(2)}, u32[]{:S(2)}) collective-permute-start(bf16[1552,128]{1,0:T(8,128)(2,1)S(1)} %get-tuple-element.48), channel_id=1, source_target_pairs={{0,8},{8,16},{16,24},{24,32},{32,40},{40,48},{48,56},{56,64},{64,7... | collective-permute-start | bytes 1191944 | tf_op jit(solution)/shard_map/ppermute | solution.py:574
  76.8 13.5 %collective-permute-start.3 = (bf16[1552,128]{1,0:T(8,128)(2,1)S(1)}, bf16[1552,128]{1,0:T(8,128)(2,1)S(1)}, u32[]{:S(2)}, u32[]{:S(2)}) collective-permute-start(bf16[1552,128]{1,0:T(8,128)(2,1)S(1)} %get-tuple-element.53), channel_id=1, source_target_pairs={{8,0},{16,8},{24,16},{32,24},{40,32},{48,40},{56,48},{64,56},{72,6... | collective-permute-start | bytes 1191944 | tf_op jit(solution)/shard_map/ppermute | solution.py:575
  91.9 10.7 %collective-permute-start.4 = (bf16[784,128]{1,0:T(8,128)(2,1)S(1)}, bf16[784,128]{1,0:T(8,128)(2,1)S(1)}, u32[]{:S(2)}, u32[]{:S(2)}) collective-permute-start(bf16[784,128]{1,0:T(8,128)(2,1)S(1)} %get-tuple-element.65), channel_id=1, source_target_pairs={{0,8},{8,16},{16,24},{24,32},{32,40},{40,48},{48,56},{56,64},{64,7... | collective-permute-start | bytes 602120 | tf_op jit(solution)/shard_map/ppermute | solution.py:574
  94.5 9.3 %collective-permute-start.5 = (bf16[784,128]{1,0:T(8,128)(2,1)S(1)}, bf16[784,128]{1,0:T(8,128)(2,1)S(1)}, u32[]{:S(2)}, u32[]{:S(2)}) collective-permute-start(bf16[784,128]{1,0:T(8,128)(2,1)S(1)} %get-tuple-element.66), channel_id=1, source_target_pairs={{8,0},{16,8},{24,16},{32,24},{40,32},{48,40},{56,48},{64,56},{72,6... | collective-permute-start | bytes 602120 | tf_op jit(solution)/shard_map/ppermute | solution.py:575
